TPU v7x, 32 devices: a whole 2x2x4 slice. The times are simulated.
32 devices in a mesh: ctx: 8 (over y, x, core), head: 4 (over z).
Axes of the slice: x: 2, y: 2, z: 4, core: 2. Of those that a mesh axis runs over, the one named last changes fastest.
Arguments:
- queries: bfloat16 [16, 2048, 128], P('head', 'ctx'), may hold values from -110 to 110
- keys: bfloat16 [2, 2048, 128], P(None, 'ctx'), may hold values from -4 to 4
- values: bfloat16 [2, 2048, 128], P(None, 'ctx'), may hold values from -6 to 6
- d_out: bfloat16 [16, 2048, 128], P('head', 'ctx'), may hold values from -6 to 6
- doc_lengths: int32 [4], replicated, may hold values from 1 to 1024, 2048 in all
Outputs:
- d_queries: bfloat16 [16, 2048, 128], P('head', 'ctx')
- d_keys: bfloat16 [2, 2048, 128], P(None, ('ctx', 'head'))
- d_values: bfloat16 [2, 2048, 128], P(None, ('ctx', 'head'))
Inputs may be any that keep to these rules, and one draw needn't show every extreme that they name: `doc_lengths`: documents lie end to end in order and their lengths sum to 2048; one of them has exactly 1024 tokens.
All inputs are finite; a program needn't handle non-finite values.
Results may differ from a plain program's by a relative error of at most 0.025.
Values may be sent and summed in bfloat16 or wider, within the bound.
No kernel may reach another device: no remote copies, remote signals or barrier semaphores. Data moves between devices by JAX's collectives and lax.ppermute only.
A program may use at most 64 MiB of HBM per device.

v0:
```python
import jax
import jax.numpy as jnp
from jax import lax
from jax.sharding import PartitionSpec as P

GROUP = 8


masked_value = -1e30


def shifted(block, axis, distance):
    devices = range(lax.axis_size(axis))
    route = [(i - distance, i) for i in devices if i - distance in devices]
    return lax.ppermute(block, axis, route)


def for_sending(shard):
    return jax.tree.map(lambda a: a.astype(jnp.bfloat16) if a.dtype == jnp.float32 else a, shard)


def from_partner(value, axis, stride):
    mask = 2**stride
    pairs = [(source, source ^ mask) for source in range(lax.axis_size(axis))]
    return lax.ppermute(value, axis, pairs)


def doc_number(positions, doc_ends):
    return jnp.sum((doc_ends[None, :] <= positions[:, None]).astype(jnp.int32), axis=1)


def window_terms(query_rows, grad_rows, window, query_pos, key_pos, doc_ends, key_scale):
    head_width = query_rows.shape[-1]
    key_rows = window[:, :head_width]
    value_rows = window[:, head_width:]
    allowed = doc_number(query_pos, doc_ends)[:, None] == doc_number(key_pos, doc_ends)[None, :]
    allowed = allowed & (key_pos[None, :] <= query_pos[:, None]) & (key_pos[None, :] >= 0)
    scores = (
        jnp.einsum("hbd,ld->hbl", query_rows, key_rows, preferred_element_type=jnp.float32)
        * key_scale
    )
    scores = jnp.where(allowed[None], scores, masked_value)
    row_max = jnp.max(scores, axis=-1, keepdims=True)
    log_total = row_max + jnp.log(jnp.sum(jnp.exp(scores - row_max), axis=-1, keepdims=True))
    attention = jnp.where(allowed[None], jnp.exp(scores - log_total), 0.0)
    attn_half = attention.astype(jnp.bfloat16)
    attended = jnp.einsum(
        "hbl,ld->hbd", attn_half, value_rows, preferred_element_type=jnp.float32
    ).astype(jnp.bfloat16)
    deltas = jnp.sum(
        grad_rows.astype(jnp.float32) * attended.astype(jnp.float32), axis=-1, keepdims=True
    )
    dattn = jnp.einsum("hbd,ld->hbl", grad_rows, value_rows, preferred_element_type=jnp.float32)
    dscores = (attention * (dattn - deltas)).astype(jnp.bfloat16)
    dquery = (
        jnp.einsum("hbl,ld->hbd", dscores, key_rows, preferred_element_type=jnp.float32) * key_scale
    ).astype(jnp.bfloat16)
    key_grad = (
        jnp.einsum("hbl,hbd->ld", dscores, query_rows, preferred_element_type=jnp.float32)
        * key_scale
    )
    dvalue = jnp.einsum("hbl,hbd->ld", attn_half, grad_rows, preferred_element_type=jnp.float32)
    return (dquery, jnp.concatenate([key_grad, dvalue], axis=1))


def per_device(queries, keys, values, d_out, doc_lengths):
    heads_here, tokens_here, head_width = queries.shape
    ctx_count = lax.axis_size("ctx")
    head_count = lax.axis_size("head")
    reach_blocks = min(4, ctx_count // 2)
    key_span = reach_blocks * tokens_here
    kv_group = lax.axis_index("head") * heads_here // GROUP
    own_keys = lax.dynamic_index_in_dim(keys, kv_group, 0, keepdims=False)
    own_values = lax.dynamic_index_in_dim(values, kv_group, 0, keepdims=False)
    own_pairs = jnp.concatenate([own_keys, own_values], axis=1)
    row_first = lax.axis_index("ctx") * tokens_here
    earlier = []
    passing = own_pairs
    for offset in range(1, reach_blocks + 1):
        passing = shifted(passing, "ctx", 1)
        earlier.insert(0, passing)
    window = jnp.concatenate(earlier + [own_pairs], axis=0)
    doc_ends = jnp.cumsum(doc_lengths)
    query_pos = row_first + jnp.arange(tokens_here, dtype=jnp.int32)
    key_pos = row_first - key_span + jnp.arange(key_span + tokens_here, dtype=jnp.int32)
    d_queries, pair_terms = window_terms(
        queries, d_out, window, query_pos, key_pos, doc_ends, head_width ** (-0.5)
    )
    own_sums = pair_terms[key_span:]
    for offset in range(1, reach_blocks + 1):
        lower_row = key_span - offset * tokens_here
        own_sums = own_sums + shifted(
            pair_terms[lower_row : lower_row + tokens_here].astype(jnp.bfloat16), "ctx", -offset
        ).astype(jnp.float32)
    pair_total = own_sums + from_partner(for_sending(own_sums), "head", 0).astype(own_sums.dtype)
    slices = lax.all_to_all(
        for_sending(pair_total[None]), "head", split_axis=1, concat_axis=0, tiled=True
    )
    slice_rows = slices.shape[1]
    group_sums = slices.reshape(head_count // 2, 2, slice_rows, 2 * head_width)[:, 0]
    d_keys = group_sums[:, :, :head_width].astype(jnp.bfloat16)
    d_values = group_sums[:, :, head_width:].astype(jnp.bfloat16)
    return (d_queries, d_keys, d_values)


def solution(mesh):
    placed = (
        P("head", "ctx", None),
        P(None, "ctx", None),
        P(None, "ctx", None),
        P("head", "ctx", None),
        P(),
    )
    return jax.shard_map(
        per_device,
        mesh=mesh,
        in_specs=placed,
        out_specs=(
            P("head", "ctx", None),
            P(None, ("ctx", "head"), None),
            P(None, ("ctx", "head"), None),
        ),
        check_vma=False,
    )
```

profile of v0, /device:TPU:4, one launch (start us, length us, event | category | flops | bytes accessed | tf_op | source)
XLA Modules:
  0.0 68.2 jit_solution(5040819909747627851)
XLA Ops:
  0.7 0.9 %dynamic-slice_bitcast_fusion = (bf16[256,128]{1,0:T(8,128)(2,1)S(1)}, bf16[256,128]{1,0:T(8,128)(2,1)S(1)}) fusion(bf16[2,256,128]{2,1,0:T(8,128)(2,1)} %param.7, s32[]{:T(128)S(6)} %select_n.18, bf16[2,256,128]{2,1,0:T(8,128)(2,1)} %param.6), kind=kLoop, calls=%fused_computation.31 | loop fusion | bytes 262148 | tf_op jit(solution)/shard_map/jit(dynamic_index_in_dim)/squeeze | solution.py:74
  1.6 1.9 %collective-permute-start = (bf16[256,256]{1,0:T(8,128)(2,1)S(1)}, bf16[256,256]{1,0:T(8,128)(2,1)S(1)}, u32[]{:S(2)}, u32[]{:S(2)}) collective-permute-start(bf16[256,256]{1,0:T(8,128)(2,1)S(1)} %pad_maximum_fusion.1), channel_id=1, source_target_pairs={{0,4},{4,8},{8,12},{12,16},{16,20},{20,24},{24,28},{1,5},{5,9},{9,... | collective-permute-start | bytes 393224 | tf_op jit(solution)/shard_map/ppermute | solution.py:15
  3.6 5.2 %collective-permute-done = bf16[256,256]{1,0:T(8,128)(2,1)S(1)} collective-permute-done((bf16[256,256]{1,0:T(8,128)(2,1)S(1)}, bf16[256,256]{1,0:T(8,128)(2,1)S(1)}, u32[]{:S(2)}, u32[]{:S(2)}) %collective-permute-start) | collective-permute-done | bytes 131104 | tf_op jit(solution)/shard_map/ppermute | solution.py:15
  8.8 1.9 %collective-permute-start.1 = (bf16[256,256]{1,0:T(8,128)(2,1)S(1)}, bf16[256,256]{1,0:T(8,128)(2,1)S(1)}, u32[]{:S(2)}, u32[]{:S(2)}) collective-permute-start(bf16[256,256]{1,0:T(8,128)(2,1)S(1)} %collective-permute-done), channel_id=1, source_target_pairs={{0,4},{4,8},{8,12},{12,16},{16,20},{20,24},{24,28},{1,5},{5,9},{9,... | collective-permute-start | bytes 393224 | tf_op jit(solution)/shard_map/ppermute | solution.py:15
  10.7 0.8 %reduce-window.8 = s32[4,1]{0,1:T(1,128)S(1)} reduce-window(s32[4,1]{0,1:T(1,128)} %bitcast.47, s32[]{:T(128)} %constant.20.clone.1), window={size=4x1 pad=3_0x0_0}, to_apply=%region_0.1 | reduce-window | flops 12 | bytes 36 | tf_op jit(solution)/shard_map/reduce-window.3
  11.7 4.3 %collective-permute-done.1 = bf16[256,256]{1,0:T(8,128)(2,1)S(1)} collective-permute-done((bf16[256,256]{1,0:T(8,128)(2,1)S(1)}, bf16[256,256]{1,0:T(8,128)(2,1)S(1)}, u32[]{:S(2)}, u32[]{:S(2)}) %collective-permute-start.1) | collective-permute-done | bytes 131104 | tf_op jit(solution)/shard_map/ppermute | solution.py:15
  16.0 1.9 %collective-permute-start.2 = (bf16[256,256]{1,0:T(8,128)(2,1)S(1)}, bf16[256,256]{1,0:T(8,128)(2,1)S(1)}, u32[]{:S(2)}, u32[]{:S(2)}) collective-permute-start(bf16[256,256]{1,0:T(8,128)(2,1)S(1)} %collective-permute-done.1), channel_id=1, source_target_pairs={{0,4},{4,8},{8,12},{12,16},{16,20},{20,24},{24,28},{1,5},{5,9},{9,... | collective-permute-start | bytes 393224 | tf_op jit(solution)/shard_map/ppermute | solution.py:15
  18.0 5.2 %collective-permute-done.2 = bf16[256,256]{1,0:T(8,128)(2,1)S(1)} collective-permute-done((bf16[256,256]{1,0:T(8,128)(2,1)S(1)}, bf16[256,256]{1,0:T(8,128)(2,1)S(1)}, u32[]{:S(2)}, u32[]{:S(2)}) %collective-permute-start.2) | collective-permute-done | bytes 131104 | tf_op jit(solution)/shard_map/ppermute | solution.py:15
  23.2 1.9 %collective-permute-start.3 = (bf16[256,256]{1,0:T(8,128)(2,1)S(1)}, bf16[256,256]{1,0:T(8,128)(2,1)S(1)}, u32[]{:S(2)}, u32[]{:S(2)}) collective-permute-start(bf16[256,256]{1,0:T(8,128)(2,1)S(1)} %collective-permute-done.2), channel_id=1, source_target_pairs={{0,4},{4,8},{8,12},{12,16},{16,20},{20,24},{24,28},{1,5},{5,9},{9,... | collective-permute-start | bytes 393224 | tf_op jit(solution)/shard_map/ppermute | solution.py:15
  25.1 1.1 %and_and_fusion = pred[256,1280]{0,1:T(8,128)(4,1)S(1)} fusion(s32[256]{0:T(256)S(1)} %iota_add_fusion.1, s32[256]{0:T(256)S(1)} %convert_reduce_fusion.1, s32[1280]{0:T(1024)S(1)} %iota_add_fusion, s32[1280]{0:T(1024)S(1)} %convert_reduce_fusion, pred[1280]{0:T(1024)(128)(4,1)S(1)} %broadcast_compare_fusion), kind=kLoop, calls=%fused_computation.13 | loop fusion | flops 1310720 | bytes 341248 | tf_op jit(solution)/shard_map/and | solution.py:37
  26.2 1.1 %copy.35 = bf16[4,256,128]{1,2,0:T(8,128)(2,1)S(1)} copy(bf16[4,256,128]{2,1,0:T(8,128)(2,1)} %param.8) | data formatting | bytes 524288 | tf_op args[3]
  27.3 3.1 %collective-permute-done.3 = bf16[256,256]{1,0:T(8,128)(2,1)S(1)} collective-permute-done((bf16[256,256]{1,0:T(8,128)(2,1)S(1)}, bf16[256,256]{1,0:T(8,128)(2,1)S(1)}, u32[]{:S(2)}, u32[]{:S(2)}) %collective-permute-start.3) | collective-permute-done | bytes 131104 | tf_op jit(solution)/shard_map/ppermute | solution.py:15
  30.5 1.0 %fusion.22 = (f32[4,256]{1,0:T(4,128)S(1)}, f32[4,256,1280]{1,2,0:T(8,128)S(1)}) fusion(bf16[4,256,128]{2,1,0:T(8,128)(2,1)S(1)} %copy-done, bf16[1280,256]{1,0:T(8,128)(2,1)S(1)} %constant_dynamic-update-slice_fusion, pred[256,1280]{0,1:T(8,128)(4,1)S(1)} %and_and_fusion), kind=kOutput, calls=%fused_computation.49 | convolution fusion | flops 339475456 | bytes 6164480 | tf_op jit(solution)/shard_map/hbd,ld->hbl/dot_general | solution.py:39
  31.4 0.7 %exponential_reduce_fusion = f32[4,256]{1,0:T(4,128)S(1)} fusion(f32[4,256,1280]{1,2,0:T(8,128)S(1)} %get-tuple-element.12, f32[4,256]{1,0:T(4,128)S(1)} %get-tuple-element.11), kind=kLoop, calls=%fused_computation.4 | loop fusion | flops 2620416 | bytes 5251072 | tf_op jit(solution)/shard_map/reduce_sum | solution.py:44
  32.2 1.1 %convolution_bitcast_fusion = f32[1280,128]{0,1:T(8,128)S(1)} fusion(bf16[4,256,128]{2,1,0:T(8,128)(2,1)S(1)} %copy-done.2, f32[4,256,1280]{1,2,0:T(8,128)S(1)} %get-tuple-element.12, f32[4,256]{1,0:T(4,128)S(1)} %log_add_fusion, pred[256,1280]{0,1:T(8,128)(4,1)S(1)} %and_and_fusion), kind=kOutput, calls=%fused_computation.6 | convolution fusion | flops 339476480 | bytes 6492160 | tf_op jit(solution)/shard_map/hbl,hbd->ld/dot_general | solution.py:62
  33.3 1.0 %fusion.7 = f32[4,256]{1,0:T(4,128)S(1)} fusion(bf16[4,256,128]{1,2,0:T(8,128)(2,1)S(1)} %copy.35, bf16[1280,256]{1,0:T(8,128)(2,1)S(1)} %constant_dynamic-update-slice_fusion, f32[4,256,1280]{1,2,0:T(8,128)S(1)} %get-tuple-element.12, f32[4,256]{1,0:T(4,128)S(1)} %log_add_fusion, pred[256,1280]{0,1:T(8,128)(4,1)S(1)} %and_and_fusion), kind=kOutput, calls=%fused_computation.19 | convolution fusion | flops 340130816 | bytes 6168576 | tf_op jit(solution)/shard_map/hbl,ld->hbd/dot_general | solution.py:47
  34.3 1.5 %fusion = bf16[4,256,1280]{1,2,0:T(8,128)(2,1)S(1)} fusion(bf16[4,256,128]{2,1,0:T(8,128)(2,1)S(1)} %copy-done.2, f32[4,256,1280]{1,2,0:T(8,128)S(1)} %get-tuple-element.12, f32[4,256]{1,0:T(4,128)S(1)} %fusion.7, f32[4,256]{1,0:T(4,128)S(1)} %log_add_fusion, pred[256,1280]{0,1:T(8,128)(4,1)S(1)} %and_and_fusion, ...), kind=kOutput, calls=%fused_computation.1 | convolution fusion | flops 342097920 | bytes 8790016 | tf_op jit(solution)/shard_map/hbd,ld->hbl/dot_general | solution.py:53
  35.8 1.0 %fusion.2 = f32[1280,128]{0,1:T(8,128)S(1)} fusion(bf16[4,256,1280]{1,2,0:T(8,128)(2,1)S(1)} %fusion, bf16[4,256,128]{2,1,0:T(8,128)(2,1)S(1)} %copy-done), kind=kOutput, calls=%fused_computation.8 | convolution fusion | flops 335708160 | bytes 3538944 | tf_op jit(solution)/shard_map/hbl,hbd->ld/dot_general | solution.py:59
  36.9 1.3 %collective-permute-start.7 = (bf16[256,256]{0,1:T(8,128)(2,1)S(1)}, bf16[256,256]{0,1:T(8,128)(2,1)S(1)}, u32[]{:S(2)}, u32[]{:S(2)}) collective-permute-start(bf16[256,256]{0,1:T(8,128)(2,1)S(1)} %get-tuple-element.6), channel_id=1, source_target_pairs={{16,0},{20,4},{24,8},{28,12},{17,1},{21,5},{25,9},{29,13},{18,2},{... | collective-permute-start | bytes 393224 | tf_op jit(solution)/shard_map/ppermute | solution.py:15
  38.2 1.9 %collective-permute-start.6 = (bf16[256,256]{0,1:T(8,128)(2,1)S(1)}, bf16[256,256]{0,1:T(8,128)(2,1)S(1)}, u32[]{:S(2)}, u32[]{:S(2)}) collective-permute-start(bf16[256,256]{0,1:T(8,128)(2,1)S(1)} %get-tuple-element.7), channel_id=1, source_target_pairs={{12,0},{16,4},{20,8},{24,12},{28,16},{13,1},{17,5},{21,9},{25,13},... | collective-permute-start | bytes 393224 | tf_op jit(solution)/shard_map/ppermute | solution.py:15
  40.1 1.9 %collective-permute-start.5 = (bf16[256,256]{0,1:T(8,128)(2,1)S(1)}, bf16[256,256]{0,1:T(8,128)(2,1)S(1)}, u32[]{:S(2)}, u32[]{:S(2)}) collective-permute-start(bf16[256,256]{0,1:T(8,128)(2,1)S(1)} %get-tuple-element.8), channel_id=1, source_target_pairs={{8,0},{12,4},{16,8},{20,12},{24,16},{28,20},{9,1},{13,5},{17,9},{2... | collective-permute-start | bytes 393224 | tf_op jit(solution)/shard_map/ppermute | solution.py:15
  42.1 1.9 %collective-permute-start.4 = (bf16[256,256]{0,1:T(8,128)(2,1)S(1)}, bf16[256,256]{0,1:T(8,128)(2,1)S(1)}, u32[]{:S(2)}, u32[]{:S(2)}) collective-permute-start(bf16[256,256]{0,1:T(8,128)(2,1)S(1)} %get-tuple-element.5), channel_id=1, source_target_pairs={{4,0},{8,4},{12,8},{16,12},{20,16},{24,20},{28,24},{5,1},{9,5},{13... | collective-permute-start | bytes 393224 | tf_op jit(solution)/shard_map/ppermute | solution.py:15
  44.5 2.8 %collective-permute-done.5 = bf16[256,256]{0,1:T(8,128)(2,1)S(1)} collective-permute-done((bf16[256,256]{0,1:T(8,128)(2,1)S(1)}, bf16[256,256]{0,1:T(8,128)(2,1)S(1)}, u32[]{:S(2)}, u32[]{:S(2)}) %collective-permute-start.5) | collective-permute-done | bytes 131104 | tf_op jit(solution)/shard_map/ppermute | solution.py:15
  47.4 1.6 %collective-permute-start.8 = (bf16[256,256]{0,1:T(8,128)(2,1)S(1)}, bf16[256,256]{0,1:T(8,128)(2,1)S(1)}, u32[]{:S(2)}, u32[]{:S(2)}) collective-permute-start(bf16[256,256]{0,1:T(8,128)(2,1)S(1)} %get-tuple-element.3), channel_id=1, source_target_pairs={{0,1},{1,0},{2,3},{3,2},{4,5},{5,4},{6,7},{7,6},{8,9},{9,8},{10,11... | collective-permute-start | bytes 393224 | tf_op jit(solution)/shard_map/ppermute | solution.py:25
  49.0 4.4 %collective-permute-done.8 = bf16[256,256]{0,1:T(8,128)(2,1)S(1)} collective-permute-done((bf16[256,256]{0,1:T(8,128)(2,1)S(1)}, bf16[256,256]{0,1:T(8,128)(2,1)S(1)}, u32[]{:S(2)}, u32[]{:S(2)}) %collective-permute-start.8) | collective-permute-done | bytes 131104 | tf_op jit(solution)/shard_map/ppermute | solution.py:25
  53.7 0.5 broadcast.74
  54.2 1.4 %reduce = bf16[256,256]{1,0:T(8,128)(2,1)S(1)} reduce(bf16[256,1,256]{2,1,0:T(2,128)(2,1)S(1)} %bitcast.42, bf16[]{:T(256)} %broadcast.74), dimensions={1}, to_apply=%bitcast.32.reduce_sub_computation | reduce | bytes 262146
  55.6 0.7 reshape.142
  56.3 4.9 %all-to-all-start = ((bf16[4,2,8192]{2,1,0:T(2,128)(2,1)}), bf16[4,2,8192]{2,1,0:T(2,128)(2,1)S(1)}, u32[]{:S(2)}, u32[]{:S(2)}) async-start(bf16[4,2,8192]{2,1,0:T(2,128)(2,1)} %reshape.142), calls=%async_computation | async-start | bytes 262144 | tf_op jit(solution)/shard_map/all_to_all | solution.py:96
  61.1 2.6 %fusion.4 = bf16[4,256,128]{2,1,0:T(8,128)(2,1)} fusion(bf16[4,256,1280]{1,2,0:T(8,128)(2,1)S(1)} %fusion, bf16[1280,256]{1,0:T(8,128)(2,1)} %copy-done.1), kind=kOutput, calls=%fused_computation.15 | convolution fusion | flops 335806464 | bytes 3211264 | tf_op jit(solution)/shard_map/hbl,ld->hbd/dot_general | solution.py:56
  63.7 3.7 %all-to-all-done = bf16[4,2,8192]{2,1,0:T(2,128)(2,1)S(1)} async-done(((bf16[4,2,8192]{2,1,0:T(2,128)(2,1)}), bf16[4,2,8192]{2,1,0:T(2,128)(2,1)S(1)}, u32[]{:S(2)}, u32[]{:S(2)}) %all-to-all-start) | async-done | bytes 131104 | tf_op jit(solution)/shard_map/all_to_all | solution.py:96
  67.6 0.6 fusion.21
  (29 shorter events, 1.4 us)
Async XLA Ops:
  0.6 29.8 %copy-start = (bf16[4,256,128]{2,1,0:T(8,128)(2,1)S(1)}, bf16[4,256,128]{2,1,0:T(8,128)(2,1)}, u32[]{:S(2)}) copy-start(bf16[4,256,128]{2,1,0:T(8,128)(2,1)} %param.5) | copy-start | bytes 786436
  1.6 7.2 %collective-permute-start = (bf16[256,256]{1,0:T(8,128)(2,1)S(1)}, bf16[256,256]{1,0:T(8,128)(2,1)S(1)}, u32[]{:S(2)}, u32[]{:S(2)}) collective-permute-start(bf16[256,256]{1,0:T(8,128)(2,1)S(1)} %pad_maximum_fusion.1), channel_id=1, source_target_pairs={{0,4},{4,8},{8,12},{12,16},{16,20},{20,24},{24,28},{1,5},{5,9},{9,... | collective-permute-start | bytes 393224 | tf_op jit(solution)/shard_map/ppermute | solution.py:15
  8.8 7.2 %collective-permute-start.1 = (bf16[256,256]{1,0:T(8,128)(2,1)S(1)}, bf16[256,256]{1,0:T(8,128)(2,1)S(1)}, u32[]{:S(2)}, u32[]{:S(2)}) collective-permute-start(bf16[256,256]{1,0:T(8,128)(2,1)S(1)} %collective-permute-done), channel_id=1, source_target_pairs={{0,4},{4,8},{8,12},{12,16},{16,20},{20,24},{24,28},{1,5},{5,9},{9,... | collective-permute-start | bytes 393224 | tf_op jit(solution)/shard_map/ppermute | solution.py:15
  16.0 7.2 %collective-permute-start.2 = (bf16[256,256]{1,0:T(8,128)(2,1)S(1)}, bf16[256,256]{1,0:T(8,128)(2,1)S(1)}, u32[]{:S(2)}, u32[]{:S(2)}) collective-permute-start(bf16[256,256]{1,0:T(8,128)(2,1)S(1)} %collective-permute-done.1), channel_id=1, source_target_pairs={{0,4},{4,8},{8,12},{12,16},{16,20},{20,24},{24,28},{1,5},{5,9},{9,... | collective-permute-start | bytes 393224 | tf_op jit(solution)/shard_map/ppermute | solution.py:15
  23.2 7.2 %collective-permute-start.3 = (bf16[256,256]{1,0:T(8,128)(2,1)S(1)}, bf16[256,256]{1,0:T(8,128)(2,1)S(1)}, u32[]{:S(2)}, u32[]{:S(2)}) collective-permute-start(bf16[256,256]{1,0:T(8,128)(2,1)S(1)} %collective-permute-done.2), channel_id=1, source_target_pairs={{0,4},{4,8},{8,12},{12,16},{16,20},{20,24},{24,28},{1,5},{5,9},{9,... | collective-permute-start | bytes 393224 | tf_op jit(solution)/shard_map/ppermute | solution.py:15
  30.4 3.9 %copy-start.1 = (bf16[1280,256]{1,0:T(8,128)(2,1)}, bf16[1280,256]{1,0:T(8,128)(2,1)S(1)}, u32[]{:S(2)}) copy-start(bf16[1280,256]{1,0:T(8,128)(2,1)S(1)} %constant_dynamic-update-slice_fusion) | copy-start | bytes 1966084
  30.4 1.7 %copy-start.2 = (bf16[4,256,128]{2,1,0:T(8,128)(2,1)S(1)}, bf16[4,256,128]{2,1,0:T(8,128)(2,1)}, u32[]{:S(2)}) copy-start(bf16[4,256,128]{2,1,0:T(8,128)(2,1)} %param.8) | copy-start | bytes 786436
  36.9 7.1 %collective-permute-start.7 = (bf16[256,256]{0,1:T(8,128)(2,1)S(1)}, bf16[256,256]{0,1:T(8,128)(2,1)S(1)}, u32[]{:S(2)}, u32[]{:S(2)}) collective-permute-start(bf16[256,256]{0,1:T(8,128)(2,1)S(1)} %get-tuple-element.6), channel_id=1, source_target_pairs={{16,0},{20,4},{24,8},{28,12},{17,1},{21,5},{25,9},{29,13},{18,2},{... | collective-permute-start | bytes 393224 | tf_op jit(solution)/shard_map/ppermute | solution.py:15
  38.2 6.3 %collective-permute-start.6 = (bf16[256,256]{0,1:T(8,128)(2,1)S(1)}, bf16[256,256]{0,1:T(8,128)(2,1)S(1)}, u32[]{:S(2)}, u32[]{:S(2)}) collective-permute-start(bf16[256,256]{0,1:T(8,128)(2,1)S(1)} %get-tuple-element.7), channel_id=1, source_target_pairs={{12,0},{16,4},{20,8},{24,12},{28,16},{13,1},{17,5},{21,9},{25,13},... | collective-permute-start | bytes 393224 | tf_op jit(solution)/shard_map/ppermute | solution.py:15
  40.1 7.2 %collective-permute-start.5 = (bf16[256,256]{0,1:T(8,128)(2,1)S(1)}, bf16[256,256]{0,1:T(8,128)(2,1)S(1)}, u32[]{:S(2)}, u32[]{:S(2)}) collective-permute-start(bf16[256,256]{0,1:T(8,128)(2,1)S(1)} %get-tuple-element.8), channel_id=1, source_target_pairs={{8,0},{12,4},{16,8},{20,12},{24,16},{28,20},{9,1},{13,5},{17,9},{2... | collective-permute-start | bytes 393224 | tf_op jit(solution)/shard_map/ppermute | solution.py:15
  42.1 5.2 %collective-permute-start.4 = (bf16[256,256]{0,1:T(8,128)(2,1)S(1)}, bf16[256,256]{0,1:T(8,128)(2,1)S(1)}, u32[]{:S(2)}, u32[]{:S(2)}) collective-permute-start(bf16[256,256]{0,1:T(8,128)(2,1)S(1)} %get-tuple-element.5), channel_id=1, source_target_pairs={{4,0},{8,4},{12,8},{16,12},{20,16},{24,20},{28,24},{5,1},{9,5},{13... | collective-permute-start | bytes 393224 | tf_op jit(solution)/shard_map/ppermute | solution.py:15
  47.4 6.0 %collective-permute-start.8 = (bf16[256,256]{0,1:T(8,128)(2,1)S(1)}, bf16[256,256]{0,1:T(8,128)(2,1)S(1)}, u32[]{:S(2)}, u32[]{:S(2)}) collective-permute-start(bf16[256,256]{0,1:T(8,128)(2,1)S(1)} %get-tuple-element.3), channel_id=1, source_target_pairs={{0,1},{1,0},{2,3},{3,2},{4,5},{5,4},{6,7},{7,6},{8,9},{9,8},{10,11... | collective-permute-start | bytes 393224 | tf_op jit(solution)/shard_map/ppermute | solution.py:25
  56.3 11.2 %all-to-all-start = ((bf16[4,2,8192]{2,1,0:T(2,128)(2,1)}), bf16[4,2,8192]{2,1,0:T(2,128)(2,1)S(1)}, u32[]{:S(2)}, u32[]{:S(2)}) async-start(bf16[4,2,8192]{2,1,0:T(2,128)(2,1)} %reshape.142), calls=%async_computation | async-start | bytes 262144 | tf_op jit(solution)/shard_map/all_to_all | solution.py:96
where the time goes:
time: 68.7 us; the launch traced here: 68.2 us
  waiting for transfers between devices  29.2 us (43%)
  starting transfers between devices  21.2 us (31%)
  matrix products  8.13 us (12%)
  other arithmetic  4.47 us (7%)
  local copies, waits for them, and re-layouts  4.25 us (6%)
  between operations  0.96 us (1%)
    ppermute x8, waiting for transfers between devices, shifted(): return lax.ppermute(block, axis, route)  21.1 us
    ppermute x8, starting transfers between devices, shifted(): return lax.ppermute(block, axis, route)  14.7 us
    all_to_all x1, starting transfers between devices, per_device(): lax.all_to_all(for_sending(pair_total[None]), 'head', split_axis=1, conca...  4.87 us
    ppermute x1, waiting for transfers between devices, from_partner(): return lax.ppermute(value, axis, pairs)  4.4 us
    all_to_all x1, waiting for transfers between devices, per_device(): lax.all_to_all(for_sending(pair_total[None]), 'head', split_axis=1, conca...  3.72 us
    dot_general x1, matrix products, window_terms(): jnp.einsum('hbl,ld->hbd', dscores, key_rows, preferred_element_type=jnp.f...  2.57 us
    unnamed x15, local copies, waits for them, and re-layouts  2.48 us
    ppermute x1, starting transfers between devices, from_partner(): return lax.ppermute(value, axis, pairs)  1.63 us
  transfers between devices with their start and end apart: 10, of which 8 were waited for; matrix products, arithmetic and copies ran while one was open for 8% of the time, Pallas kernels for 0%

commit v1 on v0

v1 whole, which is shorter than its diff:
```python
import functools
import math

import jax
import jax.numpy as jnp
from jax import lax
from jax.experimental import pallas as pl
from jax.experimental.pallas import tpu as pltpu
from jax.sharding import PartitionSpec as P

GROUP = 8
REACH = 4
MASKED = -1e30
NT = (((1,), (1,)), ((), ()))
NN = (((1,), (0,)), ((), ()))


def dot(a, b, dims):
    return lax.dot_general(a, b, dims, preferred_element_type=jnp.float32)


def attention_body(reach, blocks, ctx_ref, lengths_ref, q_ref, g_ref, kv_ref, dq_ref, terms_ref,
                   s_ref, dp_ref, p_ref, ds_ref, kt_ref):
    heads, tokens, width = q_ref.shape
    scale = width ** -0.5
    here = ctx_ref[0]
    row_pos = here * tokens + lax.broadcasted_iota(jnp.int32, (1, tokens), 1)
    doc_start = jnp.zeros((1, tokens), jnp.int32)
    end = jnp.int32(0)
    for d in range(lengths_ref.shape[0]):
        end = end + lengths_ref[d]
        doc_start = jnp.where(row_pos >= end, end, doc_start)
    key_iota = lax.broadcasted_iota(jnp.int32, (tokens, 1), 0)
    slots = [lax.rem(here - back + blocks, blocks) for back in range(reach + 1)]
    for back in range(reach + 1):
        kt_ref[back] = kv_ref[slots[back], :, :width].T

    for h in range(heads):
        q = q_ref[h]
        g = g_ref[h]
        top = jnp.full((1, tokens), MASKED, jnp.float32)
        for back in range(reach + 1):
            s = dot(kv_ref[slots[back], :, :width], q, NT)
            key_pos = (here - back) * tokens + key_iota
            allowed = key_pos >= doc_start
            if back == 0:
                allowed = allowed & (key_pos <= row_pos)
            s = jnp.where(allowed, s, MASKED)
            s_ref[back] = s
            top = jnp.maximum(top, jnp.max(s, axis=0, keepdims=True))
        factor = scale * math.log2(math.e)
        total = jnp.zeros((1, tokens), jnp.float32)
        for back in range(reach + 1):
            e = jnp.exp2((s_ref[back] - top) * factor)
            s_ref[back] = e
            total = total + jnp.sum(e, axis=0, keepdims=True)
        inverse = 1.0 / total
        delta = jnp.zeros((1, tokens), jnp.float32)
        for back in range(reach + 1):
            dp = dot(kv_ref[slots[back], :, width:], g, NT)
            p = s_ref[back] * inverse
            p_ref[back, :, h * tokens:(h + 1) * tokens] = p.astype(jnp.bfloat16)
            s_ref[back] = p
            dp_ref[back] = dp
            delta = delta + jnp.sum(p * dp, axis=0, keepdims=True)
        dqt = jnp.zeros((width, tokens), jnp.float32)
        for back in range(reach + 1):
            ds = (s_ref[back] * (dp_ref[back] - delta)).astype(jnp.bfloat16)
            ds_ref[back, :, h * tokens:(h + 1) * tokens] = ds
            dqt = dqt + dot(kt_ref[back], ds, NN)
        dq_ref[h] = (dqt.T * scale).astype(dq_ref.dtype)

    q_all = q_ref[...].reshape(heads * tokens, width)
    g_all = g_ref[...].reshape(heads * tokens, width)
    for back in range(blocks):
        slot = lax.rem(here - back + blocks, blocks)
        if back <= reach:
            dk = dot(ds_ref[back], q_all, NN) * scale
            dv = dot(p_ref[back], g_all, NN)
            terms_ref[slot, :, :width] = dk.astype(terms_ref.dtype)
            terms_ref[slot, :, width:] = dv.astype(terms_ref.dtype)
        else:
            terms_ref[slot] = jnp.zeros(terms_ref.shape[1:], terms_ref.dtype)


def attention_terms(ctx, lengths, queries, d_out, gathered, reach):
    heads, tokens, width = queries.shape
    blocks = gathered.shape[0]
    span = reach + 1
    vmem = pl.BlockSpec(memory_space=pltpu.VMEM)
    smem = pl.BlockSpec(memory_space=pltpu.SMEM)
    flops = 2 * 5 * heads * tokens * span * tokens * width
    moved = 2 * (3 * queries.size + 2 * gathered.size)
    return pl.pallas_call(
        functools.partial(attention_body, reach, blocks),
        out_shape=(
            jax.ShapeDtypeStruct(queries.shape, jnp.bfloat16),
            jax.ShapeDtypeStruct(gathered.shape, jnp.bfloat16),
        ),
        in_specs=[smem, smem, vmem, vmem, vmem],
        out_specs=(vmem, vmem),
        scratch_shapes=[
            pltpu.VMEM((span, tokens, tokens), jnp.float32),
            pltpu.VMEM((span, tokens, tokens), jnp.float32),
            pltpu.VMEM((span, tokens, heads * tokens), jnp.bfloat16),
            pltpu.VMEM((span, tokens, heads * tokens), jnp.bfloat16),
            pltpu.VMEM((span, width, tokens), jnp.bfloat16),
        ],
        compiler_params=pltpu.CompilerParams(vmem_limit_bytes=40 * 2**20),
        cost_estimate=pl.CostEstimate(
            flops=flops, bytes_accessed=moved,
            transcendentals=heads * tokens * span * tokens),
        name="attention_terms",
    )(ctx, lengths, queries, d_out, gathered)


def per_device(queries, keys, values, d_out, doc_lengths):
    heads_here, tokens, width = queries.shape
    ctx_count = lax.axis_size("ctx")
    head_count = lax.axis_size("head")
    reach = min(REACH, ctx_count // 2)
    group = lax.axis_index("head") * heads_here // GROUP
    own = jnp.concatenate(
        [lax.dynamic_index_in_dim(keys, group, 0, keepdims=False),
         lax.dynamic_index_in_dim(values, group, 0, keepdims=False)], axis=1)
    gathered = lax.all_gather(own, "ctx")
    ctx = jnp.reshape(lax.axis_index("ctx"), (1,))
    d_queries, terms = attention_terms(ctx, doc_lengths, queries, d_out, gathered, reach)
    sums = lax.psum_scatter(terms, "ctx", scatter_dimension=0)
    pieces = lax.all_to_all(
        sums.reshape(head_count, tokens // head_count, 2 * width), "head", 0, 0)
    share = GROUP // heads_here
    pieces = pieces.reshape(head_count // share, share, tokens // head_count, 2 * width)
    group_sums = jnp.sum(pieces.astype(jnp.float32), axis=1).astype(jnp.bfloat16)
    return d_queries, group_sums[..., :width], group_sums[..., width:]


def solution(mesh):
    placed = (
        P("head", "ctx", None),
        P(None, "ctx", None),
        P(None, "ctx", None),
        P("head", "ctx", None),
        P(),
    )
    return jax.shard_map(
        per_device,
        mesh=mesh,
        in_specs=placed,
        out_specs=(
            P("head", "ctx", None),
            P(None, ("ctx", "head"), None),
            P(None, ("ctx", "head"), None),
        ),
        check_vma=False,
    )
```

time: 68.7 us -> 100 us (1.46)
  the two profiles are of different devices: /device:TPU:4 before, /device:TPU:0 now
where the time goes in v1:
time: 100 us
  waiting for transfers between devices  63.9 us (64%)
  between operations  14.1 us (14%)
  blocking collectives  10.7 us (11%)
  Pallas kernels  7.09 us (7%)
  local copies, waits for them, and re-layouts  3.45 us (3%)
    reduce_scatter x1, waiting for transfers between devices, per_device(): sums = lax.psum_scatter(terms, 'ctx', scatter_dimension=0)  36.2 us
    all_gather x1, waiting for transfers between devices, per_device(): gathered = lax.all_gather(own, 'ctx')  27.8 us
    all_to_all x1, blocking collectives, per_device(): lax.all_to_all(sums.reshape(head_count, tokens // head_count, 2 * width),...  10.7 us
    pallas_call x1, Pallas kernels, attention_terms(): pl.pallas_call(functools.partial(attention_body, reach, blocks), out_shap...  7.09 us
  transfers between devices with their start and end apart: 2, of which 2 were waited for; matrix products, arithmetic and copies ran while one was open for 0% of the time, Pallas kernels for 0%

profile of v1, /device:TPU:0, one launch (start us, length us, event | category | flops | bytes accessed | tf_op | source)
XLA Modules:
  0.0 100.0 jit_solution(15751127401929232170)
XLA Ops:
  7.2 0.0 all-gather.3.cloned.1.call-start
  7.2 0.0 copy-start.2
  7.2 0.9 dynamic-slice_bitcast_fusion
  8.2 0.0 copy-start.1
  8.2 0.7 pad_maximum_fusion
  8.9 0.0 all-gather.3.cloned.1.call-update
  8.9 0.0 reduce-scatter.2.cloned.1.call-start
  8.9 27.8 %all-gather.3.cloned.1.call-done = bf16[2048,256]{1,0:T(8,128)(2,1)} async-done(((bf16[256,256]{1,0:T(8,128)(2,1)}), bf16[2048,256]{1,0:T(8,128)(2,1)}) %all-gather.3.cloned.1.call-update) | async-done | bytes 1048592 | tf_op jit(solution)/shard_map/all_gather | solution.py:126
  36.7 0.0 copy-start.3
  36.7 0.0 copy-done.2
  36.7 0.0 copy-done.1
  36.7 0.6 copy-done.3
  37.3 0.0 copy-start
  37.3 1.2 %copy-done = bf16[2048,256]{1,0:T(8,128)(2,1)S(1)} copy-done((bf16[2048,256]{1,0:T(8,128)(2,1)S(1)}, bf16[2048,256]{1,0:T(8,128)(2,1)}, u32[]{:S(2)}) %copy-start) | copy-done | bytes 1048600
  38.6 7.1 %attention_terms.1 = (bf16[4,256,128]{2,1,0:T(8,128)(2,1)}, bf16[8,256,256]{2,1,0:T(8,128)(2,1)}) custom-call(s32[1]{0:T(128)} %bitcast.ctx_ref, s32[4]{0:T(128)S(1)} %copy-done.3, bf16[4,256,128]{2,1,0:T(8,128)(2,1)S(1)} %copy-done.1, bf16[4,256,128]{2,1,0:T(8,128)(2,1)S(1)} %copy-done.2, bf16[8,256,256]{2,1,0:T(8,128)(2,1)S(1)} %bitcast.9), custom_call_target="tpu_custom_call" | custom-call | flops 1677721600 | bytes 2883584 | tf_op jit(solution)/shard_map/attention_terms/pallas_call | solution.py:94
  45.7 0.0 reduce-scatter.2.cloned.1.call-update
  45.7 36.2 %reduce-scatter.2.cloned.1.call-done = bf16[1,256,256]{2,1,0:T(8,128)(2,1)} async-done(((bf16[8,256,256]{2,1,0:T(8,128)(2,1)}), bf16[1,256,256]{2,1,0:T(8,128)(2,1)}) %reduce-scatter.2.cloned.1.call-update) | async-done | bytes 131088 | tf_op jit(solution)/shard_map/reduce_scatter | solution.py:129
  81.8 10.7 %all_to_all.5 = bf16[4,64,256]{2,1,0:T(8,128)(2,1)S(1)} all-to-all(bf16[4,64,256]{2,1,0:T(8,128)(2,1)} %bitcast.10), channel_id=1, replica_groups=mesh['ctx'=8,'head'=4] {'head'}, dimensions={0} | all-to-all | bytes 262144 | tf_op jit(solution)/shard_map/all_to_all | solution.py:130
  92.5 0.6 fusion
  (1 shorter events, 0.0 us)
Async XLA Ops:
  7.2 29.5 %all-gather.3.cloned.1.call-start = ((), (), s32[]{:S(2)}) async-start(), calls=%async_computation.3 | async-start | bytes 1179648 | tf_op jit(solution)/shard_map/all_gather | solution.py:126
  7.2 29.5 %copy-start.2 = (bf16[4,256,128]{2,1,0:T(8,128)(2,1)S(1)}, bf16[4,256,128]{2,1,0:T(8,128)(2,1)}, u32[]{:S(2)}) copy-start(bf16[4,256,128]{2,1,0:T(8,128)(2,1)} %g_ref.1) | copy-start | bytes 786436
  8.2 28.5 %copy-start.1 = (bf16[4,256,128]{2,1,0:T(8,128)(2,1)S(1)}, bf16[4,256,128]{2,1,0:T(8,128)(2,1)}, u32[]{:S(2)}) copy-start(bf16[4,256,128]{2,1,0:T(8,128)(2,1)} %q_ref.1) | copy-start | bytes 786436
  8.9 73.0 %reduce-scatter.2.cloned.1.call-start = ((), (), s32[]{:S(2)}) async-start(), calls=%async_computation.2 | async-start | bytes 1179648 | tf_op jit(solution)/shard_map/reduce_scatter | solution.py:129
  36.7 0.7 copy-start.3
  37.3 1.2 %copy-start = (bf16[2048,256]{1,0:T(8,128)(2,1)S(1)}, bf16[2048,256]{1,0:T(8,128)(2,1)}, u32[]{:S(2)}) copy-start(bf16[2048,256]{1,0:T(8,128)(2,1)} %all-gather.3.cloned.1.call-done) | copy-start | bytes 3145732
Sparse Core Ops, SparseCore 0:
  10.5 26.1 all-gather.2
  45.8 35.9 reduce-scatter.1

commit v2 on v1

v2 whole, which is shorter than its diff:
```python
import functools
import math

import jax
import jax.numpy as jnp
from jax import lax
from jax.experimental import pallas as pl
from jax.experimental.pallas import tpu as pltpu
from jax.sharding import PartitionSpec as P

GROUP = 8
REACH = 4
MASKED = -1e30
NT = (((1,), (1,)), ((), ()))
NN = (((1,), (0,)), ((), ()))
VMEM = pl.BlockSpec(memory_space=pltpu.VMEM)
SMEM = pl.BlockSpec(memory_space=pltpu.SMEM)
PARAMS = pltpu.CompilerParams(vmem_limit_bytes=24 * 2**20)


def dot(a, b, dims):
    return lax.dot_general(a, b, dims, preferred_element_type=jnp.float32)


def shifted(block, distance):
    count = lax.axis_size("ctx")
    route = [(i - distance, i) for i in range(count) if 0 <= i - distance < count]
    return lax.ppermute(block, "ctx", route)


def exchanged(block, axis, mask):
    return lax.ppermute(block, axis, [(i, i ^ mask) for i in range(lax.axis_size(axis))])


def scores_body(ctx_ref, lengths_ref, q_ref, g_ref, own_ref, two_ref, four_ref, odd_ref,
                ds_ref, p_ref, odd_terms_ref, s_ref, dp_ref, odd_p_ref):
    heads, tokens, width = q_ref.shape
    scale = width ** -0.5
    here = ctx_ref[0]
    row_pos = here * tokens + lax.broadcasted_iota(jnp.int32, (1, tokens), 1)
    doc_start = jnp.zeros((1, tokens), jnp.int32)
    end = jnp.int32(0)
    for d in range(lengths_ref.shape[0]):
        end = end + lengths_ref[d]
        doc_start = jnp.where(row_pos >= end, end, doc_start)
    key_iota = lax.broadcasted_iota(jnp.int32, (tokens, 1), 0)
    window = [own_ref, odd_ref.at[:tokens], two_ref, odd_ref.at[tokens:], four_ref]

    for h in range(heads):
        q = q_ref[h]
        g = g_ref[h]
        lanes = slice(h * tokens, (h + 1) * tokens)
        top = jnp.full((1, tokens), MASKED, jnp.float32)
        for back, pair in enumerate(window):
            s = dot(pair[:, :width], q, NT)
            key_pos = (here - back) * tokens + key_iota
            allowed = key_pos >= doc_start
            if back == 0:
                allowed = allowed & (key_pos <= row_pos)
            s = jnp.where(allowed, s, MASKED)
            s_ref[back] = s
            top = jnp.maximum(top, jnp.max(s, axis=0, keepdims=True))
        factor = scale * math.log2(math.e)
        total = jnp.zeros((1, tokens), jnp.float32)
        for back in range(len(window)):
            e = jnp.exp2((s_ref[back] - top) * factor)
            s_ref[back] = e
            total = total + jnp.sum(e, axis=0, keepdims=True)
        inverse = 1.0 / total
        delta = jnp.zeros((1, tokens), jnp.float32)
        for back, pair in enumerate(window):
            dp = dot(pair[:, width:], g, NT)
            p = s_ref[back] * inverse
            if back % 2:
                odd_p_ref[back // 2, :, lanes] = p.astype(jnp.bfloat16)
            else:
                p_ref[back // 2, :, lanes] = p.astype(jnp.bfloat16)
            s_ref[back] = p
            dp_ref[back] = dp
            delta = delta + jnp.sum(p * dp, axis=0, keepdims=True)
        for back in range(len(window)):
            ds = (s_ref[back] * (dp_ref[back] - delta)).astype(jnp.bfloat16)
            ds_ref[back, :, lanes] = ds

    q_all = q_ref[...].reshape(heads * tokens, width)
    g_all = g_ref[...].reshape(heads * tokens, width)
    for odd in range(len(window) // 2):
        rows = slice(odd * tokens, (odd + 1) * tokens)
        dk = dot(ds_ref[2 * odd + 1], q_all, NN) * scale
        dv = dot(odd_p_ref[odd], g_all, NN)
        odd_terms_ref[rows, :width] = dk.astype(jnp.bfloat16)
        odd_terms_ref[rows, width:] = dv.astype(jnp.bfloat16)


def even_body(ds_ref, p_ref, q_ref, g_ref, *terms_refs):
    heads, tokens, width = q_ref.shape
    q_all = q_ref[...].reshape(heads * tokens, width)
    g_all = g_ref[...].reshape(heads * tokens, width)
    for at, terms_ref in enumerate(terms_refs, 1):
        terms_ref[:, :width] = dot(ds_ref[2 * at], q_all, NN) * width ** -0.5
        terms_ref[:, width:] = dot(p_ref[at], g_all, NN)


def own_body(ds_ref, p_ref, q_ref, g_ref, own_ref, two_ref, four_ref, odd_ref,
             dq_ref, terms_ref):
    heads, tokens, width = q_ref.shape
    scale = width ** -0.5
    q_all = q_ref[...].reshape(heads * tokens, width)
    g_all = g_ref[...].reshape(heads * tokens, width)
    terms_ref[:, :width] = dot(ds_ref[0], q_all, NN) * scale
    terms_ref[:, width:] = dot(p_ref[0], g_all, NN)
    window = [own_ref, odd_ref.at[:tokens], two_ref, odd_ref.at[tokens:], four_ref]
    turned = [pair[:, :width].T for pair in window]
    for h in range(heads):
        lanes = slice(h * tokens, (h + 1) * tokens)
        dqt = jnp.zeros((width, tokens), jnp.float32)
        for back in range(len(window)):
            dqt = dqt + dot(turned[back], ds_ref[back, :, lanes], NN)
        dq_ref[h] = (dqt.T * scale).astype(dq_ref.dtype)


def per_device(queries, keys, values, d_out, doc_lengths):
    heads_here, tokens, width = queries.shape
    head_count = lax.axis_size("head")
    share = GROUP // heads_here
    groups = head_count // share
    blocks = REACH + 1
    ctx = lax.axis_index("ctx")
    head = lax.axis_index("head")
    second_core = ctx % 2 == 1
    bf16, f32 = jnp.bfloat16, jnp.float32

    own = jnp.concatenate(
        [lax.dynamic_index_in_dim(keys, head // share, 0, keepdims=False),
         lax.dynamic_index_in_dim(values, head // share, 0, keepdims=False)], axis=1)
    four = shifted(own, 4)
    two = shifted(own, 2)
    odd = exchanged(
        jnp.concatenate([jnp.where(second_core, two, own), jnp.where(second_core, four, two)]),
        "ctx", 1)

    work = heads_here * tokens * tokens * width * 2
    ds, p, odd_terms = pl.pallas_call(
        scores_body,
        out_shape=(
            jax.ShapeDtypeStruct((blocks, tokens, heads_here * tokens), bf16),
            jax.ShapeDtypeStruct((blocks // 2 + 1, tokens, heads_here * tokens), bf16),
            jax.ShapeDtypeStruct((2 * tokens, 2 * width), bf16),
        ),
        in_specs=[SMEM, SMEM] + [VMEM] * 6,
        out_specs=(VMEM, VMEM, VMEM),
        scratch_shapes=[
            pltpu.VMEM((blocks, tokens, tokens), f32),
            pltpu.VMEM((blocks, tokens, tokens), f32),
            pltpu.VMEM((blocks // 2, tokens, heads_here * tokens), bf16),
        ],
        compiler_params=PARAMS,
        cost_estimate=pl.CostEstimate(
            flops=work * (2 * blocks + 4), bytes_accessed=2**20, transcendentals=0),
        name="scores",
    )(ctx.reshape(1), doc_lengths, queries, d_out, own, two, four, odd)
    odd_back = exchanged(odd_terms, "ctx", 1)
    even_terms = pl.pallas_call(
        even_body,
        out_shape=(jax.ShapeDtypeStruct((tokens, 2 * width), f32),) * (REACH // 2),
        in_specs=[VMEM] * 4,
        out_specs=(VMEM,) * (REACH // 2),
        compiler_params=PARAMS,
        cost_estimate=pl.CostEstimate(
            flops=work * REACH, bytes_accessed=2**20, transcendentals=0),
        name="even_terms",
    )(ds, p, queries, d_out)
    near, far = odd_back[:tokens].astype(f32), odd_back[tokens:].astype(f32)
    four_back = shifted(
        (even_terms[1] + jnp.where(second_core, far, 0.0)).astype(bf16), -4)
    two_back = shifted(
        (even_terms[0] + jnp.where(second_core, near, far)).astype(bf16), -2)
    d_queries, own_terms = pl.pallas_call(
        own_body,
        out_shape=(
            jax.ShapeDtypeStruct(queries.shape, bf16),
            jax.ShapeDtypeStruct((tokens, 2 * width), f32),
        ),
        in_specs=[VMEM] * 8,
        out_specs=(VMEM, VMEM),
        compiler_params=PARAMS,
        cost_estimate=pl.CostEstimate(
            flops=work * (blocks + 2), bytes_accessed=2**20, transcendentals=0),
        name="own_terms",
    )(ds, p, queries, d_out, own, two, four, odd)
    sums = (own_terms + jnp.where(second_core, 0.0, near)
            + two_back.astype(f32) + four_back.astype(f32))

    sums = sums.reshape(groups, share, tokens // head_count, 2 * width)
    mine = head % share
    kept = lax.dynamic_index_in_dim(sums, mine, 1, keepdims=False)
    given = lax.dynamic_index_in_dim(sums, 1 - mine, 1, keepdims=False)
    kept = kept + exchanged(given.astype(bf16), "head", 1).astype(f32)
    kept = kept.astype(bf16)
    if groups == 2:
        at = head // share
        here = lax.dynamic_index_in_dim(kept, at, 0, keepdims=False)
        there = exchanged(
            lax.dynamic_index_in_dim(kept, 1 - at, 0, keepdims=False), "head", share)
        first = jnp.where(at == 0, here, there)
        second = jnp.where(at == 0, there, here)
        result = jnp.stack([first, second])
    else:
        result = lax.all_to_all(
            kept, "head", 0, 0, tiled=True,
            axis_index_groups=[list(range(u, head_count, share)) for u in range(share)])
    return d_queries, result[..., :width], result[..., width:]


def solution(mesh):
    placed = (
        P("head", "ctx", None),
        P(None, "ctx", None),
        P(None, "ctx", None),
        P("head", "ctx", None),
        P(),
    )
    return jax.shard_map(
        per_device,
        mesh=mesh,
        in_specs=placed,
        out_specs=(
            P("head", "ctx", None),
            P(None, ("ctx", "head"), None),
            P(None, ("ctx", "head"), None),
        ),
        check_vma=False,
    )
```

time: 100 us -> 45.6 us (0.46)
  waiting for transfers between devices: 63.9 us -> 12.6 us
  starting transfers between devices: 0.08 us -> 15.4 us
  between operations: 14.1 us -> 0.83 us
  blocking collectives: 10.7 us -> 0 us
  local copies, waits for them, and re-layouts: 3.45 us -> 5.98 us
  other arithmetic: 0.69 us -> 2.58 us
    reduce_scatter x1 -> x0, waiting for transfers between devices: 36.2 us -> none  [per_device(): sums = lax.psum_scatter(terms, 'ctx', scatter_dimension=0)]
    all_gather x1 -> x0, waiting for transfers between devices: 27.8 us -> none  [per_device(): gathered = lax.all_gather(own, 'ctx')]
    ppermute x0 -> x8, starting transfers between devices: none -> 15.4 us  [the longest x4 10.9 us: shifted(): return lax.ppermute(block, 'ctx', route)]
    ppermute x0 -> x8, waiting for transfers between devices: none -> 12.6 us  [the longest x4 7.14 us: exchanged(): lax.ppermute(block, axis, [(i, i ^ mask) for i in range(lax.axis_size(axi...]
    all_to_all x1 -> x0, blocking collectives: 10.7 us -> none  [per_device(): lax.all_to_all(sums.reshape(head_count, tokens // head_count, 2 * width),...]
    unnamed x8 -> x22, local copies, waits for them, and re-layouts: 1.88 us -> 5.02 us
    add x0 -> x1, other arithmetic: none -> 1.03 us  [per_device(): own_terms + jnp.where(second_core, 0.0, near) + two_back.astype(f32)]
    pallas_call x1 -> x3, Pallas kernels: 7.09 us -> 7.48 us  [the longest x1 5.21 us: per_device(): pl.pallas_call(scores_body, out_shape=(jax.ShapeDtypeStruct((blocks, toke...]
  transfers between devices with their start and end apart: 2 -> 8, of which waited for: 2 -> 7; matrix products, arithmetic and copies ran while one was open for 0% -> 0% of each run, Pallas kernels for 0% -> 5%
where the time goes in v2:
time: 45.6 us; the launch traced here: 44.9 us
  starting transfers between devices  15.4 us (34%)
  waiting for transfers between devices  12.6 us (28%)
  Pallas kernels  7.48 us (16%)
  local copies, waits for them, and re-layouts  5.98 us (13%)
  other arithmetic  2.58 us (6%)
  between operations  0.83 us (2%)
    ppermute x4, starting transfers between devices, shifted(): return lax.ppermute(block, 'ctx', route)  10.9 us
    ppermute x4, waiting for transfers between devices, exchanged(): lax.ppermute(block, axis, [(i, i ^ mask) for i in range(lax.axis_size(axi...  7.14 us
    ppermute x4, waiting for transfers between devices, shifted(): return lax.ppermute(block, 'ctx', route)  5.5 us
    pallas_call x1, Pallas kernels, per_device(): pl.pallas_call(scores_body, out_shape=(jax.ShapeDtypeStruct((blocks, toke...  5.21 us
    unnamed x22, local copies, waits for them, and re-layouts  5.02 us
    ppermute x4, starting transfers between devices, exchanged(): lax.ppermute(block, axis, [(i, i ^ mask) for i in range(lax.axis_size(axi...  4.55 us
    pallas_call x1, Pallas kernels, per_device(): pl.pallas_call(own_body, out_shape=(jax.ShapeDtypeStruct(queries.shape, b...  1.57 us
    add x1, other arithmetic, per_device(): own_terms + jnp.where(second_core, 0.0, near) + two_back.astype(f32)  1.03 us
  transfers between devices with their start and end apart: 8, of which 7 were waited for; matrix products, arithmetic and copies ran while one was open for 0% of the time, Pallas kernels for 5%

profile of v2, /device:TPU:0, one launch (start us, length us, event | category | flops | bytes accessed | tf_op | source)
XLA Modules:
  0.0 44.9 jit_solution(357718589513578343)
XLA Ops:
  0.6 0.0 copy-start.3
  0.7 0.9 %dynamic-slice_bitcast_fusion = (bf16[256,128]{1,0:T(8,128)(2,1)S(1)}, bf16[256,128]{1,0:T(8,128)(2,1)S(1)}) fusion(bf16[2,256,128]{2,1,0:T(8,128)(2,1)} %param.7, s32[]{:T(128)S(6)} %select_n.77, bf16[2,256,128]{2,1,0:T(8,128)(2,1)} %param.6), kind=kLoop, calls=%fused_computation.20 | loop fusion | bytes 262148 | tf_op jit(solution)/shard_map/jit(dynamic_index_in_dim)/squeeze | solution.py:135
  1.6 4.8 %collective-permute-start = (bf16[256,256]{1,0:T(8,128)(2,1)S(1)}, bf16[256,256]{1,0:T(8,128)(2,1)S(1)}, u32[]{:S(2)}, u32[]{:S(2)}) collective-permute-start(bf16[256,256]{1,0:T(8,128)(2,1)S(1)} %pad_maximum_fusion.1.own_ref), channel_id=1, source_target_pairs={{0,8},{4,12},{8,16},{12,20},{16,24},{20,28},{1,9},{5,13},{9,17},{1... | collective-permute-start | bytes 393224 | tf_op jit(solution)/shard_map/ppermute | solution.py:28
  6.5 3.4 %collective-permute-start.1 = (bf16[256,256]{1,0:T(8,128)(2,1)S(1)}, bf16[256,256]{1,0:T(8,128)(2,1)S(1)}, u32[]{:S(2)}, u32[]{:S(2)}) collective-permute-start(bf16[256,256]{1,0:T(8,128)(2,1)S(1)} %pad_maximum_fusion.1.own_ref), channel_id=1, source_target_pairs={{0,16},{4,20},{8,24},{12,28},{1,17},{5,21},{9,25},{13,29},{2,18},{... | collective-permute-start | bytes 393224 | tf_op jit(solution)/shard_map/ppermute | solution.py:28
  9.9 0.0 collective-permute-done.two_ref
  9.9 3.0 %collective-permute-done.1.four_ref = bf16[256,256]{1,0:T(8,128)(2,1)S(1)} collective-permute-done((bf16[256,256]{1,0:T(8,128)(2,1)S(1)}, bf16[256,256]{1,0:T(8,128)(2,1)S(1)}, u32[]{:S(2)}, u32[]{:S(2)}) %collective-permute-start.1) | collective-permute-done | bytes 131104 | tf_op jit(solution)/shard_map/ppermute | solution.py:28
  12.9 0.1 broadcast_select_fusion.1
  13.0 0.1 collective-permute-start.2
  13.1 1.5 %collective-permute-done.2.odd_ref = bf16[512,256]{1,0:T(8,128)(2,1)S(1)} collective-permute-done((bf16[512,256]{1,0:T(8,128)(2,1)S(1)}, bf16[512,256]{1,0:T(8,128)(2,1)S(1)}, u32[]{:S(2)}, u32[]{:S(2)}) %collective-permute-start.2) | collective-permute-done | bytes 262176 | tf_op jit(solution)/shard_map/ppermute | solution.py:32
  14.6 1.0 %copy-done.2 = bf16[4,256,128]{2,1,0:T(8,128)(2,1)S(1)} copy-done((bf16[4,256,128]{2,1,0:T(8,128)(2,1)S(1)}, bf16[4,256,128]{2,1,0:T(8,128)(2,1)}, u32[]{:S(2)}) %copy-start.2) | copy-done | bytes 262168
  15.7 0.9 %copy-done.4 = bf16[4,256,128]{2,1,0:T(8,128)(2,1)S(1)} copy-done((bf16[4,256,128]{2,1,0:T(8,128)(2,1)S(1)}, bf16[4,256,128]{2,1,0:T(8,128)(2,1)}, u32[]{:S(2)}) %copy-start.4) | copy-done | bytes 262168
  16.6 0.7 %copy-done.8 = s32[4]{0:T(128)S(1)} copy-done((s32[4]{0:T(128)S(1)}, s32[4]{0:T(128)}, u32[]{:S(2)}) %copy-start.8) | copy-done | bytes 40
  17.3 5.2 %scores.1 = (bf16[5,256,1024]{2,1,0:T(8,128)(2,1)S(1)}, bf16[3,256,1024]{2,1,0:T(8,128)(2,1)S(1)}, bf16[512,256]{1,0:T(8,128)(2,1)S(1)}) custom-call(s32[1]{0:T(128)} %bitcast.ctx_ref, s32[4]{0:T(128)S(1)} %copy-done.8, bf16[4,256,128]{2,1,0:T(8,128)(2,1)S(1)} %copy-done.2, bf16[4,256,128]{2,1,0:T(8,128)(2,1)S(1)} %copy-done.4, ...), custom_call_target="tpu_custom_call" | custom-call | flops 939524096 | bytes 1048576 | tf_op jit(solution)/shard_map/scores/pallas_call | solution.py:143
  22.5 0.0 copy-start
  22.5 0.2 collective-permute-start.3
  22.7 0.7 %even_terms.1 = (f32[256,256]{1,0:T(8,128)S(1)}, f32[256,256]{1,0:T(8,128)S(1)}) custom-call(bf16[5,256,1024]{2,1,0:T(8,128)(2,1)S(1)} %get-tuple-element.10.ds_ref, bf16[3,256,1024]{2,1,0:T(8,128)(2,1)S(1)} %get-tuple-element.11.p_ref, bf16[4,256,128]{2,1,0:T(8,128)(2,1)S(1)} %copy-done.3, bf16[4,256,128]{2,1,0:T(8,128)(2,1)S(1)} %copy-done.4), custom_call_target="tpu_custom_call" | custom-call | flops 268435456 | bytes 1048576 | tf_op jit(solution)/shard_map/even_terms/pallas_call | solution.py:163
  23.4 0.7 %collective-permute-done.3 = bf16[512,256]{1,0:T(8,128)(2,1)S(1)} collective-permute-done((bf16[512,256]{1,0:T(8,128)(2,1)S(1)}, bf16[512,256]{1,0:T(8,128)(2,1)S(1)}, u32[]{:S(2)}, u32[]{:S(2)}) %collective-permute-start.3) | collective-permute-done | bytes 262176 | tf_op jit(solution)/shard_map/ppermute | solution.py:32
  24.1 0.8 %fusion.4 = (bf16[256,256]{1,0:T(8,128)(2,1)}, bf16[256,256]{1,0:T(8,128)(2,1)}) fusion(f32[256,256]{1,0:T(8,128)S(1)} %get-tuple-element.15, pred[]{:T(512)S(6)} %eq.10, bf16[512,256]{1,0:T(8,128)(2,1)S(1)} %collective-permute-done.3, f32[256,256]{1,0:T(8,128)S(1)} %get-tuple-element.16), kind=kLoop, calls=%fused_computation.7 | loop fusion | flops 524288 | bytes 1048577 | tf_op jit(solution)/shard_map/convert_element_type | solution.py:177
  24.9 1.3 %collective-permute-start.5 = (bf16[256,256]{1,0:T(8,128)(2,1)}, bf16[256,256]{1,0:T(8,128)(2,1)}, u32[]{:S(2)}, u32[]{:S(2)}) collective-permute-start(bf16[256,256]{1,0:T(8,128)(2,1)} %get-tuple-element.18), channel_id=1, source_target_pairs={{16,0},{20,4},{24,8},{28,12},{17,1},{21,5},{25,9},{29,13},{18,2},{... | collective-permute-start | bytes 393224 | tf_op jit(solution)/shard_map/ppermute | solution.py:28
  26.2 1.3 %collective-permute-start.4 = (bf16[256,256]{1,0:T(8,128)(2,1)}, bf16[256,256]{1,0:T(8,128)(2,1)}, u32[]{:S(2)}, u32[]{:S(2)}) collective-permute-start(bf16[256,256]{1,0:T(8,128)(2,1)} %get-tuple-element.17), channel_id=1, source_target_pairs={{8,0},{12,4},{16,8},{20,12},{24,16},{28,20},{9,1},{13,5},{17,9},{2... | collective-permute-start | bytes 393224 | tf_op jit(solution)/shard_map/ppermute | solution.py:28
  27.5 1.4 %copy-done.1 = bf16[3,256,1024]{2,1,0:T(8,128)(2,1)S(1)} copy-done((bf16[3,256,1024]{2,1,0:T(8,128)(2,1)S(1)}, bf16[3,256,1024]{2,1,0:T(8,128)(2,1)}, u32[]{:S(2)}) %copy-start.1) | copy-done | bytes 1572888
  28.9 0.9 %copy-done.7 = bf16[512,256]{1,0:T(8,128)(2,1)S(1)} copy-done((bf16[512,256]{1,0:T(8,128)(2,1)S(1)}, bf16[512,256]{1,0:T(8,128)(2,1)}, u32[]{:S(2)}) %copy-start.7) | copy-done | bytes 262168
  29.9 1.6 %own_terms.1 = (bf16[4,256,128]{2,1,0:T(8,128)(2,1)}, f32[256,256]{1,0:T(8,128)S(1)}) custom-call(bf16[5,256,1024]{2,1,0:T(8,128)(2,1)S(1)} %get-tuple-element.10.ds_ref, bf16[3,256,1024]{2,1,0:T(8,128)(2,1)S(1)} %copy-done.1, bf16[4,256,128]{2,1,0:T(8,128)(2,1)S(1)} %copy-done.3, bf16[4,256,128]{2,1,0:T(8,128)(2,1)S(1)} %copy-done.5, ...), custom_call_target="tpu_custom_call" | custom-call | flops 469762048 | bytes 1048576 | tf_op jit(solution)/shard_map/own_terms/pallas_call | solution.py:178
  31.5 1.3 %collective-permute-done.5 = bf16[256,256]{1,0:T(8,128)(2,1)} collective-permute-done((bf16[256,256]{1,0:T(8,128)(2,1)}, bf16[256,256]{1,0:T(8,128)(2,1)}, u32[]{:S(2)}, u32[]{:S(2)}) %collective-permute-start.5) | collective-permute-done | bytes 131104 | tf_op jit(solution)/shard_map/ppermute | solution.py:28
  32.8 1.2 %collective-permute-done.4 = bf16[256,256]{1,0:T(8,128)(2,1)} collective-permute-done((bf16[256,256]{1,0:T(8,128)(2,1)}, bf16[256,256]{1,0:T(8,128)(2,1)}, u32[]{:S(2)}, u32[]{:S(2)}) %collective-permute-start.4) | collective-permute-done | bytes 131104 | tf_op jit(solution)/shard_map/ppermute | solution.py:28
  33.9 0.0 copy-done.10
  33.9 1.0 %fusion.2 = f32[256,256]{1,0:T(8,128)S(1)} fusion(f32[256,256]{1,0:T(8,128)S(1)} %get-tuple-element.13, bf16[256,256]{1,0:T(8,128)(2,1)} %collective-permute-done.5, bf16[256,256]{1,0:T(8,128)(2,1)} %collective-permute-done.4, pred[]{:T(512)S(6)} %eq.10, bf16[512,256]{1,0:T(8,128)(2,1)S(1)} %copy-done.10), kind=kLoop, calls=%fused_computation.5 | loop fusion | flops 458752 | bytes 917505 | tf_op jit(solution)/shard_map/add | solution.py:191
  35.0 1.6 %collective-permute-start.6 = (bf16[2,64,256]{2,1,0:T(8,128)(2,1)S(1)}, bf16[2,64,256]{2,1,0:T(8,128)(2,1)S(1)}, u32[]{:S(2)}, u32[]{:S(2)}) collective-permute-start(bf16[2,64,256]{2,1,0:T(8,128)(2,1)S(1)} %fusion.8), channel_id=1, source_target_pairs={{0,1},{1,0},{2,3},{3,2},{4,5},{5,4},{6,7},{7,6},{8,9},{9,8},{10,11... | collective-permute-start | bytes 196616 | tf_op jit(solution)/shard_map/ppermute | solution.py:32
  36.7 2.7 %collective-permute-done.6 = bf16[2,64,256]{2,1,0:T(8,128)(2,1)S(1)} collective-permute-done((bf16[2,64,256]{2,1,0:T(8,128)(2,1)S(1)}, bf16[2,64,256]{2,1,0:T(8,128)(2,1)S(1)}, u32[]{:S(2)}, u32[]{:S(2)}) %collective-permute-start.6) | collective-permute-done | bytes 65568 | tf_op jit(solution)/shard_map/ppermute | solution.py:32
  39.4 2.6 %collective-permute-start.7 = (bf16[64,256]{1,0:T(8,128)(2,1)S(1)}, bf16[64,256]{1,0:T(8,128)(2,1)S(1)}, u32[]{:S(2)}, u32[]{:S(2)}) collective-permute-start(bf16[64,256]{1,0:T(8,128)(2,1)S(1)} %dynamic-slice_bitcast_fusion.2), channel_id=1, source_target_pairs={{0,2},{1,3},{2,0},{3,1},{4,6},{5,7},{6,4},{7,5},{8,10},{9,11},{10,... | collective-permute-start | bytes 98312 | tf_op jit(solution)/shard_map/ppermute | solution.py:32
  42.0 2.2 %collective-permute-done.7 = bf16[64,256]{1,0:T(8,128)(2,1)S(1)} collective-permute-done((bf16[64,256]{1,0:T(8,128)(2,1)S(1)}, bf16[64,256]{1,0:T(8,128)(2,1)S(1)}, u32[]{:S(2)}, u32[]{:S(2)}) %collective-permute-start.7) | collective-permute-done | bytes 32800 | tf_op jit(solution)/shard_map/ppermute | solution.py:32
  44.3 0.6 %pad_maximum_fusion.2 = (bf16[2,64,128]{2,1,0:T(8,128)(2,1)}, bf16[2,64,128]{2,1,0:T(8,128)(2,1)}) fusion(bf16[1,64,256]{2,1,0:T(8,128)(2,1)S(1)} %get-tuple-element.21, bf16[1,64,256]{2,1,0:T(8,128)(2,1)S(1)} %get-tuple-element.22), kind=kLoop, calls=%fused_computation.23 | loop fusion | flops 131072 | bytes 131072 | tf_op jit(solution)/shard_map/stack | solution.py:207
  (20 shorter events, 0.1 us)
Async XLA Ops:
  0.6 22.1 %copy-start.3 = (bf16[4,256,128]{2,1,0:T(8,128)(2,1)S(1)}, bf16[4,256,128]{2,1,0:T(8,128)(2,1)}, u32[]{:S(2)}) copy-start(bf16[4,256,128]{2,1,0:T(8,128)(2,1)} %q_ref.5) | copy-start | bytes 786436
  1.6 8.3 %collective-permute-start = (bf16[256,256]{1,0:T(8,128)(2,1)S(1)}, bf16[256,256]{1,0:T(8,128)(2,1)S(1)}, u32[]{:S(2)}, u32[]{:S(2)}) collective-permute-start(bf16[256,256]{1,0:T(8,128)(2,1)S(1)} %pad_maximum_fusion.1.own_ref), channel_id=1, source_target_pairs={{0,8},{4,12},{8,16},{12,20},{16,24},{20,28},{1,9},{5,13},{9,17},{1... | collective-permute-start | bytes 393224 | tf_op jit(solution)/shard_map/ppermute | solution.py:28
  6.5 6.5 %collective-permute-start.1 = (bf16[256,256]{1,0:T(8,128)(2,1)S(1)}, bf16[256,256]{1,0:T(8,128)(2,1)S(1)}, u32[]{:S(2)}, u32[]{:S(2)}) collective-permute-start(bf16[256,256]{1,0:T(8,128)(2,1)S(1)} %pad_maximum_fusion.1.own_ref), channel_id=1, source_target_pairs={{0,16},{4,20},{8,24},{12,28},{1,17},{5,21},{9,25},{13,29},{2,18},{... | collective-permute-start | bytes 393224 | tf_op jit(solution)/shard_map/ppermute | solution.py:28
  13.0 1.6 %collective-permute-start.2 = (bf16[512,256]{1,0:T(8,128)(2,1)S(1)}, bf16[512,256]{1,0:T(8,128)(2,1)S(1)}, u32[]{:S(2)}, u32[]{:S(2)}) collective-permute-start(bf16[512,256]{1,0:T(8,128)(2,1)S(1)} %pad_maximum_fusion), channel_id=1, source_target_pairs={{0,4},{4,0},{8,12},{12,8},{16,20},{20,16},{24,28},{28,24},{1,5},{5... | collective-permute-start | bytes 786440 | tf_op jit(solution)/shard_map/ppermute | solution.py:32
  14.6 8.1 %copy-start.6 = (bf16[512,256]{1,0:T(8,128)(2,1)}, bf16[512,256]{1,0:T(8,128)(2,1)S(1)}, u32[]{:S(2)}) copy-start(bf16[512,256]{1,0:T(8,128)(2,1)S(1)} %collective-permute-done.2.odd_ref) | copy-start | bytes 786436
  14.6 1.0 %copy-start.2 = (bf16[4,256,128]{2,1,0:T(8,128)(2,1)S(1)}, bf16[4,256,128]{2,1,0:T(8,128)(2,1)}, u32[]{:S(2)}) copy-start(bf16[4,256,128]{2,1,0:T(8,128)(2,1)} %q_ref.5) | copy-start | bytes 786436
  15.7 0.9 %copy-start.4 = (bf16[4,256,128]{2,1,0:T(8,128)(2,1)S(1)}, bf16[4,256,128]{2,1,0:T(8,128)(2,1)}, u32[]{:S(2)}) copy-start(bf16[4,256,128]{2,1,0:T(8,128)(2,1)} %g_ref.5) | copy-start | bytes 786436
  16.6 0.7 %copy-start.8 = (s32[4]{0:T(128)S(1)}, s32[4]{0:T(128)}, u32[]{:S(2)}) copy-start(s32[4]{0:T(128)} %lengths_ref.1) | copy-start | bytes 52
  22.5 2.4 %copy-start = (bf16[3,256,1024]{2,1,0:T(8,128)(2,1)}, bf16[3,256,1024]{2,1,0:T(8,128)(2,1)S(1)}, u32[]{:S(2)}) copy-start(bf16[3,256,1024]{2,1,0:T(8,128)(2,1)S(1)} %get-tuple-element.11.p_ref) | copy-start | bytes 4718596
  22.5 1.6 %collective-permute-start.3 = (bf16[512,256]{1,0:T(8,128)(2,1)S(1)}, bf16[512,256]{1,0:T(8,128)(2,1)S(1)}, u32[]{:S(2)}, u32[]{:S(2)}) collective-permute-start(bf16[512,256]{1,0:T(8,128)(2,1)S(1)} %get-tuple-element.14), channel_id=1, source_target_pairs={{0,4},{4,0},{8,12},{12,8},{16,20},{20,16},{24,28},{28,24},{1,5},{5... | collective-permute-start | bytes 786440 | tf_op jit(solution)/shard_map/ppermute | solution.py:32
  22.7 4.8 %copy-start.5 = (bf16[4,256,128]{2,1,0:T(8,128)(2,1)S(1)}, bf16[4,256,128]{2,1,0:T(8,128)(2,1)}, u32[]{:S(2)}) copy-start(bf16[4,256,128]{2,1,0:T(8,128)(2,1)} %g_ref.5) | copy-start | bytes 786436
  24.1 0.8 %copy-start.9 = (bf16[512,256]{1,0:T(8,128)(2,1)}, bf16[512,256]{1,0:T(8,128)(2,1)S(1)}, u32[]{:S(2)}) copy-start(bf16[512,256]{1,0:T(8,128)(2,1)S(1)} %collective-permute-done.3) | copy-start | bytes 786436
  24.9 7.9 %collective-permute-start.5 = (bf16[256,256]{1,0:T(8,128)(2,1)}, bf16[256,256]{1,0:T(8,128)(2,1)}, u32[]{:S(2)}, u32[]{:S(2)}) collective-permute-start(bf16[256,256]{1,0:T(8,128)(2,1)} %get-tuple-element.18), channel_id=1, source_target_pairs={{16,0},{20,4},{24,8},{28,12},{17,1},{21,5},{25,9},{29,13},{18,2},{... | collective-permute-start | bytes 393224 | tf_op jit(solution)/shard_map/ppermute | solution.py:28
  26.2 7.7 %collective-permute-start.4 = (bf16[256,256]{1,0:T(8,128)(2,1)}, bf16[256,256]{1,0:T(8,128)(2,1)}, u32[]{:S(2)}, u32[]{:S(2)}) collective-permute-start(bf16[256,256]{1,0:T(8,128)(2,1)} %get-tuple-element.17), channel_id=1, source_target_pairs={{8,0},{12,4},{16,8},{20,12},{24,16},{28,20},{9,1},{13,5},{17,9},{2... | collective-permute-start | bytes 393224 | tf_op jit(solution)/shard_map/ppermute | solution.py:28
  27.5 1.4 %copy-start.1 = (bf16[3,256,1024]{2,1,0:T(8,128)(2,1)S(1)}, bf16[3,256,1024]{2,1,0:T(8,128)(2,1)}, u32[]{:S(2)}) copy-start(bf16[3,256,1024]{2,1,0:T(8,128)(2,1)} %copy-done) | copy-start | bytes 4718596
  28.9 0.9 %copy-start.7 = (bf16[512,256]{1,0:T(8,128)(2,1)S(1)}, bf16[512,256]{1,0:T(8,128)(2,1)}, u32[]{:S(2)}) copy-start(bf16[512,256]{1,0:T(8,128)(2,1)} %copy-done.6) | copy-start | bytes 786436
  29.9 4.1 %copy-start.10 = (bf16[512,256]{1,0:T(8,128)(2,1)S(1)}, bf16[512,256]{1,0:T(8,128)(2,1)}, u32[]{:S(2)}) copy-start(bf16[512,256]{1,0:T(8,128)(2,1)} %copy-done.9) | copy-start | bytes 786436
  35.0 4.3 %collective-permute-start.6 = (bf16[2,64,256]{2,1,0:T(8,128)(2,1)S(1)}, bf16[2,64,256]{2,1,0:T(8,128)(2,1)S(1)}, u32[]{:S(2)}, u32[]{:S(2)}) collective-permute-start(bf16[2,64,256]{2,1,0:T(8,128)(2,1)S(1)} %fusion.8), channel_id=1, source_target_pairs={{0,1},{1,0},{2,3},{3,2},{4,5},{5,4},{6,7},{7,6},{8,9},{9,8},{10,11... | collective-permute-start | bytes 196616 | tf_op jit(solution)/shard_map/ppermute | solution.py:32
  39.4 4.9 %collective-permute-start.7 = (bf16[64,256]{1,0:T(8,128)(2,1)S(1)}, bf16[64,256]{1,0:T(8,128)(2,1)S(1)}, u32[]{:S(2)}, u32[]{:S(2)}) collective-permute-start(bf16[64,256]{1,0:T(8,128)(2,1)S(1)} %dynamic-slice_bitcast_fusion.2), channel_id=1, source_target_pairs={{0,2},{1,3},{2,0},{3,1},{4,6},{5,7},{6,4},{7,5},{8,10},{9,11},{10,... | collective-permute-start | bytes 98312 | tf_op jit(solution)/shard_map/ppermute | solution.py:32

commit v3 on v1

v3 whole, which is shorter than its diff:
```python
import functools
import math

import jax
import jax.numpy as jnp
from jax import lax
from jax.experimental import pallas as pl
from jax.experimental.pallas import tpu as pltpu
from jax.sharding import PartitionSpec as P

GROUP = 8
REACH = 4
MASKED = -1e30
NT = (((1,), (1,)), ((), ()))
NN = (((1,), (0,)), ((), ()))
VMEM = pl.BlockSpec(memory_space=pltpu.VMEM)
SMEM = pl.BlockSpec(memory_space=pltpu.SMEM)
bf16, f32, i32 = jnp.bfloat16, jnp.float32, jnp.int32


def dot(a, b, dims):
    return lax.dot_general(a, b, dims, preferred_element_type=f32)


def shape(dims, dtype):
    return jax.ShapeDtypeStruct(dims, dtype)


def call(body, name, in_specs, outs, flops, scratch=()):
    return pl.pallas_call(
        body,
        out_shape=outs,
        in_specs=in_specs,
        out_specs=(VMEM,) * len(outs),
        scratch_shapes=scratch,
        compiler_params=pltpu.CompilerParams(vmem_limit_bytes=20 * 2**20),
        cost_estimate=pl.CostEstimate(
            flops=flops // 100, bytes_accessed=2**10, transcendentals=0),
        name=name,
    )


def shifted(block, distance):
    count = lax.axis_size("ctx")
    route = [(i - distance, i) for i in range(count) if 0 <= i - distance < count]
    return lax.ppermute(block, "ctx", route)


def exchanged(block, axis, mask):
    return lax.ppermute(block, axis, [(i, i ^ mask) for i in range(lax.axis_size(axis))])


def part(pairs, offsets, doc_start, q_ref, g_ref, e_refs, dp_refs, s_ref):
    heads, tokens, width = q_ref.shape
    here = lax.axis_index("ctx")
    factor = width ** -0.5 * math.log2(math.e)
    key_iota = lax.broadcasted_iota(i32, (tokens, 1), 0)
    row_pos = here * tokens + lax.broadcasted_iota(i32, (1, tokens), 1)
    stats = []
    for h in range(heads):
        lanes = slice(h * tokens, (h + 1) * tokens)
        top = jnp.full((1, tokens), MASKED, f32)
        for at, (pair, back) in enumerate(zip(pairs, offsets)):
            s = dot(pair[:, :width], q_ref[h], NT)
            key_pos = (here - back) * tokens + key_iota
            allowed = key_pos >= doc_start
            if isinstance(back, int) and back == 0:
                allowed = allowed & (key_pos <= row_pos)
            s = jnp.where(allowed, s, MASKED)
            s_ref[at] = s
            top = jnp.maximum(top, jnp.max(s, axis=0, keepdims=True))
        total = jnp.zeros((1, tokens), f32)
        weighted = jnp.zeros((1, tokens), f32)
        for at, pair in enumerate(pairs):
            e = jnp.exp2((s_ref[at] - top) * factor)
            dp = dot(pair[:, width:], g_ref[h], NT)
            e_refs[at][:, lanes] = e
            dp_refs[at][:, lanes] = dp
            total = total + jnp.sum(e, axis=0, keepdims=True)
            weighted = weighted + jnp.sum(e * dp, axis=0, keepdims=True)
        stats.append((top, total, weighted))
    return stats


def write_stats(stats, stats_ref):
    tokens = stats[0][0].shape[1]
    for h, values in enumerate(stats):
        for row, value in enumerate(values):
            stats_ref[row:row + 1, h * tokens:(h + 1) * tokens] = value


def own_part_body(lengths_ref, q_in, g_in, own_ref,
                  q_ref, g_ref, start_ref, e_ref, dp_ref, stats_ref, s_ref):
    tokens = q_in.shape[1]
    q_ref[...] = q_in[...]
    g_ref[...] = g_in[...]
    row_pos = lax.axis_index("ctx") * tokens + lax.broadcasted_iota(i32, (1, tokens), 1)
    doc_start = jnp.zeros((1, tokens), i32)
    end = jnp.int32(0)
    for d in range(lengths_ref.shape[0]):
        end = end + lengths_ref[d]
        doc_start = jnp.where(row_pos >= end, end, doc_start)
    start_ref[...] = doc_start
    stats = part([own_ref], [0], doc_start, q_in, g_in, [e_ref], [dp_ref], s_ref)
    write_stats(stats, stats_ref)


def block_part_body(back, start_ref, q_ref, g_ref, pair_ref, e_ref, dp_ref, stats_ref, s_ref):
    stats = part([pair_ref], [back], start_ref[...], q_ref, g_ref, [e_ref], [dp_ref], s_ref)
    write_stats(stats, stats_ref)


def odd_terms_body(start_ref, q_ref, g_ref, odd_ref, stats_own, stats_two, stats_four,
                   terms_ref, coef_ref, ds_one, ds_three, e_ref, dp_ref, s_ref, p_ref):
    heads, tokens, width = q_ref.shape
    factor = width ** -0.5 * math.log2(math.e)
    pairs = [odd_ref.at[:tokens], odd_ref.at[tokens:]]
    slopes = [ds_one, ds_three]
    stats = part(pairs, [1, 3], start_ref[...], q_ref, g_ref,
                 [e_ref.at[0], e_ref.at[1]], [dp_ref.at[0], dp_ref.at[1]], s_ref)
    for h, odd in enumerate(stats):
        lanes = slice(h * tokens, (h + 1) * tokens)
        parts = [[ref[row:row + 1, lanes] for row in range(3)]
                 for ref in (stats_own, stats_two, stats_four)] + [odd]
        top = functools.reduce(jnp.maximum, [each[0] for each in parts])
        gains = [jnp.exp2((each[0] - top) * factor) for each in parts]
        total = sum(gain * each[1] for gain, each in zip(gains, parts))
        inverse = 1.0 / total
        gains = [gain * inverse for gain in gains]
        delta = sum(gain * each[2] for gain, each in zip(gains, parts))
        for row, value in enumerate([delta] + gains[:3]):
            coef_ref[row:row + 1, lanes] = value
        for at, ds_ref in enumerate(slopes):
            p = e_ref[at, :, lanes] * gains[3]
            p_ref[at, :, lanes] = p.astype(bf16)
            ds_ref[:, lanes] = (p * (dp_ref[at, :, lanes] - delta)).astype(bf16)
    q_all = q_ref[...].reshape(heads * tokens, width)
    g_all = g_ref[...].reshape(heads * tokens, width)
    for at, ds_ref in enumerate(slopes):
        rows = slice(at * tokens, (at + 1) * tokens)
        terms_ref[rows, :width] = (dot(ds_ref[...], q_all, NN) * width ** -0.5).astype(bf16)
        terms_ref[rows, width:] = dot(p_ref[at], g_all, NN).astype(bf16)


def block_terms(e_ref, dp_ref, coef_ref, row, q_ref, g_ref, terms_ref, ds_ref, p_ref):
    heads, tokens, width = q_ref.shape
    for h in range(heads):
        lanes = slice(h * tokens, (h + 1) * tokens)
        p = e_ref[:, lanes] * coef_ref[row:row + 1, lanes]
        p_ref[:, lanes] = p.astype(bf16)
        ds_ref[:, lanes] = (p * (dp_ref[:, lanes] - coef_ref[:1, lanes])).astype(bf16)
    q_all = q_ref[...].reshape(heads * tokens, width)
    g_all = g_ref[...].reshape(heads * tokens, width)
    terms_ref[:, :width] = dot(ds_ref[...], q_all, NN) * width ** -0.5
    terms_ref[:, width:] = dot(p_ref[...], g_all, NN)


def even_terms_body(e_two, dp_two, e_four, dp_four, coef_ref, q_ref, g_ref,
                    two_terms, four_terms, ds_two, ds_four, p_ref):
    block_terms(e_two, dp_two, coef_ref, 2, q_ref, g_ref, two_terms, ds_two, p_ref.at[0])
    block_terms(e_four, dp_four, coef_ref, 3, q_ref, g_ref, four_terms, ds_four, p_ref.at[1])


def join_body(two_terms, four_terms, odd_back, two_ref, four_ref):
    tokens = two_terms.shape[0]
    second = lax.rem(lax.axis_index("ctx"), 2)
    rows = pl.ds(pl.multiple_of((1 - second) * tokens, tokens), tokens)
    two_ref[...] = (two_terms[...] + odd_back[rows].astype(f32)).astype(bf16)
    far = odd_back[tokens:].astype(f32) * second.astype(f32)
    four_ref[...] = (four_terms[...] + far).astype(bf16)


def own_terms_body(e_own, dp_own, coef_ref, q_ref, g_ref, own_ref, two_ref, four_ref, odd_ref,
                   ds_one, ds_two, ds_three, ds_four, dq_ref, terms_ref, ds_own, p_ref):
    heads, tokens, width = q_ref.shape
    block_terms(e_own, dp_own, coef_ref, 1, q_ref, g_ref, terms_ref, ds_own, p_ref)
    window = [own_ref, odd_ref.at[:tokens], two_ref, odd_ref.at[tokens:], four_ref]
    turned = [pair[:, :width].T for pair in window]
    slopes = [ds_own, ds_one, ds_two, ds_three, ds_four]
    for h in range(heads):
        lanes = slice(h * tokens, (h + 1) * tokens)
        dqt = sum(dot(kt, ds[:, lanes], NN) for kt, ds in zip(turned, slopes))
        dq_ref[h] = (dqt.T * width ** -0.5).astype(dq_ref.dtype)


def sums_body(direct, uses, own_terms, odd_back, *refs):
    backs, outs = refs[:len(uses)], refs[len(uses):]
    tokens = own_terms.shape[0]
    ctx = lax.axis_index("ctx")
    head = lax.axis_index("head")
    count = lax.axis_size("head")
    rows_each = tokens // count

    def total(rows):
        value = own_terms[rows] + odd_back[rows].astype(f32) * (1 - lax.rem(ctx, 2)).astype(f32)
        for back, use in zip(backs, uses):
            value = value + jnp.where(use(ctx), back[rows].astype(f32), 0.0)
        return value

    if not direct:
        outs[0][...] = total(slice(0, tokens)).astype(bf16)
        return
    for mask in range(count):
        place = jnp.bitwise_xor(head, mask)
        value = total(pl.ds(pl.multiple_of(place * rows_each, rows_each), rows_each))
        outs[mask][...] = value.astype(outs[mask].dtype)


def last_body(share, *refs):
    *parts, dk_ref, dv_ref = refs
    width = dk_ref.shape[-1]
    group = lax.axis_index("head") // share
    for other in range(len(parts) // share):
        mine = parts[other * share:(other + 1) * share]
        value = sum(ref[...].astype(f32) for ref in mine).astype(bf16)
        place = jnp.bitwise_xor(group, other)
        dk_ref[place] = value[:, :width]
        dv_ref[place] = value[:, width:]


def per_device(queries, keys, values, d_out, doc_lengths):
    heads, tokens, width = queries.shape
    head_count = lax.axis_size("head")
    share = GROUP // heads
    groups = head_count // share
    rows = heads * tokens
    work = rows * tokens * width * 2
    pair = (tokens, 2 * width)
    stats = shape((3, rows), f32)
    wide = shape((tokens, rows), f32)
    half = shape((tokens, rows), bf16)

    def tile(count):
        return (pltpu.VMEM((count, tokens, tokens), f32),)

    group = lax.axis_index("head") // share
    own = jnp.concatenate(
        [lax.dynamic_index_in_dim(keys, group, 0, keepdims=False),
         lax.dynamic_index_in_dim(values, group, 0, keepdims=False)], axis=1)
    ctx = lax.axis_index("ctx")
    second_core = ctx % 2 == 1
    mutual = lax.axis_size("ctx") == 2 * REACH
    four = exchanged(own, "ctx", 4) if mutual else shifted(own, 4)
    if mutual:
        two = (exchanged(own, "ctx", 2), exchanged(own, "ctx", 6))
    else:
        two = (shifted(own, 2),)
    q, g, start, e_own, dp_own, stats_own = call(
        own_part_body, "own_part", [SMEM] + [VMEM] * 3,
        (shape(queries.shape, bf16), shape(d_out.shape, bf16), shape((1, tokens), i32),
         wide, wide, stats),
        2 * work, tile(1))(doc_lengths, queries, d_out, own)
    four, start = lax.optimization_barrier((four, start))
    e_four, dp_four, stats_four = call(
        functools.partial(block_part_body, 4), "four_part", [VMEM] * 4, (wide, wide, stats),
        2 * work, tile(1))(start, q, g, four)
    *two, stats_four = lax.optimization_barrier((*two, stats_four))
    two = jnp.where(ctx & 2 == 2, *two) if mutual else two[0]
    odd = exchanged(
        jnp.concatenate([jnp.where(second_core, two, own), jnp.where(second_core, four, two)]),
        "ctx", 1)
    e_two, dp_two, stats_two = call(
        functools.partial(block_part_body, 2), "two_part", [VMEM] * 4, (wide, wide, stats),
        2 * work, tile(1))(start, q, g, two)
    odd_terms, coef, ds_one, ds_three = call(
        odd_terms_body, "odd_terms", [VMEM] * 7,
        (shape((2 * tokens, 2 * width), bf16), shape((4, rows), f32), half, half),
        6 * work,
        (pltpu.VMEM((2, tokens, rows), f32),) * 2 + tile(2)
        + (pltpu.VMEM((2, tokens, rows), bf16),),
    )(start, q, g, odd, stats_own, stats_two, stats_four)
    odd_back = exchanged(odd_terms, "ctx", 1)
    two_terms, four_terms, ds_two, ds_four = call(
        even_terms_body, "even_terms", [VMEM] * 7,
        (shape(pair, f32), shape(pair, f32), half, half), 4 * work,
        (pltpu.VMEM((2, tokens, rows), bf16),),
    )(e_two, dp_two, e_four, dp_four, coef, q, g)
    two_sum, four_sum = call(
        join_body, "join", [VMEM] * 3, (shape(pair, bf16),) * 2, 0,
    )(two_terms, four_terms, odd_back)
    if mutual:
        backs = [exchanged(four_sum, "ctx", 4), exchanged(two_sum, "ctx", 2),
                 exchanged(two_sum, "ctx", 6)]
        uses = [lambda i: i < 4, lambda i: i & 2 == 0, lambda i: i & 6 == 2]
    else:
        backs = [shifted(four_sum, -4), shifted(two_sum, -2)]
        uses = [lambda i: True] * 2
    d_queries, own_terms = call(
        own_terms_body, "own_terms", [VMEM] * 13,
        (shape(queries.shape, bf16), shape(pair, f32)), 7 * work,
        (pltpu.VMEM((tokens, rows), bf16),) * 2,
    )(e_own, dp_own, coef, q, g, own, two, four, odd, ds_one, ds_two, ds_three, ds_four)

    direct = head_count == 2 * share and share == 2
    slice_dims = (tokens // head_count, 2 * width)
    outs = ((shape(slice_dims, f32),) + (shape(slice_dims, bf16),) * (head_count - 1)
            if direct else (shape(pair, bf16),))
    sums = call(
        functools.partial(sums_body, direct, uses), "sums", [VMEM] * (2 + len(backs)), outs, 0,
    )(own_terms, odd_back, *backs)
    if direct:
        parts = [sums[0]] + [exchanged(sums[m], "head", m) for m in range(1, head_count)]
        result_dims = (groups, tokens // head_count, width)
        d_keys, d_values = call(
            functools.partial(last_body, share), "last", [VMEM] * head_count,
            (shape(result_dims, bf16),) * 2, 0)(*parts)
        return d_queries, d_keys, d_values
    slices = lax.all_to_all(sums[0].reshape(head_count, *slice_dims), "head", 0, 0)
    result = jnp.sum(slices.reshape(groups, share, *slice_dims).astype(f32), axis=1).astype(bf16)
    return d_queries, result[..., :width], result[..., width:]


def solution(mesh):
    placed = (
        P("head", "ctx", None),
        P(None, "ctx", None),
        P(None, "ctx", None),
        P("head", "ctx", None),
        P(),
    )
    return jax.shard_map(
        per_device,
        mesh=mesh,
        in_specs=placed,
        out_specs=(
            P("head", "ctx", None),
            P(None, ("ctx", "head"), None),
            P(None, ("ctx", "head"), None),
        ),
        check_vma=False,
    )
```

time: 100 us -> 38.7 us (0.39)
  waiting for transfers between devices: 63.9 us -> 15.3 us
  between operations: 14.1 us -> 0.74 us
  starting transfers between devices: 0.08 us -> 12.9 us
  blocking collectives: 10.7 us -> 0 us
  local copies, waits for them, and re-layouts: 3.45 us -> 1.6 us
    reduce_scatter x1 -> x0, waiting for transfers between devices: 36.2 us -> none  [per_device(): sums = lax.psum_scatter(terms, 'ctx', scatter_dimension=0)]
    all_gather x1 -> x0, waiting for transfers between devices: 27.8 us -> none  [per_device(): gathered = lax.all_gather(own, 'ctx')]
    ppermute x0 -> x11, waiting for transfers between devices: none -> 15.3 us  [exchanged(): lax.ppermute(block, axis, [(i, i ^ mask) for i in range(lax.axis_size(axi...]
    ppermute x0 -> x11, starting transfers between devices: none -> 12.9 us  [exchanged(): lax.ppermute(block, axis, [(i, i ^ mask) for i in range(lax.axis_size(axi...]
    all_to_all x1 -> x0, blocking collectives: 10.7 us -> none  [per_device(): lax.all_to_all(sums.reshape(head_count, tokens // head_count, 2 * width),...]
    unnamed x8 -> x6, local copies, waits for them, and re-layouts: 1.88 us -> 0.66 us
    pallas_call x1 -> x9, Pallas kernels: 7.09 us -> 7.89 us  [the longest x1 2.35 us: per_device(): call(odd_terms_body, 'odd_terms', [VMEM] * 7, (shape((2 * tokens, 2 * wid...]
  transfers between devices with their start and end apart: 2 -> 11, of which waited for: 2 -> 10; matrix products, arithmetic and copies ran while one was open for 0% -> 0% of each run, Pallas kernels for 0% -> 12%
where the time goes in v3:
time: 38.7 us; the launch traced here: 38.5 us
  waiting for transfers between devices  15.3 us (40%)
  starting transfers between devices  12.9 us (33%)
  Pallas kernels  7.89 us (20%)
  local copies, waits for them, and re-layouts  1.6 us (4%)
  between operations  0.74 us (2%)
    ppermute x11, waiting for transfers between devices, exchanged(): lax.ppermute(block, axis, [(i, i ^ mask) for i in range(lax.axis_size(axi...  15.3 us
    ppermute x11, starting transfers between devices, exchanged(): lax.ppermute(block, axis, [(i, i ^ mask) for i in range(lax.axis_size(axi...  12.9 us
    pallas_call x1, Pallas kernels, per_device(): call(odd_terms_body, 'odd_terms', [VMEM] * 7, (shape((2 * tokens, 2 * wid...  2.35 us
    pallas_call x1, Pallas kernels, per_device(): call(own_terms_body, 'own_terms', [VMEM] * 13, (shape(queries.shape, bf16...  1.61 us
    pallas_call x1, Pallas kernels, per_device(): call(own_part_body, 'own_part', [SMEM] + [VMEM] * 3, (shape(queries.shape...  1.15 us
    squeeze x1, local copies, waits for them, and re-layouts, per_device(): lax.dynamic_index_in_dim(values, group, 0, keepdims=False)  0.94 us
    pallas_call x1, Pallas kernels, per_device(): call(even_terms_body, 'even_terms', [VMEM] * 7, (shape(pair, f32), shape(...  0.81 us
  transfers between devices with their start and end apart: 11, of which 10 were waited for; matrix products, arithmetic and copies ran while one was open for 0% of the time, Pallas kernels for 12%

profile of v3, /device:TPU:0, one launch (start us, length us, event | category | flops | bytes accessed | tf_op | source)
XLA Modules:
  0.0 38.5 jit_solution(6254674994005995318)
XLA Ops:
  0.7 0.9 %dynamic-slice_bitcast_fusion = (bf16[256,128]{1,0:T(8,128)(2,1)S(1)}, bf16[256,128]{1,0:T(8,128)(2,1)S(1)}) fusion(bf16[2,256,128]{2,1,0:T(8,128)(2,1)} %param.7, s32[]{:T(128)S(6)} %select_n.35, bf16[2,256,128]{2,1,0:T(8,128)(2,1)} %param.6), kind=kLoop, calls=%fused_computation.5 | loop fusion | bytes 262148 | tf_op jit(solution)/shard_map/jit(dynamic_index_in_dim)/squeeze | solution.py:239
  1.6 3.0 %collective-permute-start = (bf16[256,256]{1,0:T(8,128)(2,1)S(1)}, bf16[256,256]{1,0:T(8,128)(2,1)S(1)}, u32[]{:S(2)}, u32[]{:S(2)}) collective-permute-start(bf16[256,256]{1,0:T(8,128)(2,1)S(1)} %pad_maximum_fusion.1.own_ref), channel_id=1, source_target_pairs={{0,16},{4,20},{8,24},{12,28},{16,0},{20,4},{24,8},{28,12},{1,17},{... | collective-permute-start | bytes 393224 | tf_op jit(solution)/shard_map/ppermute | solution.py:50
  4.7 1.4 %collective-permute-start.2 = (bf16[256,256]{1,0:T(8,128)(2,1)S(1)}, bf16[256,256]{1,0:T(8,128)(2,1)S(1)}, u32[]{:S(2)}, u32[]{:S(2)}) collective-permute-start(bf16[256,256]{1,0:T(8,128)(2,1)S(1)} %pad_maximum_fusion.1.own_ref), channel_id=1, source_target_pairs={{0,24},{4,28},{8,16},{12,20},{16,8},{20,12},{24,0},{28,4},{1,25},{... | collective-permute-start | bytes 393224 | tf_op jit(solution)/shard_map/ppermute | solution.py:50
  6.1 0.1 collective-permute-start.1
  6.2 0.6 %copy-done.2 = s32[4]{0:T(128)S(1)} copy-done((s32[4]{0:T(128)S(1)}, s32[4]{0:T(128)}, u32[]{:S(2)}) %copy-start.2) | copy-done | bytes 40
  6.9 1.2 %own_part.1 = (bf16[4,256,128]{2,1,0:T(8,128)(2,1)S(1)}, bf16[4,256,128]{2,1,0:T(8,128)(2,1)S(1)}, s32[1,256]{1,0:T(1,128)S(1)}, f32[256,1024]{1,0:T(8,128)S(1)}...) custom-call(s32[4]{0:T(128)S(1)} %copy-done.2, bf16[4,256,128]{2,1,0:T(8,128)(2,1)S(1)} %copy-done, ...), custom_call_target="tpu_custom_call" | custom-call | flops 1342177 | bytes 1024 | tf_op jit(solution)/shard_map/own_part/pallas_call | solution.py:248
  8.0 2.2 %collective-permute-done.pair_ref.four_ref = bf16[256,256]{1,0:T(8,128)(2,1)S(1)} collective-permute-done((bf16[256,256]{1,0:T(8,128)(2,1)S(1)}, bf16[256,256]{1,0:T(8,128)(2,1)S(1)}, u32[]{:S(2)}, u32[]{:S(2)}) %collective-permute-start) | collective-permute-done | bytes 131104 | tf_op jit(solution)/shard_map/ppermute | solution.py:50
  10.2 0.6 %four_part.1 = (f32[256,1024]{1,0:T(8,128)S(1)}, f32[256,1024]{1,0:T(8,128)S(1)}, f32[3,1024]{1,0:T(4,128)S(1)}) custom-call(s32[1,256]{1,0:T(1,128)S(1)} %get-tuple-element.41.start_ref, bf16[4,256,128]{2,1,0:T(8,128)(2,1)S(1)} %get-tuple-element.42.q_ref, bf16[4,256,128]{2,1,0:T(8,128)(2,1)S(1)} %get-tuple-element.43.g_ref, ...), custom_call_target="tpu_custom_call" | custom-call | flops 1342177 | bytes 1024 | tf_op jit(solution)/shard_map/four_part/pallas_call | solution.py:254
  10.8 1.2 %collective-permute-done.2 = bf16[256,256]{1,0:T(8,128)(2,1)S(1)} collective-permute-done((bf16[256,256]{1,0:T(8,128)(2,1)S(1)}, bf16[256,256]{1,0:T(8,128)(2,1)S(1)}, u32[]{:S(2)}, u32[]{:S(2)}) %collective-permute-start.2) | collective-permute-done | bytes 131104 | tf_op jit(solution)/shard_map/ppermute | solution.py:50
  12.0 0.3 collective-permute-done.1
  12.4 0.1 collective-permute-start.3
  12.5 0.6 %two_part.1 = (f32[256,1024]{1,0:T(8,128)S(1)}, f32[256,1024]{1,0:T(8,128)S(1)}, f32[3,1024]{1,0:T(4,128)S(1)}) custom-call(s32[1,256]{1,0:T(1,128)S(1)} %get-tuple-element.41.start_ref, bf16[4,256,128]{2,1,0:T(8,128)(2,1)S(1)} %get-tuple-element.42.q_ref, bf16[4,256,128]{2,1,0:T(8,128)(2,1)S(1)} %get-tuple-element.43.g_ref, ...), custom_call_target="tpu_custom_call" | custom-call | flops 1342177 | bytes 1024 | tf_op jit(solution)/shard_map/two_part/pallas_call | solution.py:262
  13.1 0.9 %collective-permute-done.3.odd_ref = bf16[512,256]{1,0:T(8,128)(2,1)S(1)} collective-permute-done((bf16[512,256]{1,0:T(8,128)(2,1)S(1)}, bf16[512,256]{1,0:T(8,128)(2,1)S(1)}, u32[]{:S(2)}, u32[]{:S(2)}) %collective-permute-start.3) | collective-permute-done | bytes 262176 | tf_op jit(solution)/shard_map/ppermute | solution.py:50
  14.0 2.4 %odd_terms.1 = (bf16[512,256]{1,0:T(8,128)(2,1)S(1)}, f32[4,1024]{1,0:T(4,128)S(1)}, bf16[256,1024]{1,0:T(8,128)(2,1)S(1)}, bf16[256,1024]{1,0:T(8,128)(2,1)S(1)}) custom-call(s32[1,256]{1,0:T(1,128)S(1)} %get-tuple-element.41.start_ref, bf16[4,256,128]{2,1,0:T(8,128)(2,1)S(1)} %get-tuple-element.42.q_ref, bf16[4,256,128]{2,1,0:T(8,128)(2,1)S(1)} %get-tuple-element.43.g_ref, ...), custom_call_target="tpu_custom_call" | custom-call | flops 4026531 | bytes 1024 | tf_op jit(solution)/shard_map/odd_terms/pallas_call | solution.py:265
  16.4 0.2 collective-permute-start.4
  16.6 0.8 %even_terms.1 = (f32[256,256]{1,0:T(8,128)S(1)}, f32[256,256]{1,0:T(8,128)S(1)}, bf16[256,1024]{1,0:T(8,128)(2,1)S(1)}, bf16[256,1024]{1,0:T(8,128)(2,1)S(1)}) custom-call(f32[256,1024]{1,0:T(8,128)S(1)} %get-tuple-element.53.e_two, f32[256,1024]{1,0:T(8,128)S(1)} %get-tuple-element.54.dp_two, f32[256,1024]{1,0:T(8,128)S(1)} %get-tuple-element.55.e_four, ...), custom_call_target="tpu_custom_call" | custom-call | flops 2684354 | bytes 1024 | tf_op jit(solution)/shard_map/even_terms/pallas_call | solution.py:273
  17.4 0.6 %collective-permute-done.4.odd_back = bf16[512,256]{1,0:T(8,128)(2,1)S(1)} collective-permute-done((bf16[512,256]{1,0:T(8,128)(2,1)S(1)}, bf16[512,256]{1,0:T(8,128)(2,1)S(1)}, u32[]{:S(2)}, u32[]{:S(2)}) %collective-permute-start.4) | collective-permute-done | bytes 262176 | tf_op jit(solution)/shard_map/ppermute | solution.py:50
  18.0 0.1 join.1
  18.0 1.7 %collective-permute-start.5 = (bf16[256,256]{1,0:T(8,128)(2,1)S(1)}, bf16[256,256]{1,0:T(8,128)(2,1)S(1)}, u32[]{:S(2)}, u32[]{:S(2)}) collective-permute-start(bf16[256,256]{1,0:T(8,128)(2,1)S(1)} %get-tuple-element.65), channel_id=1, source_target_pairs={{0,16},{4,20},{8,24},{12,28},{16,0},{20,4},{24,8},{28,12},{1,17},{... | collective-permute-start | bytes 393224 | tf_op jit(solution)/shard_map/ppermute | solution.py:50
  19.8 1.4 %collective-permute-start.7 = (bf16[256,256]{1,0:T(8,128)(2,1)S(1)}, bf16[256,256]{1,0:T(8,128)(2,1)S(1)}, u32[]{:S(2)}, u32[]{:S(2)}) collective-permute-start(bf16[256,256]{1,0:T(8,128)(2,1)S(1)} %get-tuple-element.66), channel_id=1, source_target_pairs={{0,24},{4,28},{8,16},{12,20},{16,8},{20,12},{24,0},{28,4},{1,25},{... | collective-permute-start | bytes 393224 | tf_op jit(solution)/shard_map/ppermute | solution.py:50
  21.2 0.4 %collective-permute-start.6 = (bf16[256,256]{1,0:T(8,128)(2,1)S(1)}, bf16[256,256]{1,0:T(8,128)(2,1)S(1)}, u32[]{:S(2)}, u32[]{:S(2)}) collective-permute-start(bf16[256,256]{1,0:T(8,128)(2,1)S(1)} %get-tuple-element.66), channel_id=1, source_target_pairs={{0,8},{4,12},{8,0},{12,4},{16,24},{20,28},{24,16},{28,20},{1,9},{5... | collective-permute-start | bytes 393224 | tf_op jit(solution)/shard_map/ppermute | solution.py:50
  21.6 1.6 %own_terms.1 = (bf16[4,256,128]{2,1,0:T(8,128)(2,1)}, f32[256,256]{1,0:T(8,128)S(1)}) custom-call(f32[256,1024]{1,0:T(8,128)S(1)} %get-tuple-element.38.e_own, f32[256,1024]{1,0:T(8,128)S(1)} %get-tuple-element.39.dp_own, f32[4,1024]{1,0:T(4,128)S(1)} %get-tuple-element.51.coef_ref, bf16[4,256,128]{2,1,0:T(8,128)(2,1)S(1)} %get-tuple-element.42.q_ref, ...), custom_call_target="tpu_custom_call" | custom-call | flops 4697620 | bytes 1024 | tf_op jit(solution)/shard_map/own_terms/pallas_call | solution.py:288
  23.2 2.6 %collective-permute-done.5.refs_0_ = bf16[256,256]{1,0:T(8,128)(2,1)S(1)} collective-permute-done((bf16[256,256]{1,0:T(8,128)(2,1)S(1)}, bf16[256,256]{1,0:T(8,128)(2,1)S(1)}, u32[]{:S(2)}, u32[]{:S(2)}) %collective-permute-start.5) | collective-permute-done | bytes 131104 | tf_op jit(solution)/shard_map/ppermute | solution.py:50
  25.8 1.2 %collective-permute-done.7.refs_2_ = bf16[256,256]{1,0:T(8,128)(2,1)S(1)} collective-permute-done((bf16[256,256]{1,0:T(8,128)(2,1)S(1)}, bf16[256,256]{1,0:T(8,128)(2,1)S(1)}, u32[]{:S(2)}, u32[]{:S(2)}) %collective-permute-start.7) | collective-permute-done | bytes 131104 | tf_op jit(solution)/shard_map/ppermute | solution.py:50
  27.0 0.6 %collective-permute-done.6.refs_1_ = bf16[256,256]{1,0:T(8,128)(2,1)S(1)} collective-permute-done((bf16[256,256]{1,0:T(8,128)(2,1)S(1)}, bf16[256,256]{1,0:T(8,128)(2,1)S(1)}, u32[]{:S(2)}, u32[]{:S(2)}) %collective-permute-start.6) | collective-permute-done | bytes 131104 | tf_op jit(solution)/shard_map/ppermute | solution.py:50
  27.7 0.1 sums.1
  27.8 1.8 %collective-permute-start.8 = (bf16[64,256]{1,0:T(8,128)(2,1)S(1)}, bf16[64,256]{1,0:T(8,128)(2,1)S(1)}, u32[]{:S(2)}, u32[]{:S(2)}) collective-permute-start(bf16[64,256]{1,0:T(8,128)(2,1)S(1)} %get-tuple-element.68), channel_id=1, source_target_pairs={{0,1},{1,0},{2,3},{3,2},{4,5},{5,4},{6,7},{7,6},{8,9},{9,8},{10,11... | collective-permute-start | bytes 98312 | tf_op jit(solution)/shard_map/ppermute | solution.py:50
  29.6 2.6 %collective-permute-start.9 = (bf16[64,256]{1,0:T(8,128)(2,1)S(1)}, bf16[64,256]{1,0:T(8,128)(2,1)S(1)}, u32[]{:S(2)}, u32[]{:S(2)}) collective-permute-start(bf16[64,256]{1,0:T(8,128)(2,1)S(1)} %get-tuple-element.69), channel_id=1, source_target_pairs={{0,2},{1,3},{2,0},{3,1},{4,6},{5,7},{6,4},{7,5},{8,10},{9,11},{10,... | collective-permute-start | bytes 98312 | tf_op jit(solution)/shard_map/ppermute | solution.py:50
  32.2 0.1 collective-permute-start.10
  32.2 2.4 %collective-permute-done.9.refs_2_ = bf16[64,256]{1,0:T(8,128)(2,1)S(1)} collective-permute-done((bf16[64,256]{1,0:T(8,128)(2,1)S(1)}, bf16[64,256]{1,0:T(8,128)(2,1)S(1)}, u32[]{:S(2)}, u32[]{:S(2)}) %collective-permute-start.9) | collective-permute-done | bytes 32800 | tf_op jit(solution)/shard_map/ppermute | solution.py:50
  34.6 3.2 %collective-permute-done.10.refs_3_ = bf16[64,256]{1,0:T(8,128)(2,1)S(1)} collective-permute-done((bf16[64,256]{1,0:T(8,128)(2,1)S(1)}, bf16[64,256]{1,0:T(8,128)(2,1)S(1)}, u32[]{:S(2)}, u32[]{:S(2)}) %collective-permute-start.10) | collective-permute-done | bytes 32800 | tf_op jit(solution)/shard_map/ppermute | solution.py:50
  37.9 0.6 %last.1 = (bf16[2,64,128]{2,1,0:T(8,128)(2,1)}, bf16[2,64,128]{2,1,0:T(8,128)(2,1)}) custom-call(f32[64,256]{1,0:T(8,128)S(1)} %get-tuple-element.67.refs_0_, bf16[64,256]{1,0:T(8,128)(2,1)S(1)} %collective-permute-done.8.refs_1_, bf16[64,256]{1,0:T(8,128)(2,1)S(1)} %collective-permute-done.9.refs_2_, bf16[64,256]{1,0:T(8,128)(2,1)S(1)} %collective-permute-done.10.refs_3_), custom_call_target="tpu_custom_call" | custom-call | bytes 1024 | tf_op jit(solution)/shard_map/last/pallas_call | solution.py:304
  (10 shorter events, 0.1 us)
Async XLA Ops:
  0.6 5.6 %copy-start = (bf16[4,256,128]{2,1,0:T(8,128)(2,1)S(1)}, bf16[4,256,128]{2,1,0:T(8,128)(2,1)}, u32[]{:S(2)}) copy-start(bf16[4,256,128]{2,1,0:T(8,128)(2,1)} %q_in.1) | copy-start | bytes 786436
  0.7 5.6 %copy-start.1 = (bf16[4,256,128]{2,1,0:T(8,128)(2,1)S(1)}, bf16[4,256,128]{2,1,0:T(8,128)(2,1)}, u32[]{:S(2)}) copy-start(bf16[4,256,128]{2,1,0:T(8,128)(2,1)} %g_in.1) | copy-start | bytes 786436
  1.6 8.6 %collective-permute-start = (bf16[256,256]{1,0:T(8,128)(2,1)S(1)}, bf16[256,256]{1,0:T(8,128)(2,1)S(1)}, u32[]{:S(2)}, u32[]{:S(2)}) collective-permute-start(bf16[256,256]{1,0:T(8,128)(2,1)S(1)} %pad_maximum_fusion.1.own_ref), channel_id=1, source_target_pairs={{0,16},{4,20},{8,24},{12,28},{16,0},{20,4},{24,8},{28,12},{1,17},{... | collective-permute-start | bytes 393224 | tf_op jit(solution)/shard_map/ppermute | solution.py:50
  4.7 7.3 %collective-permute-start.2 = (bf16[256,256]{1,0:T(8,128)(2,1)S(1)}, bf16[256,256]{1,0:T(8,128)(2,1)S(1)}, u32[]{:S(2)}, u32[]{:S(2)}) collective-permute-start(bf16[256,256]{1,0:T(8,128)(2,1)S(1)} %pad_maximum_fusion.1.own_ref), channel_id=1, source_target_pairs={{0,24},{4,28},{8,16},{12,20},{16,8},{20,12},{24,0},{28,4},{1,25},{... | collective-permute-start | bytes 393224 | tf_op jit(solution)/shard_map/ppermute | solution.py:50
  6.1 6.2 %collective-permute-start.1 = (bf16[256,256]{1,0:T(8,128)(2,1)S(1)}, bf16[256,256]{1,0:T(8,128)(2,1)S(1)}, u32[]{:S(2)}, u32[]{:S(2)}) collective-permute-start(bf16[256,256]{1,0:T(8,128)(2,1)S(1)} %pad_maximum_fusion.1.own_ref), channel_id=1, source_target_pairs={{0,8},{4,12},{8,0},{12,4},{16,24},{20,28},{24,16},{28,20},{1,9},{5... | collective-permute-start | bytes 393224 | tf_op jit(solution)/shard_map/ppermute | solution.py:50
  6.2 0.7 %copy-start.2 = (s32[4]{0:T(128)S(1)}, s32[4]{0:T(128)}, u32[]{:S(2)}) copy-start(s32[4]{0:T(128)} %lengths_ref.1) | copy-start | bytes 52
  12.4 1.6 %collective-permute-start.3 = (bf16[512,256]{1,0:T(8,128)(2,1)S(1)}, bf16[512,256]{1,0:T(8,128)(2,1)S(1)}, u32[]{:S(2)}, u32[]{:S(2)}) collective-permute-start(bf16[512,256]{1,0:T(8,128)(2,1)S(1)} %pad_maximum_fusion), channel_id=1, source_target_pairs={{0,4},{4,0},{8,12},{12,8},{16,20},{20,16},{24,28},{28,24},{1,5},{5... | collective-permute-start | bytes 786440 | tf_op jit(solution)/shard_map/ppermute | solution.py:50
  16.4 1.6 %collective-permute-start.4 = (bf16[512,256]{1,0:T(8,128)(2,1)S(1)}, bf16[512,256]{1,0:T(8,128)(2,1)S(1)}, u32[]{:S(2)}, u32[]{:S(2)}) collective-permute-start(bf16[512,256]{1,0:T(8,128)(2,1)S(1)} %get-tuple-element.62), channel_id=1, source_target_pairs={{0,4},{4,0},{8,12},{12,8},{16,20},{20,16},{24,28},{28,24},{1,5},{5... | collective-permute-start | bytes 786440 | tf_op jit(solution)/shard_map/ppermute | solution.py:50
  18.0 7.8 %collective-permute-start.5 = (bf16[256,256]{1,0:T(8,128)(2,1)S(1)}, bf16[256,256]{1,0:T(8,128)(2,1)S(1)}, u32[]{:S(2)}, u32[]{:S(2)}) collective-permute-start(bf16[256,256]{1,0:T(8,128)(2,1)S(1)} %get-tuple-element.65), channel_id=1, source_target_pairs={{0,16},{4,20},{8,24},{12,28},{16,0},{20,4},{24,8},{28,12},{1,17},{... | collective-permute-start | bytes 393224 | tf_op jit(solution)/shard_map/ppermute | solution.py:50
  19.8 7.3 %collective-permute-start.7 = (bf16[256,256]{1,0:T(8,128)(2,1)S(1)}, bf16[256,256]{1,0:T(8,128)(2,1)S(1)}, u32[]{:S(2)}, u32[]{:S(2)}) collective-permute-start(bf16[256,256]{1,0:T(8,128)(2,1)S(1)} %get-tuple-element.66), channel_id=1, source_target_pairs={{0,24},{4,28},{8,16},{12,20},{16,8},{20,12},{24,0},{28,4},{1,25},{... | collective-permute-start | bytes 393224 | tf_op jit(solution)/shard_map/ppermute | solution.py:50
  21.2 6.5 %collective-permute-start.6 = (bf16[256,256]{1,0:T(8,128)(2,1)S(1)}, bf16[256,256]{1,0:T(8,128)(2,1)S(1)}, u32[]{:S(2)}, u32[]{:S(2)}) collective-permute-start(bf16[256,256]{1,0:T(8,128)(2,1)S(1)} %get-tuple-element.66), channel_id=1, source_target_pairs={{0,8},{4,12},{8,0},{12,4},{16,24},{20,28},{24,16},{28,20},{1,9},{5... | collective-permute-start | bytes 393224 | tf_op jit(solution)/shard_map/ppermute | solution.py:50
  27.8 4.5 %collective-permute-start.8 = (bf16[64,256]{1,0:T(8,128)(2,1)S(1)}, bf16[64,256]{1,0:T(8,128)(2,1)S(1)}, u32[]{:S(2)}, u32[]{:S(2)}) collective-permute-start(bf16[64,256]{1,0:T(8,128)(2,1)S(1)} %get-tuple-element.68), channel_id=1, source_target_pairs={{0,1},{1,0},{2,3},{3,2},{4,5},{5,4},{6,7},{7,6},{8,9},{9,8},{10,11... | collective-permute-start | bytes 98312 | tf_op jit(solution)/shard_map/ppermute | solution.py:50
  29.6 5.1 %collective-permute-start.9 = (bf16[64,256]{1,0:T(8,128)(2,1)S(1)}, bf16[64,256]{1,0:T(8,128)(2,1)S(1)}, u32[]{:S(2)}, u32[]{:S(2)}) collective-permute-start(bf16[64,256]{1,0:T(8,128)(2,1)S(1)} %get-tuple-element.69), channel_id=1, source_target_pairs={{0,2},{1,3},{2,0},{3,1},{4,6},{5,7},{6,4},{7,5},{8,10},{9,11},{10,... | collective-permute-start | bytes 98312 | tf_op jit(solution)/shard_map/ppermute | solution.py:50
  32.2 5.7 %collective-permute-start.10 = (bf16[64,256]{1,0:T(8,128)(2,1)S(1)}, bf16[64,256]{1,0:T(8,128)(2,1)S(1)}, u32[]{:S(2)}, u32[]{:S(2)}) collective-permute-start(bf16[64,256]{1,0:T(8,128)(2,1)S(1)} %get-tuple-element.70), channel_id=1, source_target_pairs={{0,3},{1,2},{2,1},{3,0},{4,7},{5,6},{6,5},{7,4},{8,11},{9,10},{10,... | collective-permute-start | bytes 98312 | tf_op jit(solution)/shard_map/ppermute | solution.py:50

commit v4 on v3

--- a/solution.py
+++ b/solution.py
@@ -48,6 +48,10 @@
 
 def exchanged(block, axis, mask):
     return lax.ppermute(block, axis, [(i, i ^ mask) for i in range(lax.axis_size(axis))])
+
+
+def crossed(block):
+    return lax.ppermute(block, "ctx", [(2, 4), (4, 2), (3, 5), (5, 3)])
 
 
 def part(pairs, offsets, doc_start, q_ref, g_ref, e_refs, dp_refs, s_ref):
@@ -207,7 +211,7 @@
 
 
 def last_body(share, *refs):
-    *parts, dk_ref, dv_ref = refs
+    parts, (dk_ref, dv_ref) = refs[-3::-1], refs[-2:]
     width = dk_ref.shape[-1]
     group = lax.axis_index("head") // share
     for other in range(len(parts) // share):
@@ -242,7 +246,7 @@
     mutual = lax.axis_size("ctx") == 2 * REACH
     four = exchanged(own, "ctx", 4) if mutual else shifted(own, 4)
     if mutual:
-        two = (exchanged(own, "ctx", 2), exchanged(own, "ctx", 6))
+        two = (exchanged(own, "ctx", 2), crossed(own))
     else:
         two = (shifted(own, 2),)
     q, g, start, e_own, dp_own, stats_own = call(
@@ -280,7 +284,7 @@
     )(two_terms, four_terms, odd_back)
     if mutual:
         backs = [exchanged(four_sum, "ctx", 4), exchanged(two_sum, "ctx", 2),
-                 exchanged(two_sum, "ctx", 6)]
+                 crossed(two_sum)]
         uses = [lambda i: i < 4, lambda i: i & 2 == 0, lambda i: i & 6 == 2]
     else:
         backs = [shifted(four_sum, -4), shifted(two_sum, -2)]
@@ -299,7 +303,8 @@
         functools.partial(sums_body, direct, uses), "sums", [VMEM] * (2 + len(backs)), outs, 0,
     )(own_terms, odd_back, *backs)
     if direct:
-        parts = [sums[0]] + [exchanged(sums[m], "head", m) for m in range(1, head_count)]
+        parts = [exchanged(sums[m], "head", m) for m in reversed(range(1, head_count))]
+        parts.append(sums[0])
         result_dims = (groups, tokens // head_count, width)
         d_keys, d_values = call(
             functools.partial(last_body, share), "last", [VMEM] * head_count,

time: 38.7 us -> 40.9 us (1.057)
  starting transfers between devices: 12.9 us -> 16.8 us
  waiting for transfers between devices: 15.3 us -> 13.6 us
    ppermute x11 -> x9, starting transfers between devices: 12.9 us -> 15.5 us  [exchanged(): lax.ppermute(block, axis, [(i, i ^ mask) for i in range(lax.axis_size(axi...]
    ppermute x11 -> x9, waiting for transfers between devices: 15.3 us -> 13.6 us  [exchanged(): lax.ppermute(block, axis, [(i, i ^ mask) for i in range(lax.axis_size(axi...]
    ppermute x0 -> x2, starting transfers between devices: none -> 1.31 us  [crossed(): return lax.ppermute(block, 'ctx', [(2, 4), (4, 2), (3, 5), (5, 3)])]
  transfers between devices with their start and end apart: 11 -> 11, of which waited for: 10 -> 6; matrix products, arithmetic and copies ran while one was open for 0% -> 0% of each run, Pallas kernels for 12% -> 12%
where the time goes in v4:
time: 40.9 us; the launch traced here: 40.7 us
  starting transfers between devices  16.8 us (41%)
  waiting for transfers between devices  13.6 us (33%)
  Pallas kernels  7.9 us (19%)
  local copies, waits for them, and re-layouts  1.6 us (4%)
  between operations  0.77 us (2%)
    ppermute x9, starting transfers between devices, exchanged(): lax.ppermute(block, axis, [(i, i ^ mask) for i in range(lax.axis_size(axi...  15.5 us
    ppermute x9, waiting for transfers between devices, exchanged(): lax.ppermute(block, axis, [(i, i ^ mask) for i in range(lax.axis_size(axi...  13.6 us
    pallas_call x1, Pallas kernels, per_device(): call(odd_terms_body, 'odd_terms', [VMEM] * 7, (shape((2 * tokens, 2 * wid...  2.35 us
    pallas_call x1, Pallas kernels, per_device(): call(own_terms_body, 'own_terms', [VMEM] * 13, (shape(queries.shape, bf16...  1.61 us
    ppermute x2, starting transfers between devices, crossed(): return lax.ppermute(block, 'ctx', [(2, 4), (4, 2), (3, 5), (5, 3)])  1.31 us
    pallas_call x1, Pallas kernels, per_device(): call(own_part_body, 'own_part', [SMEM] + [VMEM] * 3, (shape(queries.shape...  1.15 us
    squeeze x1, local copies, waits for them, and re-layouts, per_device(): lax.dynamic_index_in_dim(values, group, 0, keepdims=False)  0.94 us
  transfers between devices with their start and end apart: 11, of which 6 were waited for; matrix products, arithmetic and copies ran while one was open for 0% of the time, Pallas kernels for 12%

profile of v4, /device:TPU:0, one launch (start us, length us, event | category | flops | bytes accessed | tf_op | source)
XLA Modules:
  0.0 40.7 jit_solution(17660954834587615341)
XLA Ops:
  0.7 0.9 %dynamic-slice_bitcast_fusion = (bf16[256,128]{1,0:T(8,128)(2,1)S(1)}, bf16[256,128]{1,0:T(8,128)(2,1)S(1)}) fusion(bf16[2,256,128]{2,1,0:T(8,128)(2,1)} %param.7, s32[]{:T(128)S(6)} %select_n.35, bf16[2,256,128]{2,1,0:T(8,128)(2,1)} %param.6), kind=kLoop, calls=%fused_computation.5 | loop fusion | bytes 262148 | tf_op jit(solution)/shard_map/jit(dynamic_index_in_dim)/squeeze | solution.py:243
  1.6 3.0 %collective-permute-start = (bf16[256,256]{1,0:T(8,128)(2,1)S(1)}, bf16[256,256]{1,0:T(8,128)(2,1)S(1)}, u32[]{:S(2)}, u32[]{:S(2)}) collective-permute-start(bf16[256,256]{1,0:T(8,128)(2,1)S(1)} %pad_maximum_fusion.1.own_ref), channel_id=1, source_target_pairs={{0,16},{4,20},{8,24},{12,28},{16,0},{20,4},{24,8},{28,12},{1,17},{... | collective-permute-start | bytes 393224 | tf_op jit(solution)/shard_map/ppermute | solution.py:50
  4.7 0.7 %collective-permute-start.2 = (bf16[256,256]{1,0:T(8,128)(2,1)S(1)}, bf16[256,256]{1,0:T(8,128)(2,1)S(1)}, u32[]{:S(2)}, u32[]{:S(2)}) collective-permute-start(bf16[256,256]{1,0:T(8,128)(2,1)S(1)} %pad_maximum_fusion.1.own_ref), channel_id=1, source_target_pairs={{8,16},{16,8},{12,20},{20,12},{9,17},{17,9},{13,21},{21,13},{10,18... | collective-permute-start | bytes 393224 | tf_op jit(solution)/shard_map/ppermute | solution.py:54
  5.3 2.8 %collective-permute-start.1 = (bf16[256,256]{1,0:T(8,128)(2,1)S(1)}, bf16[256,256]{1,0:T(8,128)(2,1)S(1)}, u32[]{:S(2)}, u32[]{:S(2)}) collective-permute-start(bf16[256,256]{1,0:T(8,128)(2,1)S(1)} %pad_maximum_fusion.1.own_ref), channel_id=1, source_target_pairs={{0,8},{4,12},{8,0},{12,4},{16,24},{20,28},{24,16},{28,20},{1,9},{5... | collective-permute-start | bytes 393224 | tf_op jit(solution)/shard_map/ppermute | solution.py:50
  8.1 0.6 %copy-done.2 = s32[4]{0:T(128)S(1)} copy-done((s32[4]{0:T(128)S(1)}, s32[4]{0:T(128)}, u32[]{:S(2)}) %copy-start.2) | copy-done | bytes 40
  8.8 1.2 %own_part.1 = (bf16[4,256,128]{2,1,0:T(8,128)(2,1)S(1)}, bf16[4,256,128]{2,1,0:T(8,128)(2,1)S(1)}, s32[1,256]{1,0:T(1,128)S(1)}, f32[256,1024]{1,0:T(8,128)S(1)}...) custom-call(s32[4]{0:T(128)S(1)} %copy-done.2, bf16[4,256,128]{2,1,0:T(8,128)(2,1)S(1)} %copy-done, ...), custom_call_target="tpu_custom_call" | custom-call | flops 1342177 | bytes 1024 | tf_op jit(solution)/shard_map/own_part/pallas_call | solution.py:252
  10.0 0.0 collective-permute-done.pair_ref.four_ref
  10.0 0.6 %four_part.1 = (f32[256,1024]{1,0:T(8,128)S(1)}, f32[256,1024]{1,0:T(8,128)S(1)}, f32[3,1024]{1,0:T(4,128)S(1)}) custom-call(s32[1,256]{1,0:T(1,128)S(1)} %get-tuple-element.41.start_ref, bf16[4,256,128]{2,1,0:T(8,128)(2,1)S(1)} %get-tuple-element.42.q_ref, bf16[4,256,128]{2,1,0:T(8,128)(2,1)S(1)} %get-tuple-element.43.g_ref, ...), custom_call_target="tpu_custom_call" | custom-call | flops 1342177 | bytes 1024 | tf_op jit(solution)/shard_map/four_part/pallas_call | solution.py:258
  10.6 3.5 %collective-permute-done.1 = bf16[256,256]{1,0:T(8,128)(2,1)S(1)} collective-permute-done((bf16[256,256]{1,0:T(8,128)(2,1)S(1)}, bf16[256,256]{1,0:T(8,128)(2,1)S(1)}, u32[]{:S(2)}, u32[]{:S(2)}) %collective-permute-start.1) | collective-permute-done | bytes 131104 | tf_op jit(solution)/shard_map/ppermute | solution.py:50
  14.1 0.1 broadcast_select_fusion.2
  14.2 0.1 collective-permute-start.3
  14.3 0.6 %two_part.1 = (f32[256,1024]{1,0:T(8,128)S(1)}, f32[256,1024]{1,0:T(8,128)S(1)}, f32[3,1024]{1,0:T(4,128)S(1)}) custom-call(s32[1,256]{1,0:T(1,128)S(1)} %get-tuple-element.41.start_ref, bf16[4,256,128]{2,1,0:T(8,128)(2,1)S(1)} %get-tuple-element.42.q_ref, bf16[4,256,128]{2,1,0:T(8,128)(2,1)S(1)} %get-tuple-element.43.g_ref, ...), custom_call_target="tpu_custom_call" | custom-call | flops 1342177 | bytes 1024 | tf_op jit(solution)/shard_map/two_part/pallas_call | solution.py:266
  14.8 0.9 %collective-permute-done.3.odd_ref = bf16[512,256]{1,0:T(8,128)(2,1)S(1)} collective-permute-done((bf16[512,256]{1,0:T(8,128)(2,1)S(1)}, bf16[512,256]{1,0:T(8,128)(2,1)S(1)}, u32[]{:S(2)}, u32[]{:S(2)}) %collective-permute-start.3) | collective-permute-done | bytes 262176 | tf_op jit(solution)/shard_map/ppermute | solution.py:50
  15.8 2.3 %odd_terms.1 = (bf16[512,256]{1,0:T(8,128)(2,1)S(1)}, f32[4,1024]{1,0:T(4,128)S(1)}, bf16[256,1024]{1,0:T(8,128)(2,1)S(1)}, bf16[256,1024]{1,0:T(8,128)(2,1)S(1)}) custom-call(s32[1,256]{1,0:T(1,128)S(1)} %get-tuple-element.41.start_ref, bf16[4,256,128]{2,1,0:T(8,128)(2,1)S(1)} %get-tuple-element.42.q_ref, bf16[4,256,128]{2,1,0:T(8,128)(2,1)S(1)} %get-tuple-element.43.g_ref, ...), custom_call_target="tpu_custom_call" | custom-call | flops 4026531 | bytes 1024 | tf_op jit(solution)/shard_map/odd_terms/pallas_call | solution.py:269
  18.1 0.2 collective-permute-start.4
  18.4 0.8 %even_terms.1 = (f32[256,256]{1,0:T(8,128)S(1)}, f32[256,256]{1,0:T(8,128)S(1)}, bf16[256,1024]{1,0:T(8,128)(2,1)S(1)}, bf16[256,1024]{1,0:T(8,128)(2,1)S(1)}) custom-call(f32[256,1024]{1,0:T(8,128)S(1)} %get-tuple-element.53.e_two, f32[256,1024]{1,0:T(8,128)S(1)} %get-tuple-element.54.dp_two, f32[256,1024]{1,0:T(8,128)S(1)} %get-tuple-element.55.e_four, ...), custom_call_target="tpu_custom_call" | custom-call | flops 2684354 | bytes 1024 | tf_op jit(solution)/shard_map/even_terms/pallas_call | solution.py:277
  19.2 0.6 %collective-permute-done.4.odd_back = bf16[512,256]{1,0:T(8,128)(2,1)S(1)} collective-permute-done((bf16[512,256]{1,0:T(8,128)(2,1)S(1)}, bf16[512,256]{1,0:T(8,128)(2,1)S(1)}, u32[]{:S(2)}, u32[]{:S(2)}) %collective-permute-start.4) | collective-permute-done | bytes 262176 | tf_op jit(solution)/shard_map/ppermute | solution.py:50
  19.7 0.1 join.1
  19.8 0.8 %collective-permute-start.5 = (bf16[256,256]{1,0:T(8,128)(2,1)S(1)}, bf16[256,256]{1,0:T(8,128)(2,1)S(1)}, u32[]{:S(2)}, u32[]{:S(2)}) collective-permute-start(bf16[256,256]{1,0:T(8,128)(2,1)S(1)} %get-tuple-element.65), channel_id=1, source_target_pairs={{0,16},{4,20},{8,24},{12,28},{16,0},{20,4},{24,8},{28,12},{1,17},{... | collective-permute-start | bytes 393224 | tf_op jit(solution)/shard_map/ppermute | solution.py:50
  20.6 0.7 %collective-permute-start.7 = (bf16[256,256]{1,0:T(8,128)(2,1)S(1)}, bf16[256,256]{1,0:T(8,128)(2,1)S(1)}, u32[]{:S(2)}, u32[]{:S(2)}) collective-permute-start(bf16[256,256]{1,0:T(8,128)(2,1)S(1)} %get-tuple-element.66), channel_id=1, source_target_pairs={{8,16},{16,8},{12,20},{20,12},{9,17},{17,9},{13,21},{21,13},{10,18... | collective-permute-start | bytes 393224 | tf_op jit(solution)/shard_map/ppermute | solution.py:54
  21.3 4.1 %collective-permute-start.6 = (bf16[256,256]{1,0:T(8,128)(2,1)S(1)}, bf16[256,256]{1,0:T(8,128)(2,1)S(1)}, u32[]{:S(2)}, u32[]{:S(2)}) collective-permute-start(bf16[256,256]{1,0:T(8,128)(2,1)S(1)} %get-tuple-element.66), channel_id=1, source_target_pairs={{0,8},{4,12},{8,0},{12,4},{16,24},{20,28},{24,16},{28,20},{1,9},{5... | collective-permute-start | bytes 393224 | tf_op jit(solution)/shard_map/ppermute | solution.py:50
  25.3 1.6 %own_terms.1 = (bf16[4,256,128]{2,1,0:T(8,128)(2,1)}, f32[256,256]{1,0:T(8,128)S(1)}) custom-call(f32[256,1024]{1,0:T(8,128)S(1)} %get-tuple-element.38.e_own, f32[256,1024]{1,0:T(8,128)S(1)} %get-tuple-element.39.dp_own, f32[4,1024]{1,0:T(4,128)S(1)} %get-tuple-element.51.coef_ref, bf16[4,256,128]{2,1,0:T(8,128)(2,1)S(1)} %get-tuple-element.42.q_ref, ...), custom_call_target="tpu_custom_call" | custom-call | flops 4697620 | bytes 1024 | tf_op jit(solution)/shard_map/own_terms/pallas_call | solution.py:292
  26.9 0.0 collective-permute-done.5.refs_0_
  26.9 0.0 collective-permute-done.7.refs_2_
  27.0 4.3 %collective-permute-done.6.refs_1_ = bf16[256,256]{1,0:T(8,128)(2,1)S(1)} collective-permute-done((bf16[256,256]{1,0:T(8,128)(2,1)S(1)}, bf16[256,256]{1,0:T(8,128)(2,1)S(1)}, u32[]{:S(2)}, u32[]{:S(2)}) %collective-permute-start.6) | collective-permute-done | bytes 131104 | tf_op jit(solution)/shard_map/ppermute | solution.py:50
  31.3 0.1 sums.1
  31.4 3.9 %collective-permute-start.8 = (bf16[64,256]{1,0:T(8,128)(2,1)S(1)}, bf16[64,256]{1,0:T(8,128)(2,1)S(1)}, u32[]{:S(2)}, u32[]{:S(2)}) collective-permute-start(bf16[64,256]{1,0:T(8,128)(2,1)S(1)} %get-tuple-element.67), channel_id=1, source_target_pairs={{0,3},{1,2},{2,1},{3,0},{4,7},{5,6},{6,5},{7,4},{8,11},{9,10},{10,... | collective-permute-start | bytes 98312 | tf_op jit(solution)/shard_map/ppermute | solution.py:50
  35.3 0.0 collective-permute-start.9
  35.3 0.6 %collective-permute-start.10 = (bf16[64,256]{1,0:T(8,128)(2,1)S(1)}, bf16[64,256]{1,0:T(8,128)(2,1)S(1)}, u32[]{:S(2)}, u32[]{:S(2)}) collective-permute-start(bf16[64,256]{1,0:T(8,128)(2,1)S(1)} %get-tuple-element.69), channel_id=1, source_target_pairs={{0,1},{1,0},{2,3},{3,2},{4,5},{5,4},{6,7},{7,6},{8,9},{9,8},{10,11... | collective-permute-start | bytes 98312 | tf_op jit(solution)/shard_map/ppermute | solution.py:50
  35.9 1.4 %collective-permute-done.8.refs_0_ = bf16[64,256]{1,0:T(8,128)(2,1)S(1)} collective-permute-done((bf16[64,256]{1,0:T(8,128)(2,1)S(1)}, bf16[64,256]{1,0:T(8,128)(2,1)S(1)}, u32[]{:S(2)}, u32[]{:S(2)}) %collective-permute-start.8) | collective-permute-done | bytes 32800 | tf_op jit(solution)/shard_map/ppermute | solution.py:50
  37.3 2.8 %collective-permute-done.9.refs_1_ = bf16[64,256]{1,0:T(8,128)(2,1)S(1)} collective-permute-done((bf16[64,256]{1,0:T(8,128)(2,1)S(1)}, bf16[64,256]{1,0:T(8,128)(2,1)S(1)}, u32[]{:S(2)}, u32[]{:S(2)}) %collective-permute-start.9) | collective-permute-done | bytes 32800 | tf_op jit(solution)/shard_map/ppermute | solution.py:50
  40.1 0.6 %last.1 = (bf16[2,64,128]{2,1,0:T(8,128)(2,1)}, bf16[2,64,128]{2,1,0:T(8,128)(2,1)}) custom-call(bf16[64,256]{1,0:T(8,128)(2,1)S(1)} %collective-permute-done.8.refs_0_, bf16[64,256]{1,0:T(8,128)(2,1)S(1)} %collective-permute-done.9.refs_1_, bf16[64,256]{1,0:T(8,128)(2,1)S(1)} %collective-permute-done.10.refs_2_, f32[64,256]{1,0:T(8,128)S(1)} %get-tuple-element.70.refs_3_), custom_call_target="tpu_custom_call" | custom-call | bytes 1024 | tf_op jit(solution)/shard_map/last/pallas_call | solution.py:309
  (10 shorter events, 0.1 us)
Async XLA Ops:
  0.6 7.5 %copy-start = (bf16[4,256,128]{2,1,0:T(8,128)(2,1)S(1)}, bf16[4,256,128]{2,1,0:T(8,128)(2,1)}, u32[]{:S(2)}) copy-start(bf16[4,256,128]{2,1,0:T(8,128)(2,1)} %q_in.1) | copy-start | bytes 786436
  0.7 7.5 %copy-start.1 = (bf16[4,256,128]{2,1,0:T(8,128)(2,1)S(1)}, bf16[4,256,128]{2,1,0:T(8,128)(2,1)}, u32[]{:S(2)}) copy-start(bf16[4,256,128]{2,1,0:T(8,128)(2,1)} %g_in.1) | copy-start | bytes 786436
  1.6 8.3 %collective-permute-start = (bf16[256,256]{1,0:T(8,128)(2,1)S(1)}, bf16[256,256]{1,0:T(8,128)(2,1)S(1)}, u32[]{:S(2)}, u32[]{:S(2)}) collective-permute-start(bf16[256,256]{1,0:T(8,128)(2,1)S(1)} %pad_maximum_fusion.1.own_ref), channel_id=1, source_target_pairs={{0,16},{4,20},{8,24},{12,28},{16,0},{20,4},{24,8},{28,12},{1,17},{... | collective-permute-start | bytes 393224 | tf_op jit(solution)/shard_map/ppermute | solution.py:50
  4.7 5.9 %collective-permute-start.2 = (bf16[256,256]{1,0:T(8,128)(2,1)S(1)}, bf16[256,256]{1,0:T(8,128)(2,1)S(1)}, u32[]{:S(2)}, u32[]{:S(2)}) collective-permute-start(bf16[256,256]{1,0:T(8,128)(2,1)S(1)} %pad_maximum_fusion.1.own_ref), channel_id=1, source_target_pairs={{8,16},{16,8},{12,20},{20,12},{9,17},{17,9},{13,21},{21,13},{10,18... | collective-permute-start | bytes 393224 | tf_op jit(solution)/shard_map/ppermute | solution.py:54
  5.3 8.7 %collective-permute-start.1 = (bf16[256,256]{1,0:T(8,128)(2,1)S(1)}, bf16[256,256]{1,0:T(8,128)(2,1)S(1)}, u32[]{:S(2)}, u32[]{:S(2)}) collective-permute-start(bf16[256,256]{1,0:T(8,128)(2,1)S(1)} %pad_maximum_fusion.1.own_ref), channel_id=1, source_target_pairs={{0,8},{4,12},{8,0},{12,4},{16,24},{20,28},{24,16},{28,20},{1,9},{5... | collective-permute-start | bytes 393224 | tf_op jit(solution)/shard_map/ppermute | solution.py:50
  8.1 0.7 %copy-start.2 = (s32[4]{0:T(128)S(1)}, s32[4]{0:T(128)}, u32[]{:S(2)}) copy-start(s32[4]{0:T(128)} %lengths_ref.1) | copy-start | bytes 52
  14.2 1.6 %collective-permute-start.3 = (bf16[512,256]{1,0:T(8,128)(2,1)S(1)}, bf16[512,256]{1,0:T(8,128)(2,1)S(1)}, u32[]{:S(2)}, u32[]{:S(2)}) collective-permute-start(bf16[512,256]{1,0:T(8,128)(2,1)S(1)} %pad_maximum_fusion), channel_id=1, source_target_pairs={{0,4},{4,0},{8,12},{12,8},{16,20},{20,16},{24,28},{28,24},{1,5},{5... | collective-permute-start | bytes 786440 | tf_op jit(solution)/shard_map/ppermute | solution.py:50
  18.1 1.6 %collective-permute-start.4 = (bf16[512,256]{1,0:T(8,128)(2,1)S(1)}, bf16[512,256]{1,0:T(8,128)(2,1)S(1)}, u32[]{:S(2)}, u32[]{:S(2)}) collective-permute-start(bf16[512,256]{1,0:T(8,128)(2,1)S(1)} %get-tuple-element.62), channel_id=1, source_target_pairs={{0,4},{4,0},{8,12},{12,8},{16,20},{20,16},{24,28},{28,24},{1,5},{5... | collective-permute-start | bytes 786440 | tf_op jit(solution)/shard_map/ppermute | solution.py:50
  19.8 7.1 %collective-permute-start.5 = (bf16[256,256]{1,0:T(8,128)(2,1)S(1)}, bf16[256,256]{1,0:T(8,128)(2,1)S(1)}, u32[]{:S(2)}, u32[]{:S(2)}) collective-permute-start(bf16[256,256]{1,0:T(8,128)(2,1)S(1)} %get-tuple-element.65), channel_id=1, source_target_pairs={{0,16},{4,20},{8,24},{12,28},{16,0},{20,4},{24,8},{28,12},{1,17},{... | collective-permute-start | bytes 393224 | tf_op jit(solution)/shard_map/ppermute | solution.py:50
  20.6 6.4 %collective-permute-start.7 = (bf16[256,256]{1,0:T(8,128)(2,1)S(1)}, bf16[256,256]{1,0:T(8,128)(2,1)S(1)}, u32[]{:S(2)}, u32[]{:S(2)}) collective-permute-start(bf16[256,256]{1,0:T(8,128)(2,1)S(1)} %get-tuple-element.66), channel_id=1, source_target_pairs={{8,16},{16,8},{12,20},{20,12},{9,17},{17,9},{13,21},{21,13},{10,18... | collective-permute-start | bytes 393224 | tf_op jit(solution)/shard_map/ppermute | solution.py:54
  21.3 10.0 %collective-permute-start.6 = (bf16[256,256]{1,0:T(8,128)(2,1)S(1)}, bf16[256,256]{1,0:T(8,128)(2,1)S(1)}, u32[]{:S(2)}, u32[]{:S(2)}) collective-permute-start(bf16[256,256]{1,0:T(8,128)(2,1)S(1)} %get-tuple-element.66), channel_id=1, source_target_pairs={{0,8},{4,12},{8,0},{12,4},{16,24},{20,28},{24,16},{28,20},{1,9},{5... | collective-permute-start | bytes 393224 | tf_op jit(solution)/shard_map/ppermute | solution.py:50
  31.4 5.9 %collective-permute-start.8 = (bf16[64,256]{1,0:T(8,128)(2,1)S(1)}, bf16[64,256]{1,0:T(8,128)(2,1)S(1)}, u32[]{:S(2)}, u32[]{:S(2)}) collective-permute-start(bf16[64,256]{1,0:T(8,128)(2,1)S(1)} %get-tuple-element.67), channel_id=1, source_target_pairs={{0,3},{1,2},{2,1},{3,0},{4,7},{5,6},{6,5},{7,4},{8,11},{9,10},{10,... | collective-permute-start | bytes 98312 | tf_op jit(solution)/shard_map/ppermute | solution.py:50
  35.3 4.8 %collective-permute-start.9 = (bf16[64,256]{1,0:T(8,128)(2,1)S(1)}, bf16[64,256]{1,0:T(8,128)(2,1)S(1)}, u32[]{:S(2)}, u32[]{:S(2)}) collective-permute-start(bf16[64,256]{1,0:T(8,128)(2,1)S(1)} %get-tuple-element.68), channel_id=1, source_target_pairs={{0,2},{1,3},{2,0},{3,1},{4,6},{5,7},{6,4},{7,5},{8,10},{9,11},{10,... | collective-permute-start | bytes 98312 | tf_op jit(solution)/shard_map/ppermute | solution.py:50
  35.3 4.8 %collective-permute-start.10 = (bf16[64,256]{1,0:T(8,128)(2,1)S(1)}, bf16[64,256]{1,0:T(8,128)(2,1)S(1)}, u32[]{:S(2)}, u32[]{:S(2)}) collective-permute-start(bf16[64,256]{1,0:T(8,128)(2,1)S(1)} %get-tuple-element.69), channel_id=1, source_target_pairs={{0,1},{1,0},{2,3},{3,2},{4,5},{5,4},{6,7},{7,6},{8,9},{9,8},{10,11... | collective-permute-start | bytes 98312 | tf_op jit(solution)/shard_map/ppermute | solution.py:50

commit v5 on v4

v5 whole, which is shorter than its diff:
```python
import functools
import math

import jax
import jax.numpy as jnp
from jax import lax
from jax.experimental import pallas as pl
from jax.experimental.pallas import tpu as pltpu
from jax.sharding import PartitionSpec as P

GROUP = 8
REACH = 4
MASKED = -1e30
NT = (((1,), (1,)), ((), ()))
NN = (((1,), (0,)), ((), ()))
VMEM = pl.BlockSpec(memory_space=pltpu.VMEM)
SMEM = pl.BlockSpec(memory_space=pltpu.SMEM)
bf16, f32, i32 = jnp.bfloat16, jnp.float32, jnp.int32


def dot(a, b, dims=NN):
    return lax.dot_general(a, b, dims, preferred_element_type=f32)


def shape(dims, dtype):
    return jax.ShapeDtypeStruct(dims, dtype)


def call(body, name, in_specs, outs, scratch=()):
    return pl.pallas_call(
        body,
        out_shape=outs,
        in_specs=in_specs,
        out_specs=(VMEM,) * len(outs),
        scratch_shapes=scratch,
        compiler_params=pltpu.CompilerParams(vmem_limit_bytes=20 * 2**20),
        cost_estimate=pl.CostEstimate(flops=2**20, bytes_accessed=2**10, transcendentals=0),
        name=name,
    )


def shifted(block, distance):
    count = lax.axis_size("ctx")
    route = [(i - distance, i) for i in range(count) if 0 <= i - distance < count]
    return lax.ppermute(block, "ctx", route)


def exchanged(block, axis, mask):
    return lax.ppermute(block, axis, [(i, i ^ mask) for i in range(lax.axis_size(axis))])


def second_core():
    return lax.rem(lax.axis_index("ctx"), 2) == 1


def doc_starts(lengths_ref, block, tokens):
    row_pos = block * tokens + lax.broadcasted_iota(i32, (1, tokens), 1)
    starts = jnp.zeros((1, tokens), i32)
    end = jnp.int32(0)
    for d in range(lengths_ref.shape[0]):
        end = end + lengths_ref[d]
        starts = jnp.where(row_pos >= end, end, starts)
    return starts


def unit(pair, key_block, starts, q_ref, g_ref, e_ref, dp_ref, stats_ref, causal=False):
    heads, tokens, width = q_ref.shape
    factor = width ** -0.5 * math.log2(math.e)
    key_iota = lax.broadcasted_iota(i32, (tokens, 1), 0)
    allowed = key_block * tokens + key_iota >= starts
    if causal:
        allowed = allowed & (key_iota <= lax.broadcasted_iota(i32, (1, tokens), 1))
    for h in range(heads):
        lanes = slice(h * tokens, (h + 1) * tokens)
        s = jnp.where(allowed, dot(pair[:, :width], q_ref[h], NT), MASKED)
        top = jnp.max(s, axis=0, keepdims=True)
        e = jnp.exp2((s - top) * factor)
        dp = dot(pair[:, width:], g_ref[h], NT)
        e_ref[:, lanes] = e
        dp_ref[:, lanes] = dp
        stats_ref[0:1, lanes] = top
        stats_ref[1:2, lanes] = jnp.sum(e, axis=0, keepdims=True)
        stats_ref[2:3, lanes] = jnp.sum(e * dp, axis=0, keepdims=True)


def rows_of(ref, first=0):
    return [ref[first + row:first + row + 1] for row in range(3)]


def joined(parts, factor):
    top = functools.reduce(jnp.maximum, [part[0] for part in parts])
    gains = [jnp.exp2((part[0] - top) * factor) for part in parts]
    total = sum(gain * part[1] for gain, part in zip(gains, parts))
    weighted = sum(gain * part[2] for gain, part in zip(gains, parts))
    return top, total, weighted


def own_unit_body(lengths_ref, q_in, g_in, own_ref,
                  q_ref, g_ref, starts_ref, e_ref, dp_ref, stats_ref):
    tokens = q_in.shape[1]
    here = lax.axis_index("ctx")
    starts = doc_starts(lengths_ref, here, tokens)
    starts_ref[0:1] = starts
    starts_ref[1:2] = doc_starts(lengths_ref, jnp.bitwise_xor(here, 1), tokens)
    q_ref[...] = q_in[...]
    g_ref[...] = g_in[...]
    unit(own_ref, here, starts, q_in, g_in, e_ref, dp_ref, stats_ref, causal=True)


def four_units_body(starts_ref, q_ref, g_ref, other_q, other_g, own_ref, four_ref,
                    e_four, dp_four, stats_four, e_side, dp_side, stats_side):
    here = lax.axis_index("ctx")
    unit(four_ref, here - 4, starts_ref[0:1], q_ref, g_ref, e_four, dp_four, stats_four)
    side = jnp.where(second_core(), four_ref[...], own_ref[...])
    unit(side, here - jnp.where(second_core(), 4, 0), starts_ref[1:2], other_q, other_g,
         e_side, dp_side, stats_side)


def two_units_body(starts_ref, q_ref, g_ref, other_q, other_g, two_ref,
                   stats_own, stats_four, stats_side,
                   e_two, dp_two, stats_two, e_cross, dp_cross, stats_cross, given_ref):
    here = lax.axis_index("ctx")
    factor = q_ref.shape[-1] ** -0.5 * math.log2(math.e)
    unit(two_ref, here - 2, starts_ref[0:1], q_ref, g_ref, e_two, dp_two, stats_two)
    unit(two_ref, here - 2, starts_ref[1:2], other_q, other_g, e_cross, dp_cross, stats_cross)
    mine = joined([rows_of(ref) for ref in (stats_own, stats_four, stats_two)], factor)
    others = joined([rows_of(ref) for ref in (stats_side, stats_cross)], factor)
    for row, value in enumerate(mine + others):
        given_ref[row:row + 1] = value
    given_ref[6:8] = jnp.zeros((2, given_ref.shape[1]), f32)


def slopes(e_ref, dp_ref, gain, delta, p_ref, ds_ref):
    p = e_ref[...] * gain
    p_ref[...] = p.astype(bf16)
    ds_ref[...] = (p * (dp_ref[...] - delta)).astype(bf16)


def flat(ref):
    heads, tokens, width = ref.shape
    return ref[...].reshape(heads * tokens, width)


def add_terms(sum_ref, ds_ref, p_ref, q_ref, g_ref, fresh):
    width = q_ref.shape[-1]
    dk = dot(ds_ref[...], flat(q_ref)) * width ** -0.5
    dv = dot(p_ref[...], flat(g_ref))
    if fresh:
        sum_ref[:, :width] = dk
        sum_ref[:, width:] = dv
    else:
        sum_ref[:, :width] += dk
        sum_ref[:, width:] += dv


def four_terms_body(given_ref, taken_ref, stats_own, stats_four, stats_two, stats_side,
                    stats_cross, e_four, dp_four, e_side, dp_side,
                    q_ref, g_ref, other_q, other_g,
                    coef_ref, terms_ref, ds_four, ds_side, p_side, p_four, sum_ref):
    factor = q_ref.shape[-1] ** -0.5 * math.log2(math.e)
    coefs = []
    for at, refs in ((0, (stats_own, stats_four, stats_two)), (3, (stats_side, stats_cross))):
        parts = [rows_of(given_ref, at), rows_of(taken_ref, 3 - at)]
        top, total, weighted = joined(parts, factor)
        inverse = 1.0 / total
        coefs.append(weighted * inverse)
        coefs.extend(jnp.exp2((ref[0:1] - top) * factor) * inverse for ref in refs)
    for row, value in enumerate(coefs):
        coef_ref[row:row + 1] = value
    slopes(e_four, dp_four, coefs[2], coefs[0], p_four, ds_four)
    slopes(e_side, dp_side, coefs[5], coefs[4], p_side, ds_side)
    add_terms(sum_ref, ds_four, p_four, q_ref, g_ref, True)

    @pl.when(second_core())
    def _():
        add_terms(sum_ref, ds_side, p_side, other_q, other_g, False)

    terms_ref[...] = sum_ref[...].astype(bf16)


def two_terms_body(coef_ref, e_two, dp_two, e_cross, dp_cross, q_ref, g_ref, other_q, other_g,
                   terms_ref, ds_two, ds_cross, p_ref, sum_ref):
    slopes(e_two, dp_two, coef_ref[3:4], coef_ref[0:1], p_ref.at[0], ds_two)
    slopes(e_cross, dp_cross, coef_ref[6:7], coef_ref[4:5], p_ref.at[1], ds_cross)
    add_terms(sum_ref, ds_two, p_ref.at[0], q_ref, g_ref, True)
    add_terms(sum_ref, ds_cross, p_ref.at[1], other_q, other_g, False)
    terms_ref[...] = sum_ref[...].astype(bf16)


def query_grads(keys, ds_refs, out_ref):
    heads, tokens, width = out_ref.shape
    turned = [key.T for key in keys]
    for h in range(heads):
        lanes = slice(h * tokens, (h + 1) * tokens)
        dqt = sum(dot(kt, ds[:, lanes]) for kt, ds in zip(turned, ds_refs))
        out_ref[h] = (dqt.T * width ** -0.5).astype(out_ref.dtype)


def own_terms_body(coef_ref, e_own, dp_own, q_ref, g_ref, other_q, other_g, ds_side, p_side,
                   own_ref, two_ref, four_ref, ds_two, ds_four, ds_cross,
                   terms_ref, dq_ref, other_dq_ref, ds_own, p_ref):
    width = q_ref.shape[-1]
    own, two, four = [ref[:, :width] for ref in (own_ref, two_ref, four_ref)]
    query_grads([jnp.where(second_core(), four, own), two], [ds_side, ds_cross], other_dq_ref)
    slopes(e_own, dp_own, coef_ref[1:2], coef_ref[0:1], p_ref, ds_own)
    add_terms(terms_ref, ds_own, p_ref, q_ref, g_ref, True)

    @pl.when(jnp.logical_not(second_core()))
    def _():
        add_terms(terms_ref, ds_side, p_side, other_q, other_g, False)

    query_grads([own, two, four], [ds_own, ds_two, ds_four], dq_ref)


def add_grads_body(mine_ref, taken_ref, dq_ref):
    dq_ref[...] = (mine_ref[...] + taken_ref[...].astype(f32)).astype(dq_ref.dtype)


def first_sum_body(use, own_terms, back, out_ref):
    taken = jnp.where(use(lax.axis_index("ctx")), back[...].astype(f32), 0.0)
    out_ref[...] = own_terms[...] + taken


def sums_body(direct, uses, own_terms, *refs):
    backs, outs = refs[:len(uses)], refs[len(uses):]
    tokens = own_terms.shape[0]
    ctx = lax.axis_index("ctx")
    head = lax.axis_index("head")
    count = lax.axis_size("head")
    rows_each = tokens // count

    def total(rows):
        value = own_terms[rows]
        for back, use in zip(backs, uses):
            value = value + jnp.where(use(ctx), back[rows].astype(f32), 0.0)
        return value

    if not direct:
        outs[0][...] = total(slice(0, tokens)).astype(bf16)
        return
    for mask in range(count):
        place = jnp.bitwise_xor(head, mask)
        value = total(pl.ds(pl.multiple_of(place * rows_each, rows_each), rows_each))
        outs[mask][...] = value.astype(outs[mask].dtype)


def last_body(share, *refs):
    parts, (dk_ref, dv_ref) = refs[-3::-1], refs[-2:]
    width = dk_ref.shape[-1]
    group = lax.axis_index("head") // share
    for other in range(len(parts) // share):
        mine = parts[other * share:(other + 1) * share]
        value = sum(ref[...].astype(f32) for ref in mine).astype(bf16)
        place = jnp.bitwise_xor(group, other)
        dk_ref[place] = value[:, :width]
        dv_ref[place] = value[:, width:]


def per_device(queries, keys, values, d_out, doc_lengths):
    heads, tokens, width = queries.shape
    head_count = lax.axis_size("head")
    share = GROUP // heads
    groups = head_count // share
    rows = heads * tokens
    ctx = lax.axis_index("ctx")
    mutual = lax.axis_size("ctx") == 2 * REACH
    pair = (tokens, 2 * width)
    all_rows = (heads, tokens, width)
    stats = shape((3, rows), f32)
    wide = shape((tokens, rows), f32)
    half = shape((tokens, rows), bf16)
    half_scratch = pltpu.VMEM((tokens, rows), bf16)
    pair_scratch = pltpu.VMEM(pair, f32)

    group = lax.axis_index("head") // share
    own = jnp.concatenate(
        [lax.dynamic_index_in_dim(keys, group, 0, keepdims=False),
         lax.dynamic_index_in_dim(values, group, 0, keepdims=False)], axis=1)
    four = exchanged(own, "ctx", 4) if mutual else shifted(own, 4)
    if mutual:
        two = (exchanged(own, "ctx", 6), exchanged(own, "ctx", 2))
    else:
        two = (shifted(own, 2),)
    q, g, starts, e_own, dp_own, stats_own = call(
        own_unit_body, "own_unit", [SMEM] + [VMEM] * 3,
        (shape(all_rows, bf16), shape(all_rows, bf16), shape((2, tokens), i32),
         wide, wide, stats))(doc_lengths, queries, d_out, own)
    other_q = exchanged(queries, "ctx", 1)
    other_g = exchanged(d_out, "ctx", 1)
    four, starts = lax.optimization_barrier((four, starts))
    e_four, dp_four, stats_four, e_side, dp_side, stats_side = call(
        four_units_body, "four_units", [VMEM] * 7, (wide, wide, stats) * 2,
    )(starts, q, g, other_q, other_g, own, four)
    *two, stats_four = lax.optimization_barrier((*two, stats_four))
    two = jnp.where(ctx & 2 == 2, two[1], two[0]) if mutual else two[0]
    e_two, dp_two, stats_two, e_cross, dp_cross, stats_cross, given = call(
        two_units_body, "two_units", [VMEM] * 9,
        (wide, wide, stats) * 2 + (shape((8, rows), f32),),
    )(starts, q, g, other_q, other_g, two, stats_own, stats_four, stats_side)
    taken = exchanged(given, "ctx", 1)
    coef, four_terms, ds_four, ds_side, p_side = call(
        four_terms_body, "four_terms", [VMEM] * 15,
        (shape((8, rows), f32), shape(pair, bf16), half, half, half),
        (half_scratch, pair_scratch),
    )(given, taken, stats_own, stats_four, stats_two, stats_side, stats_cross,
      e_four, dp_four, e_side, dp_side, q, g, other_q, other_g)
    two_terms, ds_two, ds_cross = call(
        two_terms_body, "two_terms", [VMEM] * 9, (shape(pair, bf16), half, half),
        (pltpu.VMEM((2, tokens, rows), bf16), pair_scratch),
    )(coef, e_two, dp_two, e_cross, dp_cross, q, g, other_q, other_g)
    if mutual:
        backs = [exchanged(four_terms, "ctx", 4), exchanged(two_terms, "ctx", 6),
                 exchanged(two_terms, "ctx", 2)]
        uses = [lambda i: i < 4, lambda i: i & 6 == 2, lambda i: i & 2 == 0]
    else:
        backs = [shifted(four_terms, -4), shifted(two_terms, -2)]
        uses = [lambda i: True] * 2
    own_terms, my_grads, other_grads = call(
        own_terms_body, "own_terms", [VMEM] * 15,
        (shape(pair, f32), shape(all_rows, f32), shape(all_rows, bf16)),
        (half_scratch, half_scratch),
    )(coef, e_own, dp_own, q, g, other_q, other_g, ds_side, p_side, own, two, four,
      ds_two, ds_four, ds_cross)
    own_terms, = call(
        functools.partial(first_sum_body, uses[0]), "first_sum", [VMEM] * 2,
        (shape(pair, f32),))(own_terms, backs[0])
    direct = head_count == 2 * share and share == 2
    slice_dims = (tokens // head_count, 2 * width)
    outs = ((shape(slice_dims, f32),) + (shape(slice_dims, bf16),) * (head_count - 1)
            if direct else (shape(pair, bf16),))
    sums = call(
        functools.partial(sums_body, direct, uses[1:]), "sums", [VMEM] * len(backs), outs,
    )(own_terms, *backs[1:])
    other_grads, kept = lax.optimization_barrier((other_grads, sums[0]))
    taken_grads = exchanged(other_grads, "ctx", 1)
    d_queries, = call(
        add_grads_body, "add_grads", [VMEM] * 2, (shape(all_rows, bf16),),
    )(my_grads, taken_grads)
    if direct:
        parts = [exchanged(sums[m], "head", m) for m in reversed(range(1, head_count))]
        parts.append(kept)
        *parts, d_queries = lax.optimization_barrier((*parts, d_queries))
        result_dims = (groups, tokens // head_count, width)
        d_keys, d_values = call(
            functools.partial(last_body, share), "last", [VMEM] * head_count,
            (shape(result_dims, bf16),) * 2)(*parts)
        return d_queries, d_keys, d_values
    slices = lax.all_to_all(kept.reshape(head_count, *slice_dims), "head", 0, 0)
    result = jnp.sum(slices.reshape(groups, share, *slice_dims).astype(f32), axis=1).astype(bf16)
    return d_queries, result[..., :width], result[..., width:]


def solution(mesh):
    placed = (
        P("head", "ctx", None),
        P(None, "ctx", None),
        P(None, "ctx", None),
        P("head", "ctx", None),
        P(),
    )
    return jax.shard_map(
        per_device,
        mesh=mesh,
        in_specs=placed,
        out_specs=(
            P("head", "ctx", None),
            P(None, ("ctx", "head"), None),
            P(None, ("ctx", "head"), None),
        ),
        check_vma=False,
    )
```

time: 40.9 us -> 36.7 us (0.90)
  starting transfers between devices: 16.8 us -> 13.4 us
  waiting for transfers between devices: 13.6 us -> 12.8 us
    ppermute x9 -> x13, starting transfers between devices: 15.5 us -> 13.4 us  [exchanged(): lax.ppermute(block, axis, [(i, i ^ mask) for i in range(lax.axis_size(axi...]
    ppermute x2 -> x0, starting transfers between devices: 1.31 us -> none  [crossed(): return lax.ppermute(block, 'ctx', [(2, 4), (4, 2), (3, 5), (5, 3)])]
    ppermute x9 -> x13, waiting for transfers between devices: 13.6 us -> 12.8 us  [exchanged(): lax.ppermute(block, axis, [(i, i ^ mask) for i in range(lax.axis_size(axi...]
    pallas_call x8 -> x9, Pallas kernels: 7.25 us -> 7.3 us  [the longest x1 1.57 us: per_device(): call(own_terms_body, 'own_terms', [VMEM] * 15, (shape(pair, f32), shape(a...]
  transfers between devices with their start and end apart: 11 -> 13, of which waited for: 6 -> 9; matrix products, arithmetic and copies ran while one was open for 0% -> 3% of each run, Pallas kernels for 12% -> 15%
where the time goes in v5:
time: 36.7 us; the launch traced here: 36.5 us
  starting transfers between devices  13.4 us (37%)
  waiting for transfers between devices  12.8 us (35%)
  Pallas kernels  7.94 us (22%)
  local copies, waits for them, and re-layouts  1.6 us (4%)
  between operations  0.72 us (2%)
    ppermute x13, starting transfers between devices, exchanged(): lax.ppermute(block, axis, [(i, i ^ mask) for i in range(lax.axis_size(axi...  13.4 us
    ppermute x13, waiting for transfers between devices, exchanged(): lax.ppermute(block, axis, [(i, i ^ mask) for i in range(lax.axis_size(axi...  12.8 us
    pallas_call x1, Pallas kernels, per_device(): call(own_terms_body, 'own_terms', [VMEM] * 15, (shape(pair, f32), shape(a...  1.57 us
    pallas_call x1, Pallas kernels, per_device(): call(own_unit_body, 'own_unit', [SMEM] + [VMEM] * 3, (shape(all_rows, bf1...  1.2 us
    pallas_call x1, Pallas kernels, per_device(): call(two_units_body, 'two_units', [VMEM] * 9, (wide, wide, stats) * 2 + (...  1.06 us
    pallas_call x1, Pallas kernels, per_device(): call(four_units_body, 'four_units', [VMEM] * 7, (wide, wide, stats) * 2)  1.04 us
    squeeze x1, local copies, waits for them, and re-layouts, per_device(): lax.dynamic_index_in_dim(values, group, 0, keepdims=False)  0.94 us
    pallas_call x1, Pallas kernels, per_device(): call(four_terms_body, 'four_terms', [VMEM] * 15, (shape((8, rows), f32),...  0.81 us
  transfers between devices with their start and end apart: 13, of which 9 were waited for; matrix products, arithmetic and copies ran while one was open for 3% of the time, Pallas kernels for 15%

profile of v5, /device:TPU:0, one launch (start us, length us, event | category | flops | bytes accessed | tf_op | source)
XLA Modules:
  0.0 36.5 jit_solution(480461009888320712)
XLA Ops:
  0.6 0.5 %collective-permute-start.1 = (bf16[4,256,128]{2,1,0:T(8,128)(2,1)}, bf16[4,256,128]{2,1,0:T(8,128)(2,1)S(1)}, u32[]{:S(2)}, u32[]{:S(2)}) collective-permute-start(bf16[4,256,128]{2,1,0:T(8,128)(2,1)} %q_in.1), channel_id=1, source_target_pairs={{0,4},{4,0},{8,12},{12,8},{16,20},{20,16},{24,28},{28,24},{1,5},{5... | collective-permute-start | bytes 786440 | tf_op jit(solution)/shard_map/ppermute | solution.py:49
  1.1 0.1 collective-permute-start.2
  1.2 0.9 %dynamic-slice_bitcast_fusion = (bf16[256,128]{1,0:T(8,128)(2,1)S(1)}, bf16[256,128]{1,0:T(8,128)(2,1)S(1)}) fusion(bf16[2,256,128]{2,1,0:T(8,128)(2,1)} %param.7, s32[]{:T(128)S(6)} %select_n.19, bf16[2,256,128]{2,1,0:T(8,128)(2,1)} %param.6), kind=kLoop, calls=%fused_computation.2 | loop fusion | bytes 262148 | tf_op jit(solution)/shard_map/jit(dynamic_index_in_dim)/squeeze | solution.py:278
  2.2 3.0 %collective-permute-start = (bf16[256,256]{1,0:T(8,128)(2,1)S(1)}, bf16[256,256]{1,0:T(8,128)(2,1)S(1)}, u32[]{:S(2)}, u32[]{:S(2)}) collective-permute-start(bf16[256,256]{1,0:T(8,128)(2,1)S(1)} %pad_maximum_fusion.own_ref), channel_id=1, source_target_pairs={{0,16},{4,20},{8,24},{12,28},{16,0},{20,4},{24,8},{28,12},{1,17},{... | collective-permute-start | bytes 393224 | tf_op jit(solution)/shard_map/ppermute | solution.py:49
  5.2 1.5 %collective-permute-start.4 = (bf16[256,256]{1,0:T(8,128)(2,1)S(1)}, bf16[256,256]{1,0:T(8,128)(2,1)S(1)}, u32[]{:S(2)}, u32[]{:S(2)}) collective-permute-start(bf16[256,256]{1,0:T(8,128)(2,1)S(1)} %pad_maximum_fusion.own_ref), channel_id=1, source_target_pairs={{0,8},{4,12},{8,0},{12,4},{16,24},{20,28},{24,16},{28,20},{1,9},{5... | collective-permute-start | bytes 393224 | tf_op jit(solution)/shard_map/ppermute | solution.py:49
  6.7 0.0 collective-permute-start.3
  6.8 0.6 %copy-done.2 = s32[4]{0:T(128)S(1)} copy-done((s32[4]{0:T(128)S(1)}, s32[4]{0:T(128)}, u32[]{:S(2)}) %copy-start.2) | copy-done | bytes 40
  7.4 1.2 %own_unit.1 = (bf16[4,256,128]{2,1,0:T(8,128)(2,1)S(1)}, bf16[4,256,128]{2,1,0:T(8,128)(2,1)S(1)}, s32[2,256]{1,0:T(2,128)S(1)}, f32[256,1024]{1,0:T(8,128)S(1)}...) custom-call(s32[4]{0:T(128)S(1)} %copy-done.2, bf16[4,256,128]{2,1,0:T(8,128)(2,1)S(1)} %copy-done, ...), custom_call_target="tpu_custom_call" | custom-call | flops 1048576 | bytes 1024 | tf_op jit(solution)/shard_map/own_unit/pallas_call | solution.py:284
  8.6 0.3 collective-permute-done.four_ref
  9.0 1.0 %four_units.1 = (f32[256,1024]{1,0:T(8,128)S(1)}, f32[256,1024]{1,0:T(8,128)S(1)}, f32[3,1024]{1,0:T(4,128)S(1)}, f32[256,1024]{1,0:T(8,128)S(1)}, f32[256,1024]{1,0:T(8,128)S(1)}, /*index=5*/f32[3,1024]{1,0:T(4,128)S(1)}) custom-call(s32[2,256]{1,0:T(2,128)S(1)} %get-tuple-element.52.starts_ref, bf16[4,256,128]{2,1,0:T(8,128)(2,1)S(1)} %get-tuple-element.53.q_ref, ...), custom_call_target="tpu_custom_call" | custom-call | flops 1048576 | bytes 1024 | tf_op jit(solution)/shard_map/four_units/pallas_call | solution.py:291
  10.0 1.6 %collective-permute-done.4 = bf16[256,256]{1,0:T(8,128)(2,1)S(1)} collective-permute-done((bf16[256,256]{1,0:T(8,128)(2,1)S(1)}, bf16[256,256]{1,0:T(8,128)(2,1)S(1)}, u32[]{:S(2)}, u32[]{:S(2)}) %collective-permute-start.4) | collective-permute-done | bytes 131104 | tf_op jit(solution)/shard_map/ppermute | solution.py:49
  11.6 1.4 %collective-permute-done.3 = bf16[256,256]{1,0:T(8,128)(2,1)S(1)} collective-permute-done((bf16[256,256]{1,0:T(8,128)(2,1)S(1)}, bf16[256,256]{1,0:T(8,128)(2,1)S(1)}, u32[]{:S(2)}, u32[]{:S(2)}) %collective-permute-start.3) | collective-permute-done | bytes 131104 | tf_op jit(solution)/shard_map/ppermute | solution.py:49
  13.0 1.1 %two_units.1 = (f32[256,1024]{1,0:T(8,128)S(1)}, f32[256,1024]{1,0:T(8,128)S(1)}, f32[3,1024]{1,0:T(4,128)S(1)}, f32[256,1024]{1,0:T(8,128)S(1)}, f32[256,1024]{...) custom-call(s32[2,256]{1,0:T(2,128)S(1)} %get-tuple-element.52.starts_ref, ...), custom_call_target="tpu_custom_call" | custom-call | flops 1048576 | bytes 1024 | tf_op jit(solution)/shard_map/two_units/pallas_call | solution.py:296
  14.1 0.1 collective-permute-start.5
  14.2 1.2 %collective-permute-done.5.taken_ref = f32[8,1024]{1,0:T(8,128)S(1)} collective-permute-done((f32[8,1024]{1,0:T(8,128)S(1)}, f32[8,1024]{1,0:T(8,128)S(1)}, u32[]{:S(2)}, u32[]{:S(2)}) %collective-permute-start.5) | collective-permute-done | bytes 32800 | tf_op jit(solution)/shard_map/ppermute | solution.py:49
  15.4 0.8 %four_terms.1 = (f32[8,1024]{1,0:T(8,128)S(1)}, bf16[256,256]{1,0:T(8,128)(2,1)S(1)}, bf16[256,1024]{1,0:T(8,128)(2,1)S(1)}, bf16[256,1024]{1,0:T(8,128)(2,1)S(1)}, bf16[256,1024]{1,0:T(8,128)(2,1)S(1)}) custom-call(f32[8,1024]{1,0:T(8,128)S(1)} %get-tuple-element.62.given_ref, f32[8,1024]{1,0:T(8,128)S(1)} %collective-permute-done.5.taken_ref, ...), custom_call_target="tpu_custom_call" | custom-call | flops 1048576 | bytes 1024 | tf_op jit(solution)/shard_map/four_terms/pallas_call | solution.py:301
  16.2 1.7 %collective-permute-start.6 = (bf16[256,256]{1,0:T(8,128)(2,1)S(1)}, bf16[256,256]{1,0:T(8,128)(2,1)S(1)}, u32[]{:S(2)}, u32[]{:S(2)}) collective-permute-start(bf16[256,256]{1,0:T(8,128)(2,1)S(1)} %get-tuple-element.82), channel_id=1, source_target_pairs={{0,16},{4,20},{8,24},{12,28},{16,0},{20,4},{24,8},{28,12},{1,17},{... | collective-permute-start | bytes 393224 | tf_op jit(solution)/shard_map/ppermute | solution.py:49
  17.9 0.8 %two_terms.1 = (bf16[256,256]{1,0:T(8,128)(2,1)S(1)}, bf16[256,1024]{1,0:T(8,128)(2,1)S(1)}, bf16[256,1024]{1,0:T(8,128)(2,1)S(1)}) custom-call(f32[8,1024]{1,0:T(8,128)S(1)} %get-tuple-element.69.coef_ref, f32[256,1024]{1,0:T(8,128)S(1)} %get-tuple-element.74.e_two, f32[256,1024]{1,0:T(8,128)S(1)} %get-tuple-element.75.dp_two, ...), custom_call_target="tpu_custom_call" | custom-call | flops 1048576 | bytes 1024 | tf_op jit(solution)/shard_map/two_terms/pallas_call | solution.py:307
  18.7 1.6 %collective-permute-start.8 = (bf16[256,256]{1,0:T(8,128)(2,1)S(1)}, bf16[256,256]{1,0:T(8,128)(2,1)S(1)}, u32[]{:S(2)}, u32[]{:S(2)}) collective-permute-start(bf16[256,256]{1,0:T(8,128)(2,1)S(1)} %get-tuple-element.83), channel_id=1, source_target_pairs={{0,8},{4,12},{8,0},{12,4},{16,24},{20,28},{24,16},{28,20},{1,9},{5... | collective-permute-start | bytes 393224 | tf_op jit(solution)/shard_map/ppermute | solution.py:49
  20.3 0.3 collective-permute-start.7
  20.6 1.6 %own_terms.1 = (f32[256,256]{1,0:T(8,128)S(1)}, f32[4,256,128]{2,1,0:T(8,128)S(1)}, bf16[4,256,128]{2,1,0:T(8,128)(2,1)S(1)}) custom-call(f32[8,1024]{1,0:T(8,128)S(1)} %get-tuple-element.69.coef_ref, f32[256,1024]{1,0:T(8,128)S(1)} %get-tuple-element.70.e_own, f32[256,1024]{1,0:T(8,128)S(1)} %get-tuple-element.71.dp_own, ...), custom_call_target="tpu_custom_call" | custom-call | flops 1048576 | bytes 1024 | tf_op jit(solution)/shard_map/own_terms/pallas_call | solution.py:318
  22.2 0.1 collective-permute-done.6.back
  22.3 2.8 %collective-permute-done.8.refs_1_ = bf16[256,256]{1,0:T(8,128)(2,1)S(1)} collective-permute-done((bf16[256,256]{1,0:T(8,128)(2,1)S(1)}, bf16[256,256]{1,0:T(8,128)(2,1)S(1)}, u32[]{:S(2)}, u32[]{:S(2)}) %collective-permute-start.8) | collective-permute-done | bytes 131104 | tf_op jit(solution)/shard_map/ppermute | solution.py:49
  25.1 2.0 %collective-permute-done.7.refs_0_ = bf16[256,256]{1,0:T(8,128)(2,1)S(1)} collective-permute-done((bf16[256,256]{1,0:T(8,128)(2,1)S(1)}, bf16[256,256]{1,0:T(8,128)(2,1)S(1)}, u32[]{:S(2)}, u32[]{:S(2)}) %collective-permute-start.7) | collective-permute-done | bytes 131104 | tf_op jit(solution)/shard_map/ppermute | solution.py:49
  27.1 0.1 sums.1
  27.1 0.1 collective-permute-start.12
  27.2 3.8 %collective-permute-start.9 = (bf16[64,256]{1,0:T(8,128)(2,1)S(1)}, bf16[64,256]{1,0:T(8,128)(2,1)S(1)}, u32[]{:S(2)}, u32[]{:S(2)}) collective-permute-start(bf16[64,256]{1,0:T(8,128)(2,1)S(1)} %get-tuple-element.84), channel_id=1, source_target_pairs={{0,3},{1,2},{2,1},{3,0},{4,7},{5,6},{6,5},{7,4},{8,11},{9,10},{10,... | collective-permute-start | bytes 98312 | tf_op jit(solution)/shard_map/ppermute | solution.py:49
  31.0 0.6 %collective-permute-start.11 = (bf16[64,256]{1,0:T(8,128)(2,1)S(1)}, bf16[64,256]{1,0:T(8,128)(2,1)S(1)}, u32[]{:S(2)}, u32[]{:S(2)}) collective-permute-start(bf16[64,256]{1,0:T(8,128)(2,1)S(1)} %get-tuple-element.86), channel_id=1, source_target_pairs={{0,1},{1,0},{2,3},{3,2},{4,5},{5,4},{6,7},{7,6},{8,9},{9,8},{10,11... | collective-permute-start | bytes 98312 | tf_op jit(solution)/shard_map/ppermute | solution.py:49
  31.7 0.7 %add_grads.1 = bf16[4,256,128]{2,1,0:T(8,128)(2,1)} custom-call(f32[4,256,128]{2,1,0:T(8,128)S(1)} %get-tuple-element.90.mine_ref, bf16[4,256,128]{2,1,0:T(8,128)(2,1)S(1)} %collective-permute-done.12.taken_ref), custom_call_target="tpu_custom_call" | custom-call | flops 1048576 | bytes 1024 | tf_op jit(solution)/shard_map/add_grads/pallas_call | solution.py:336
  32.4 0.6 %collective-permute-done.9.refs_0_ = bf16[64,256]{1,0:T(8,128)(2,1)S(1)} collective-permute-done((bf16[64,256]{1,0:T(8,128)(2,1)S(1)}, bf16[64,256]{1,0:T(8,128)(2,1)S(1)}, u32[]{:S(2)}, u32[]{:S(2)}) %collective-permute-start.9) | collective-permute-done | bytes 32800 | tf_op jit(solution)/shard_map/ppermute | solution.py:49
  33.1 2.8 %collective-permute-done.10.refs_1_ = bf16[64,256]{1,0:T(8,128)(2,1)S(1)} collective-permute-done((bf16[64,256]{1,0:T(8,128)(2,1)S(1)}, bf16[64,256]{1,0:T(8,128)(2,1)S(1)}, u32[]{:S(2)}, u32[]{:S(2)}) %collective-permute-start.10) | collective-permute-done | bytes 32800 | tf_op jit(solution)/shard_map/ppermute | solution.py:49
  35.9 0.6 %last.1 = (bf16[2,64,128]{2,1,0:T(8,128)(2,1)}, bf16[2,64,128]{2,1,0:T(8,128)(2,1)}) custom-call(bf16[64,256]{1,0:T(8,128)(2,1)S(1)} %collective-permute-done.9.refs_0_, bf16[64,256]{1,0:T(8,128)(2,1)S(1)} %collective-permute-done.10.refs_1_, bf16[64,256]{1,0:T(8,128)(2,1)S(1)} %collective-permute-done.11.refs_2_, f32[64,256]{1,0:T(8,128)S(1)} %get-tuple-element.96.refs_3_), custom_call_target="tpu_custom_call" | custom-call | flops 1048576 | bytes 1024 | tf_op jit(solution)/shard_map/last/pallas_call | solution.py:344
  (13 shorter events, 0.1 us)
Async XLA Ops:
  0.6 8.3 %collective-permute-start.1 = (bf16[4,256,128]{2,1,0:T(8,128)(2,1)}, bf16[4,256,128]{2,1,0:T(8,128)(2,1)S(1)}, u32[]{:S(2)}, u32[]{:S(2)}) collective-permute-start(bf16[4,256,128]{2,1,0:T(8,128)(2,1)} %q_in.1), channel_id=1, source_target_pairs={{0,4},{4,0},{8,12},{12,8},{16,20},{20,16},{24,28},{28,24},{1,5},{5... | collective-permute-start | bytes 786440 | tf_op jit(solution)/shard_map/ppermute | solution.py:49
  1.1 7.8 %collective-permute-start.2 = (bf16[4,256,128]{2,1,0:T(8,128)(2,1)}, bf16[4,256,128]{2,1,0:T(8,128)(2,1)S(1)}, u32[]{:S(2)}, u32[]{:S(2)}) collective-permute-start(bf16[4,256,128]{2,1,0:T(8,128)(2,1)} %g_in.1), channel_id=1, source_target_pairs={{0,4},{4,0},{8,12},{12,8},{16,20},{20,16},{24,28},{28,24},{1,5},{5... | collective-permute-start | bytes 786440 | tf_op jit(solution)/shard_map/ppermute | solution.py:49
  1.2 5.5 %copy-start = (bf16[4,256,128]{2,1,0:T(8,128)(2,1)S(1)}, bf16[4,256,128]{2,1,0:T(8,128)(2,1)}, u32[]{:S(2)}) copy-start(bf16[4,256,128]{2,1,0:T(8,128)(2,1)} %q_in.1) | copy-start | bytes 786436
  1.2 5.5 %copy-start.1 = (bf16[4,256,128]{2,1,0:T(8,128)(2,1)S(1)}, bf16[4,256,128]{2,1,0:T(8,128)(2,1)}, u32[]{:S(2)}) copy-start(bf16[4,256,128]{2,1,0:T(8,128)(2,1)} %g_in.1) | copy-start | bytes 786436
  2.2 6.8 %collective-permute-start = (bf16[256,256]{1,0:T(8,128)(2,1)S(1)}, bf16[256,256]{1,0:T(8,128)(2,1)S(1)}, u32[]{:S(2)}, u32[]{:S(2)}) collective-permute-start(bf16[256,256]{1,0:T(8,128)(2,1)S(1)} %pad_maximum_fusion.own_ref), channel_id=1, source_target_pairs={{0,16},{4,20},{8,24},{12,28},{16,0},{20,4},{24,8},{28,12},{1,17},{... | collective-permute-start | bytes 393224 | tf_op jit(solution)/shard_map/ppermute | solution.py:49
  5.2 6.4 %collective-permute-start.4 = (bf16[256,256]{1,0:T(8,128)(2,1)S(1)}, bf16[256,256]{1,0:T(8,128)(2,1)S(1)}, u32[]{:S(2)}, u32[]{:S(2)}) collective-permute-start(bf16[256,256]{1,0:T(8,128)(2,1)S(1)} %pad_maximum_fusion.own_ref), channel_id=1, source_target_pairs={{0,8},{4,12},{8,0},{12,4},{16,24},{20,28},{24,16},{28,20},{1,9},{5... | collective-permute-start | bytes 393224 | tf_op jit(solution)/shard_map/ppermute | solution.py:49
  6.7 6.3 %collective-permute-start.3 = (bf16[256,256]{1,0:T(8,128)(2,1)S(1)}, bf16[256,256]{1,0:T(8,128)(2,1)S(1)}, u32[]{:S(2)}, u32[]{:S(2)}) collective-permute-start(bf16[256,256]{1,0:T(8,128)(2,1)S(1)} %pad_maximum_fusion.own_ref), channel_id=1, source_target_pairs={{0,24},{4,28},{8,16},{12,20},{16,8},{20,12},{24,0},{28,4},{1,25},{... | collective-permute-start | bytes 393224 | tf_op jit(solution)/shard_map/ppermute | solution.py:49
  6.8 0.7 %copy-start.2 = (s32[4]{0:T(128)S(1)}, s32[4]{0:T(128)}, u32[]{:S(2)}) copy-start(s32[4]{0:T(128)} %lengths_ref.1) | copy-start | bytes 52
  14.1 1.3 %collective-permute-start.5 = (f32[8,1024]{1,0:T(8,128)S(1)}, f32[8,1024]{1,0:T(8,128)S(1)}, u32[]{:S(2)}, u32[]{:S(2)}) collective-permute-start(f32[8,1024]{1,0:T(8,128)S(1)} %get-tuple-element.62.given_ref), channel_id=1, source_target_pairs={{0,4},{4,0},{8,12},{12,8},{16,20},{20,16},{24,28},{28,24},{1,5},{5... | collective-permute-start | bytes 98312 | tf_op jit(solution)/shard_map/ppermute | solution.py:49
  16.2 6.1 %collective-permute-start.6 = (bf16[256,256]{1,0:T(8,128)(2,1)S(1)}, bf16[256,256]{1,0:T(8,128)(2,1)S(1)}, u32[]{:S(2)}, u32[]{:S(2)}) collective-permute-start(bf16[256,256]{1,0:T(8,128)(2,1)S(1)} %get-tuple-element.82), channel_id=1, source_target_pairs={{0,16},{4,20},{8,24},{12,28},{16,0},{20,4},{24,8},{28,12},{1,17},{... | collective-permute-start | bytes 393224 | tf_op jit(solution)/shard_map/ppermute | solution.py:49
  18.7 6.4 %collective-permute-start.8 = (bf16[256,256]{1,0:T(8,128)(2,1)S(1)}, bf16[256,256]{1,0:T(8,128)(2,1)S(1)}, u32[]{:S(2)}, u32[]{:S(2)}) collective-permute-start(bf16[256,256]{1,0:T(8,128)(2,1)S(1)} %get-tuple-element.83), channel_id=1, source_target_pairs={{0,8},{4,12},{8,0},{12,4},{16,24},{20,28},{24,16},{28,20},{1,9},{5... | collective-permute-start | bytes 393224 | tf_op jit(solution)/shard_map/ppermute | solution.py:49
  20.3 6.8 %collective-permute-start.7 = (bf16[256,256]{1,0:T(8,128)(2,1)S(1)}, bf16[256,256]{1,0:T(8,128)(2,1)S(1)}, u32[]{:S(2)}, u32[]{:S(2)}) collective-permute-start(bf16[256,256]{1,0:T(8,128)(2,1)S(1)} %get-tuple-element.83), channel_id=1, source_target_pairs={{0,24},{4,28},{8,16},{12,20},{16,8},{20,12},{24,0},{28,4},{1,25},{... | collective-permute-start | bytes 393224 | tf_op jit(solution)/shard_map/ppermute | solution.py:49
  27.1 4.5 %collective-permute-start.12 = (bf16[4,256,128]{2,1,0:T(8,128)(2,1)S(1)}, bf16[4,256,128]{2,1,0:T(8,128)(2,1)S(1)}, u32[]{:S(2)}, u32[]{:S(2)}) collective-permute-start(bf16[4,256,128]{2,1,0:T(8,128)(2,1)S(1)} %get-tuple-element.91), channel_id=1, source_target_pairs={{0,4},{4,0},{8,12},{12,8},{16,20},{20,16},{24,28},{28,24},{1,5},{5... | collective-permute-start | bytes 786440 | tf_op jit(solution)/shard_map/ppermute | solution.py:49
  27.2 5.8 %collective-permute-start.9 = (bf16[64,256]{1,0:T(8,128)(2,1)S(1)}, bf16[64,256]{1,0:T(8,128)(2,1)S(1)}, u32[]{:S(2)}, u32[]{:S(2)}) collective-permute-start(bf16[64,256]{1,0:T(8,128)(2,1)S(1)} %get-tuple-element.84), channel_id=1, source_target_pairs={{0,3},{1,2},{2,1},{3,0},{4,7},{5,6},{6,5},{7,4},{8,11},{9,10},{10,... | collective-permute-start | bytes 98312 | tf_op jit(solution)/shard_map/ppermute | solution.py:49
  31.0 4.8 %collective-permute-start.10 = (bf16[64,256]{1,0:T(8,128)(2,1)S(1)}, bf16[64,256]{1,0:T(8,128)(2,1)S(1)}, u32[]{:S(2)}, u32[]{:S(2)}) collective-permute-start(bf16[64,256]{1,0:T(8,128)(2,1)S(1)} %get-tuple-element.85), channel_id=1, source_target_pairs={{0,2},{1,3},{2,0},{3,1},{4,6},{5,7},{6,4},{7,5},{8,10},{9,11},{10,... | collective-permute-start | bytes 98312 | tf_op jit(solution)/shard_map/ppermute | solution.py:49
  31.0 4.8 %collective-permute-start.11 = (bf16[64,256]{1,0:T(8,128)(2,1)S(1)}, bf16[64,256]{1,0:T(8,128)(2,1)S(1)}, u32[]{:S(2)}, u32[]{:S(2)}) collective-permute-start(bf16[64,256]{1,0:T(8,128)(2,1)S(1)} %get-tuple-element.86), channel_id=1, source_target_pairs={{0,1},{1,0},{2,3},{3,2},{4,5},{5,4},{6,7},{7,6},{8,9},{9,8},{10,11... | collective-permute-start | bytes 98312 | tf_op jit(solution)/shard_map/ppermute | solution.py:49

commit v6 on v5

--- a/solution.py
+++ b/solution.py
@@ -107,13 +107,15 @@
     unit(own_ref, here, starts, q_in, g_in, e_ref, dp_ref, stats_ref, causal=True)
 
 
-def four_units_body(starts_ref, q_ref, g_ref, other_q, other_g, own_ref, four_ref,
-                    e_four, dp_four, stats_four, e_side, dp_side, stats_side):
+def four_unit_body(starts_ref, q_ref, g_ref, four_ref, e_ref, dp_ref, stats_ref):
     here = lax.axis_index("ctx")
-    unit(four_ref, here - 4, starts_ref[0:1], q_ref, g_ref, e_four, dp_four, stats_four)
+    unit(four_ref, here - 4, starts_ref[0:1], q_ref, g_ref, e_ref, dp_ref, stats_ref)
+
+
+def side_unit_body(starts_ref, other_q, other_g, own_ref, four_ref, e_ref, dp_ref, stats_ref):
     side = jnp.where(second_core(), four_ref[...], own_ref[...])
-    unit(side, here - jnp.where(second_core(), 4, 0), starts_ref[1:2], other_q, other_g,
-         e_side, dp_side, stats_side)
+    block = lax.axis_index("ctx") - jnp.where(second_core(), 4, 0)
+    unit(side, block, starts_ref[1:2], other_q, other_g, e_ref, dp_ref, stats_ref)
 
 
 def two_units_body(starts_ref, q_ref, g_ref, other_q, other_g, two_ref,
@@ -156,7 +158,7 @@
 def four_terms_body(given_ref, taken_ref, stats_own, stats_four, stats_two, stats_side,
                     stats_cross, e_four, dp_four, e_side, dp_side,
                     q_ref, g_ref, other_q, other_g,
-                    coef_ref, terms_ref, ds_four, ds_side, p_side, p_four, sum_ref):
+                    coef_ref, terms_ref, ds_four, ds_side, p_ref, sum_ref):
     factor = q_ref.shape[-1] ** -0.5 * math.log2(math.e)
     coefs = []
     for at, refs in ((0, (stats_own, stats_four, stats_two)), (3, (stats_side, stats_cross))):
@@ -167,13 +169,13 @@
         coefs.extend(jnp.exp2((ref[0:1] - top) * factor) * inverse for ref in refs)
     for row, value in enumerate(coefs):
         coef_ref[row:row + 1] = value
-    slopes(e_four, dp_four, coefs[2], coefs[0], p_four, ds_four)
-    slopes(e_side, dp_side, coefs[5], coefs[4], p_side, ds_side)
-    add_terms(sum_ref, ds_four, p_four, q_ref, g_ref, True)
+    slopes(e_four, dp_four, coefs[2], coefs[0], p_ref.at[0], ds_four)
+    add_terms(sum_ref, ds_four, p_ref.at[0], q_ref, g_ref, True)
 
     @pl.when(second_core())
     def _():
-        add_terms(sum_ref, ds_side, p_side, other_q, other_g, False)
+        slopes(e_side, dp_side, coef_ref[5:6], coef_ref[4:5], p_ref.at[1], ds_side)
+        add_terms(sum_ref, ds_side, p_ref.at[1], other_q, other_g, False)
 
     terms_ref[...] = sum_ref[...].astype(bf16)
 
@@ -196,11 +198,12 @@
         out_ref[h] = (dqt.T * width ** -0.5).astype(out_ref.dtype)
 
 
-def own_terms_body(coef_ref, e_own, dp_own, q_ref, g_ref, other_q, other_g, ds_side, p_side,
+def own_terms_body(coef_ref, e_own, dp_own, e_side, dp_side, q_ref, g_ref, other_q, other_g,
                    own_ref, two_ref, four_ref, ds_two, ds_four, ds_cross,
-                   terms_ref, dq_ref, other_dq_ref, ds_own, p_ref):
+                   terms_ref, dq_ref, other_dq_ref, ds_own, ds_side, p_ref, p_side):
     width = q_ref.shape[-1]
     own, two, four = [ref[:, :width] for ref in (own_ref, two_ref, four_ref)]
+    slopes(e_side, dp_side, coef_ref[5:6], coef_ref[4:5], p_side, ds_side)
     query_grads([jnp.where(second_core(), four, own), two], [ds_side, ds_cross], other_dq_ref)
     slopes(e_own, dp_own, coef_ref[1:2], coef_ref[0:1], p_ref, ds_own)
     add_terms(terms_ref, ds_own, p_ref, q_ref, g_ref, True)
@@ -278,7 +281,7 @@
          lax.dynamic_index_in_dim(values, group, 0, keepdims=False)], axis=1)
     four = exchanged(own, "ctx", 4) if mutual else shifted(own, 4)
     if mutual:
-        two = (exchanged(own, "ctx", 6), exchanged(own, "ctx", 2))
+        two = (exchanged(own, "ctx", 2), exchanged(own, "ctx", 6))
     else:
         two = (shifted(own, 2),)
     q, g, starts, e_own, dp_own, stats_own = call(
@@ -288,20 +291,23 @@
     other_q = exchanged(queries, "ctx", 1)
     other_g = exchanged(d_out, "ctx", 1)
     four, starts = lax.optimization_barrier((four, starts))
-    e_four, dp_four, stats_four, e_side, dp_side, stats_side = call(
-        four_units_body, "four_units", [VMEM] * 7, (wide, wide, stats) * 2,
-    )(starts, q, g, other_q, other_g, own, four)
-    *two, stats_four = lax.optimization_barrier((*two, stats_four))
-    two = jnp.where(ctx & 2 == 2, two[1], two[0]) if mutual else two[0]
+    e_four, dp_four, stats_four = call(
+        four_unit_body, "four_unit", [VMEM] * 4, (wide, wide, stats))(starts, q, g, four)
+    other_q, stats_four = lax.optimization_barrier((other_q, stats_four))
+    e_side, dp_side, stats_side = call(
+        side_unit_body, "side_unit", [VMEM] * 5, (wide, wide, stats),
+    )(starts, other_q, other_g, own, four)
+    *two, stats_side = lax.optimization_barrier((*two, stats_side))
+    two = jnp.where(ctx & 2 == 2, *two) if mutual else two[0]
     e_two, dp_two, stats_two, e_cross, dp_cross, stats_cross, given = call(
         two_units_body, "two_units", [VMEM] * 9,
         (wide, wide, stats) * 2 + (shape((8, rows), f32),),
     )(starts, q, g, other_q, other_g, two, stats_own, stats_four, stats_side)
     taken = exchanged(given, "ctx", 1)
-    coef, four_terms, ds_four, ds_side, p_side = call(
+    coef, four_terms, ds_four = call(
         four_terms_body, "four_terms", [VMEM] * 15,
-        (shape((8, rows), f32), shape(pair, bf16), half, half, half),
-        (half_scratch, pair_scratch),
+        (shape((8, rows), f32), shape(pair, bf16), half),
+        (half_scratch, pltpu.VMEM((2, tokens, rows), bf16), pair_scratch),
     )(given, taken, stats_own, stats_four, stats_two, stats_side, stats_cross,
       e_four, dp_four, e_side, dp_side, q, g, other_q, other_g)
     two_terms, ds_two, ds_cross = call(
@@ -309,17 +315,17 @@
         (pltpu.VMEM((2, tokens, rows), bf16), pair_scratch),
     )(coef, e_two, dp_two, e_cross, dp_cross, q, g, other_q, other_g)
     if mutual:
-        backs = [exchanged(four_terms, "ctx", 4), exchanged(two_terms, "ctx", 6),
-                 exchanged(two_terms, "ctx", 2)]
-        uses = [lambda i: i < 4, lambda i: i & 6 == 2, lambda i: i & 2 == 0]
+        backs = [exchanged(four_terms, "ctx", 4), exchanged(two_terms, "ctx", 2),
+                 exchanged(two_terms, "ctx", 6)]
+        uses = [lambda i: i < 4, lambda i: i & 2 == 0, lambda i: i & 6 == 2]
     else:
         backs = [shifted(four_terms, -4), shifted(two_terms, -2)]
         uses = [lambda i: True] * 2
     own_terms, my_grads, other_grads = call(
         own_terms_body, "own_terms", [VMEM] * 15,
         (shape(pair, f32), shape(all_rows, f32), shape(all_rows, bf16)),
-        (half_scratch, half_scratch),
-    )(coef, e_own, dp_own, q, g, other_q, other_g, ds_side, p_side, own, two, four,
+        (half_scratch,) * 4,
+    )(coef, e_own, dp_own, e_side, dp_side, q, g, other_q, other_g, own, two, four,
       ds_two, ds_four, ds_cross)
     own_terms, = call(
         functools.partial(first_sum_body, uses[0]), "first_sum", [VMEM] * 2,

time: 36.7 us -> 36.5 us (level)
    pallas_call x1 -> x2, Pallas kernels: 1.04 us -> 1.16 us  [the longest x1 0.59 us: per_device(): call(side_unit_body, 'side_unit', [VMEM] * 5, (wide, wide, stats))]
where the time goes in v6:
time: 36.5 us; the launch traced here: 36.4 us
  starting transfers between devices  13.4 us (37%)
  waiting for transfers between devices  12.7 us (35%)
  Pallas kernels  7.9 us (22%)
  local copies, waits for them, and re-layouts  1.6 us (4%)
  between operations  0.74 us (2%)
    ppermute x13, starting transfers between devices, exchanged(): lax.ppermute(block, axis, [(i, i ^ mask) for i in range(lax.axis_size(axi...  13.4 us
    ppermute x13, waiting for transfers between devices, exchanged(): lax.ppermute(block, axis, [(i, i ^ mask) for i in range(lax.axis_size(axi...  12.7 us
    pallas_call x1, Pallas kernels, per_device(): call(own_terms_body, 'own_terms', [VMEM] * 15, (shape(pair, f32), shape(a...  1.66 us
    pallas_call x1, Pallas kernels, per_device(): call(own_unit_body, 'own_unit', [SMEM] + [VMEM] * 3, (shape(all_rows, bf1...  1.2 us
    pallas_call x1, Pallas kernels, per_device(): call(two_units_body, 'two_units', [VMEM] * 9, (wide, wide, stats) * 2 + (...  1.06 us
    squeeze x1, local copies, waits for them, and re-layouts, per_device(): lax.dynamic_index_in_dim(values, group, 0, keepdims=False)  0.94 us
    pallas_call x1, Pallas kernels, per_device(): call(two_terms_body, 'two_terms', [VMEM] * 9, (shape(pair, bf16), half, h...  0.82 us
    pallas_call x1, Pallas kernels, per_device(): call(add_grads_body, 'add_grads', [VMEM] * 2, (shape(all_rows, bf16),))  0.75 us
  transfers between devices with their start and end apart: 13, of which 9 were waited for; matrix products, arithmetic and copies ran while one was open for 3% of the time, Pallas kernels for 15%

profile of v6, /device:TPU:0, one launch (start us, length us, event | category | flops | bytes accessed | tf_op | source)
XLA Modules:
  0.0 36.4 jit_solution(3173444892403187277)
XLA Ops:
  0.6 0.5 %collective-permute-start.1 = (bf16[4,256,128]{2,1,0:T(8,128)(2,1)}, bf16[4,256,128]{2,1,0:T(8,128)(2,1)S(1)}, u32[]{:S(2)}, u32[]{:S(2)}) collective-permute-start(bf16[4,256,128]{2,1,0:T(8,128)(2,1)} %q_in.1), channel_id=1, source_target_pairs={{0,4},{4,0},{8,12},{12,8},{16,20},{20,16},{24,28},{28,24},{1,5},{5... | collective-permute-start | bytes 786440 | tf_op jit(solution)/shard_map/ppermute | solution.py:49
  1.1 0.1 collective-permute-start.2
  1.2 0.9 %dynamic-slice_bitcast_fusion = (bf16[256,128]{1,0:T(8,128)(2,1)S(1)}, bf16[256,128]{1,0:T(8,128)(2,1)S(1)}) fusion(bf16[2,256,128]{2,1,0:T(8,128)(2,1)} %param.7, s32[]{:T(128)S(6)} %select_n.19, bf16[2,256,128]{2,1,0:T(8,128)(2,1)} %param.6), kind=kLoop, calls=%fused_computation.2 | loop fusion | bytes 262148 | tf_op jit(solution)/shard_map/jit(dynamic_index_in_dim)/squeeze | solution.py:281
  2.2 3.0 %collective-permute-start = (bf16[256,256]{1,0:T(8,128)(2,1)S(1)}, bf16[256,256]{1,0:T(8,128)(2,1)S(1)}, u32[]{:S(2)}, u32[]{:S(2)}) collective-permute-start(bf16[256,256]{1,0:T(8,128)(2,1)S(1)} %pad_maximum_fusion.own_ref), channel_id=1, source_target_pairs={{0,16},{4,20},{8,24},{12,28},{16,0},{20,4},{24,8},{28,12},{1,17},{... | collective-permute-start | bytes 393224 | tf_op jit(solution)/shard_map/ppermute | solution.py:49
  5.2 1.4 %collective-permute-start.4 = (bf16[256,256]{1,0:T(8,128)(2,1)S(1)}, bf16[256,256]{1,0:T(8,128)(2,1)S(1)}, u32[]{:S(2)}, u32[]{:S(2)}) collective-permute-start(bf16[256,256]{1,0:T(8,128)(2,1)S(1)} %pad_maximum_fusion.own_ref), channel_id=1, source_target_pairs={{0,24},{4,28},{8,16},{12,20},{16,8},{20,12},{24,0},{28,4},{1,25},{... | collective-permute-start | bytes 393224 | tf_op jit(solution)/shard_map/ppermute | solution.py:49
  6.6 0.1 collective-permute-start.3
  6.8 0.6 %copy-done.2 = s32[4]{0:T(128)S(1)} copy-done((s32[4]{0:T(128)S(1)}, s32[4]{0:T(128)}, u32[]{:S(2)}) %copy-start.2) | copy-done | bytes 40
  7.4 1.2 %own_unit.1 = (bf16[4,256,128]{2,1,0:T(8,128)(2,1)S(1)}, bf16[4,256,128]{2,1,0:T(8,128)(2,1)S(1)}, s32[2,256]{1,0:T(2,128)S(1)}, f32[256,1024]{1,0:T(8,128)S(1)}...) custom-call(s32[4]{0:T(128)S(1)} %copy-done.2, bf16[4,256,128]{2,1,0:T(8,128)(2,1)S(1)} %copy-done, ...), custom_call_target="tpu_custom_call" | custom-call | flops 1048576 | bytes 1024 | tf_op jit(solution)/shard_map/own_unit/pallas_call | solution.py:287
  8.6 2.4 %collective-permute-done.four_ref = bf16[256,256]{1,0:T(8,128)(2,1)S(1)} collective-permute-done((bf16[256,256]{1,0:T(8,128)(2,1)S(1)}, bf16[256,256]{1,0:T(8,128)(2,1)S(1)}, u32[]{:S(2)}, u32[]{:S(2)}) %collective-permute-start) | collective-permute-done | bytes 131104 | tf_op jit(solution)/shard_map/ppermute | solution.py:49
  11.0 0.6 %four_unit.1 = (f32[256,1024]{1,0:T(8,128)S(1)}, f32[256,1024]{1,0:T(8,128)S(1)}, f32[3,1024]{1,0:T(4,128)S(1)}) custom-call(s32[2,256]{1,0:T(2,128)S(1)} %get-tuple-element.52.starts_ref, bf16[4,256,128]{2,1,0:T(8,128)(2,1)S(1)} %get-tuple-element.53.q_ref, bf16[4,256,128]{2,1,0:T(8,128)(2,1)S(1)} %get-tuple-element.54.g_ref, ...), custom_call_target="tpu_custom_call" | custom-call | flops 1048576 | bytes 1024 | tf_op jit(solution)/shard_map/four_unit/pallas_call | solution.py:294
  11.6 0.6 %side_unit.1 = (f32[256,1024]{1,0:T(8,128)S(1)}, f32[256,1024]{1,0:T(8,128)S(1)}, f32[3,1024]{1,0:T(4,128)S(1)}) custom-call(s32[2,256]{1,0:T(2,128)S(1)} %get-tuple-element.52.starts_ref, bf16[4,256,128]{2,1,0:T(8,128)(2,1)S(1)} %collective-permute-done.1.other_q, bf16[4,256,128]{2,1,0:T(8,128)(2,1)S(1)} %collective-permute-done.2.other_g, ...), custom_call_target="tpu_custom_call" | custom-call | flops 1048576 | bytes 1024 | tf_op jit(solution)/shard_map/side_unit/pallas_call | solution.py:297
  12.2 0.3 collective-permute-done.4
  12.5 0.6 %collective-permute-done.3 = bf16[256,256]{1,0:T(8,128)(2,1)S(1)} collective-permute-done((bf16[256,256]{1,0:T(8,128)(2,1)S(1)}, bf16[256,256]{1,0:T(8,128)(2,1)S(1)}, u32[]{:S(2)}, u32[]{:S(2)}) %collective-permute-start.3) | collective-permute-done | bytes 131104 | tf_op jit(solution)/shard_map/ppermute | solution.py:49
  13.1 1.1 %two_units.1 = (f32[256,1024]{1,0:T(8,128)S(1)}, f32[256,1024]{1,0:T(8,128)S(1)}, f32[3,1024]{1,0:T(4,128)S(1)}, f32[256,1024]{1,0:T(8,128)S(1)}, f32[256,1024]{...) custom-call(s32[2,256]{1,0:T(2,128)S(1)} %get-tuple-element.52.starts_ref, ...), custom_call_target="tpu_custom_call" | custom-call | flops 1048576 | bytes 1024 | tf_op jit(solution)/shard_map/two_units/pallas_call | solution.py:302
  14.1 0.1 collective-permute-start.5
  14.2 1.2 %collective-permute-done.5.taken_ref = f32[8,1024]{1,0:T(8,128)S(1)} collective-permute-done((f32[8,1024]{1,0:T(8,128)S(1)}, f32[8,1024]{1,0:T(8,128)S(1)}, u32[]{:S(2)}, u32[]{:S(2)}) %collective-permute-start.5) | collective-permute-done | bytes 32800 | tf_op jit(solution)/shard_map/ppermute | solution.py:49
  15.4 0.5 %four_terms.1 = (f32[8,1024]{1,0:T(8,128)S(1)}, bf16[256,256]{1,0:T(8,128)(2,1)S(1)}, bf16[256,1024]{1,0:T(8,128)(2,1)S(1)}) custom-call(f32[8,1024]{1,0:T(8,128)S(1)} %get-tuple-element.64.given_ref, f32[8,1024]{1,0:T(8,128)S(1)} %collective-permute-done.5.taken_ref, f32[3,1024]{1,0:T(4,128)S(1)} %get-tuple-element.61.stats_own, ...), custom_call_target="tpu_custom_call" | custom-call | flops 1048576 | bytes 1024 | tf_op jit(solution)/shard_map/four_terms/pallas_call | solution.py:307
  15.9 1.7 %collective-permute-start.6 = (bf16[256,256]{1,0:T(8,128)(2,1)S(1)}, bf16[256,256]{1,0:T(8,128)(2,1)S(1)}, u32[]{:S(2)}, u32[]{:S(2)}) collective-permute-start(bf16[256,256]{1,0:T(8,128)(2,1)S(1)} %get-tuple-element.82), channel_id=1, source_target_pairs={{0,16},{4,20},{8,24},{12,28},{16,0},{20,4},{24,8},{28,12},{1,17},{... | collective-permute-start | bytes 393224 | tf_op jit(solution)/shard_map/ppermute | solution.py:49
  17.7 0.8 %two_terms.1 = (bf16[256,256]{1,0:T(8,128)(2,1)S(1)}, bf16[256,1024]{1,0:T(8,128)(2,1)S(1)}, bf16[256,1024]{1,0:T(8,128)(2,1)S(1)}) custom-call(f32[8,1024]{1,0:T(8,128)S(1)} %get-tuple-element.71.coef_ref, f32[256,1024]{1,0:T(8,128)S(1)} %get-tuple-element.74.e_two, f32[256,1024]{1,0:T(8,128)S(1)} %get-tuple-element.75.dp_two, ...), custom_call_target="tpu_custom_call" | custom-call | flops 1048576 | bytes 1024 | tf_op jit(solution)/shard_map/two_terms/pallas_call | solution.py:313
  18.5 1.5 %collective-permute-start.8 = (bf16[256,256]{1,0:T(8,128)(2,1)S(1)}, bf16[256,256]{1,0:T(8,128)(2,1)S(1)}, u32[]{:S(2)}, u32[]{:S(2)}) collective-permute-start(bf16[256,256]{1,0:T(8,128)(2,1)S(1)} %get-tuple-element.83), channel_id=1, source_target_pairs={{0,24},{4,28},{8,16},{12,20},{16,8},{20,12},{24,0},{28,4},{1,25},{... | collective-permute-start | bytes 393224 | tf_op jit(solution)/shard_map/ppermute | solution.py:49
  20.0 0.4 %collective-permute-start.7 = (bf16[256,256]{1,0:T(8,128)(2,1)S(1)}, bf16[256,256]{1,0:T(8,128)(2,1)S(1)}, u32[]{:S(2)}, u32[]{:S(2)}) collective-permute-start(bf16[256,256]{1,0:T(8,128)(2,1)S(1)} %get-tuple-element.83), channel_id=1, source_target_pairs={{0,8},{4,12},{8,0},{12,4},{16,24},{20,28},{24,16},{28,20},{1,9},{5... | collective-permute-start | bytes 393224 | tf_op jit(solution)/shard_map/ppermute | solution.py:49
  20.4 1.7 %own_terms.1 = (f32[256,256]{1,0:T(8,128)S(1)}, f32[4,256,128]{2,1,0:T(8,128)S(1)}, bf16[4,256,128]{2,1,0:T(8,128)(2,1)S(1)}) custom-call(f32[8,1024]{1,0:T(8,128)S(1)} %get-tuple-element.71.coef_ref, f32[256,1024]{1,0:T(8,128)S(1)} %get-tuple-element.72.e_own, f32[256,1024]{1,0:T(8,128)S(1)} %get-tuple-element.73.dp_own, ...), custom_call_target="tpu_custom_call" | custom-call | flops 1048576 | bytes 1024 | tf_op jit(solution)/shard_map/own_terms/pallas_call | solution.py:324
  22.0 2.0 %collective-permute-done.6.back = bf16[256,256]{1,0:T(8,128)(2,1)S(1)} collective-permute-done((bf16[256,256]{1,0:T(8,128)(2,1)S(1)}, bf16[256,256]{1,0:T(8,128)(2,1)S(1)}, u32[]{:S(2)}, u32[]{:S(2)}) %collective-permute-start.6) | collective-permute-done | bytes 131104 | tf_op jit(solution)/shard_map/ppermute | solution.py:49
  24.1 1.7 %collective-permute-done.8.refs_1_ = bf16[256,256]{1,0:T(8,128)(2,1)S(1)} collective-permute-done((bf16[256,256]{1,0:T(8,128)(2,1)S(1)}, bf16[256,256]{1,0:T(8,128)(2,1)S(1)}, u32[]{:S(2)}, u32[]{:S(2)}) %collective-permute-start.8) | collective-permute-done | bytes 131104 | tf_op jit(solution)/shard_map/ppermute | solution.py:49
  25.8 1.2 %collective-permute-done.7.refs_0_ = bf16[256,256]{1,0:T(8,128)(2,1)S(1)} collective-permute-done((bf16[256,256]{1,0:T(8,128)(2,1)S(1)}, bf16[256,256]{1,0:T(8,128)(2,1)S(1)}, u32[]{:S(2)}, u32[]{:S(2)}) %collective-permute-start.7) | collective-permute-done | bytes 131104 | tf_op jit(solution)/shard_map/ppermute | solution.py:49
  27.0 0.1 collective-permute-start.12
  27.1 3.8 %collective-permute-start.9 = (bf16[64,256]{1,0:T(8,128)(2,1)S(1)}, bf16[64,256]{1,0:T(8,128)(2,1)S(1)}, u32[]{:S(2)}, u32[]{:S(2)}) collective-permute-start(bf16[64,256]{1,0:T(8,128)(2,1)S(1)} %get-tuple-element.84), channel_id=1, source_target_pairs={{0,3},{1,2},{2,1},{3,0},{4,7},{5,6},{6,5},{7,4},{8,11},{9,10},{10,... | collective-permute-start | bytes 98312 | tf_op jit(solution)/shard_map/ppermute | solution.py:49
  30.9 0.6 %collective-permute-start.11 = (bf16[64,256]{1,0:T(8,128)(2,1)S(1)}, bf16[64,256]{1,0:T(8,128)(2,1)S(1)}, u32[]{:S(2)}, u32[]{:S(2)}) collective-permute-start(bf16[64,256]{1,0:T(8,128)(2,1)S(1)} %get-tuple-element.86), channel_id=1, source_target_pairs={{0,1},{1,0},{2,3},{3,2},{4,5},{5,4},{6,7},{7,6},{8,9},{9,8},{10,11... | collective-permute-start | bytes 98312 | tf_op jit(solution)/shard_map/ppermute | solution.py:49
  31.5 0.7 %add_grads.1 = bf16[4,256,128]{2,1,0:T(8,128)(2,1)} custom-call(f32[4,256,128]{2,1,0:T(8,128)S(1)} %get-tuple-element.90.mine_ref, bf16[4,256,128]{2,1,0:T(8,128)(2,1)S(1)} %collective-permute-done.12.taken_ref), custom_call_target="tpu_custom_call" | custom-call | flops 1048576 | bytes 1024 | tf_op jit(solution)/shard_map/add_grads/pallas_call | solution.py:342
  32.3 0.6 %collective-permute-done.9.refs_0_ = bf16[64,256]{1,0:T(8,128)(2,1)S(1)} collective-permute-done((bf16[64,256]{1,0:T(8,128)(2,1)S(1)}, bf16[64,256]{1,0:T(8,128)(2,1)S(1)}, u32[]{:S(2)}, u32[]{:S(2)}) %collective-permute-start.9) | collective-permute-done | bytes 32800 | tf_op jit(solution)/shard_map/ppermute | solution.py:49
  32.9 2.8 %collective-permute-done.10.refs_1_ = bf16[64,256]{1,0:T(8,128)(2,1)S(1)} collective-permute-done((bf16[64,256]{1,0:T(8,128)(2,1)S(1)}, bf16[64,256]{1,0:T(8,128)(2,1)S(1)}, u32[]{:S(2)}, u32[]{:S(2)}) %collective-permute-start.10) | collective-permute-done | bytes 32800 | tf_op jit(solution)/shard_map/ppermute | solution.py:49
  35.7 0.6 %last.1 = (bf16[2,64,128]{2,1,0:T(8,128)(2,1)}, bf16[2,64,128]{2,1,0:T(8,128)(2,1)}) custom-call(bf16[64,256]{1,0:T(8,128)(2,1)S(1)} %collective-permute-done.9.refs_0_, bf16[64,256]{1,0:T(8,128)(2,1)S(1)} %collective-permute-done.10.refs_1_, bf16[64,256]{1,0:T(8,128)(2,1)S(1)} %collective-permute-done.11.refs_2_, f32[64,256]{1,0:T(8,128)S(1)} %get-tuple-element.96.refs_3_), custom_call_target="tpu_custom_call" | custom-call | flops 1048576 | bytes 1024 | tf_op jit(solution)/shard_map/last/pallas_call | solution.py:350
  (14 shorter events, 0.2 us)
Async XLA Ops:
  0.6 11.0 %collective-permute-start.1 = (bf16[4,256,128]{2,1,0:T(8,128)(2,1)}, bf16[4,256,128]{2,1,0:T(8,128)(2,1)S(1)}, u32[]{:S(2)}, u32[]{:S(2)}) collective-permute-start(bf16[4,256,128]{2,1,0:T(8,128)(2,1)} %q_in.1), channel_id=1, source_target_pairs={{0,4},{4,0},{8,12},{12,8},{16,20},{20,16},{24,28},{28,24},{1,5},{5... | collective-permute-start | bytes 786440 | tf_op jit(solution)/shard_map/ppermute | solution.py:49
  1.1 10.5 %collective-permute-start.2 = (bf16[4,256,128]{2,1,0:T(8,128)(2,1)}, bf16[4,256,128]{2,1,0:T(8,128)(2,1)S(1)}, u32[]{:S(2)}, u32[]{:S(2)}) collective-permute-start(bf16[4,256,128]{2,1,0:T(8,128)(2,1)} %g_in.1), channel_id=1, source_target_pairs={{0,4},{4,0},{8,12},{12,8},{16,20},{20,16},{24,28},{28,24},{1,5},{5... | collective-permute-start | bytes 786440 | tf_op jit(solution)/shard_map/ppermute | solution.py:49
  1.2 5.5 %copy-start = (bf16[4,256,128]{2,1,0:T(8,128)(2,1)S(1)}, bf16[4,256,128]{2,1,0:T(8,128)(2,1)}, u32[]{:S(2)}) copy-start(bf16[4,256,128]{2,1,0:T(8,128)(2,1)} %q_in.1) | copy-start | bytes 786436
  1.2 5.5 %copy-start.1 = (bf16[4,256,128]{2,1,0:T(8,128)(2,1)S(1)}, bf16[4,256,128]{2,1,0:T(8,128)(2,1)}, u32[]{:S(2)}) copy-start(bf16[4,256,128]{2,1,0:T(8,128)(2,1)} %g_in.1) | copy-start | bytes 786436
  2.2 8.8 %collective-permute-start = (bf16[256,256]{1,0:T(8,128)(2,1)S(1)}, bf16[256,256]{1,0:T(8,128)(2,1)S(1)}, u32[]{:S(2)}, u32[]{:S(2)}) collective-permute-start(bf16[256,256]{1,0:T(8,128)(2,1)S(1)} %pad_maximum_fusion.own_ref), channel_id=1, source_target_pairs={{0,16},{4,20},{8,24},{12,28},{16,0},{20,4},{24,8},{28,12},{1,17},{... | collective-permute-start | bytes 393224 | tf_op jit(solution)/shard_map/ppermute | solution.py:49
  5.2 7.3 %collective-permute-start.4 = (bf16[256,256]{1,0:T(8,128)(2,1)S(1)}, bf16[256,256]{1,0:T(8,128)(2,1)S(1)}, u32[]{:S(2)}, u32[]{:S(2)}) collective-permute-start(bf16[256,256]{1,0:T(8,128)(2,1)S(1)} %pad_maximum_fusion.own_ref), channel_id=1, source_target_pairs={{0,24},{4,28},{8,16},{12,20},{16,8},{20,12},{24,0},{28,4},{1,25},{... | collective-permute-start | bytes 393224 | tf_op jit(solution)/shard_map/ppermute | solution.py:49
  6.6 6.4 %collective-permute-start.3 = (bf16[256,256]{1,0:T(8,128)(2,1)S(1)}, bf16[256,256]{1,0:T(8,128)(2,1)S(1)}, u32[]{:S(2)}, u32[]{:S(2)}) collective-permute-start(bf16[256,256]{1,0:T(8,128)(2,1)S(1)} %pad_maximum_fusion.own_ref), channel_id=1, source_target_pairs={{0,8},{4,12},{8,0},{12,4},{16,24},{20,28},{24,16},{28,20},{1,9},{5... | collective-permute-start | bytes 393224 | tf_op jit(solution)/shard_map/ppermute | solution.py:49
  6.8 0.7 %copy-start.2 = (s32[4]{0:T(128)S(1)}, s32[4]{0:T(128)}, u32[]{:S(2)}) copy-start(s32[4]{0:T(128)} %lengths_ref.1) | copy-start | bytes 52
  14.1 1.3 %collective-permute-start.5 = (f32[8,1024]{1,0:T(8,128)S(1)}, f32[8,1024]{1,0:T(8,128)S(1)}, u32[]{:S(2)}, u32[]{:S(2)}) collective-permute-start(f32[8,1024]{1,0:T(8,128)S(1)} %get-tuple-element.64.given_ref), channel_id=1, source_target_pairs={{0,4},{4,0},{8,12},{12,8},{16,20},{20,16},{24,28},{28,24},{1,5},{5... | collective-permute-start | bytes 98312 | tf_op jit(solution)/shard_map/ppermute | solution.py:49
  15.9 8.1 %collective-permute-start.6 = (bf16[256,256]{1,0:T(8,128)(2,1)S(1)}, bf16[256,256]{1,0:T(8,128)(2,1)S(1)}, u32[]{:S(2)}, u32[]{:S(2)}) collective-permute-start(bf16[256,256]{1,0:T(8,128)(2,1)S(1)} %get-tuple-element.82), channel_id=1, source_target_pairs={{0,16},{4,20},{8,24},{12,28},{16,0},{20,4},{24,8},{28,12},{1,17},{... | collective-permute-start | bytes 393224 | tf_op jit(solution)/shard_map/ppermute | solution.py:49
  18.5 7.3 %collective-permute-start.8 = (bf16[256,256]{1,0:T(8,128)(2,1)S(1)}, bf16[256,256]{1,0:T(8,128)(2,1)S(1)}, u32[]{:S(2)}, u32[]{:S(2)}) collective-permute-start(bf16[256,256]{1,0:T(8,128)(2,1)S(1)} %get-tuple-element.83), channel_id=1, source_target_pairs={{0,24},{4,28},{8,16},{12,20},{16,8},{20,12},{24,0},{28,4},{1,25},{... | collective-permute-start | bytes 393224 | tf_op jit(solution)/shard_map/ppermute | solution.py:49
  20.0 6.9 %collective-permute-start.7 = (bf16[256,256]{1,0:T(8,128)(2,1)S(1)}, bf16[256,256]{1,0:T(8,128)(2,1)S(1)}, u32[]{:S(2)}, u32[]{:S(2)}) collective-permute-start(bf16[256,256]{1,0:T(8,128)(2,1)S(1)} %get-tuple-element.83), channel_id=1, source_target_pairs={{0,8},{4,12},{8,0},{12,4},{16,24},{20,28},{24,16},{28,20},{1,9},{5... | collective-permute-start | bytes 393224 | tf_op jit(solution)/shard_map/ppermute | solution.py:49
  27.0 4.5 %collective-permute-start.12 = (bf16[4,256,128]{2,1,0:T(8,128)(2,1)S(1)}, bf16[4,256,128]{2,1,0:T(8,128)(2,1)S(1)}, u32[]{:S(2)}, u32[]{:S(2)}) collective-permute-start(bf16[4,256,128]{2,1,0:T(8,128)(2,1)S(1)} %get-tuple-element.91), channel_id=1, source_target_pairs={{0,4},{4,0},{8,12},{12,8},{16,20},{20,16},{24,28},{28,24},{1,5},{5... | collective-permute-start | bytes 786440 | tf_op jit(solution)/shard_map/ppermute | solution.py:49
  27.1 5.8 %collective-permute-start.9 = (bf16[64,256]{1,0:T(8,128)(2,1)S(1)}, bf16[64,256]{1,0:T(8,128)(2,1)S(1)}, u32[]{:S(2)}, u32[]{:S(2)}) collective-permute-start(bf16[64,256]{1,0:T(8,128)(2,1)S(1)} %get-tuple-element.84), channel_id=1, source_target_pairs={{0,3},{1,2},{2,1},{3,0},{4,7},{5,6},{6,5},{7,4},{8,11},{9,10},{10,... | collective-permute-start | bytes 98312 | tf_op jit(solution)/shard_map/ppermute | solution.py:49
  30.9 4.8 %collective-permute-start.10 = (bf16[64,256]{1,0:T(8,128)(2,1)S(1)}, bf16[64,256]{1,0:T(8,128)(2,1)S(1)}, u32[]{:S(2)}, u32[]{:S(2)}) collective-permute-start(bf16[64,256]{1,0:T(8,128)(2,1)S(1)} %get-tuple-element.85), channel_id=1, source_target_pairs={{0,2},{1,3},{2,0},{3,1},{4,6},{5,7},{6,4},{7,5},{8,10},{9,11},{10,... | collective-permute-start | bytes 98312 | tf_op jit(solution)/shard_map/ppermute | solution.py:49
  30.9 4.8 %collective-permute-start.11 = (bf16[64,256]{1,0:T(8,128)(2,1)S(1)}, bf16[64,256]{1,0:T(8,128)(2,1)S(1)}, u32[]{:S(2)}, u32[]{:S(2)}) collective-permute-start(bf16[64,256]{1,0:T(8,128)(2,1)S(1)} %get-tuple-element.86), channel_id=1, source_target_pairs={{0,1},{1,0},{2,3},{3,2},{4,5},{5,4},{6,7},{7,6},{8,9},{9,8},{10,11... | collective-permute-start | bytes 98312 | tf_op jit(solution)/shard_map/ppermute | solution.py:49

commit v7 on v6

--- a/solution.py
+++ b/solution.py
@@ -280,14 +280,15 @@
         [lax.dynamic_index_in_dim(keys, group, 0, keepdims=False),
          lax.dynamic_index_in_dim(values, group, 0, keepdims=False)], axis=1)
     four = exchanged(own, "ctx", 4) if mutual else shifted(own, 4)
-    if mutual:
-        two = (exchanged(own, "ctx", 2), exchanged(own, "ctx", 6))
-    else:
-        two = (shifted(own, 2),)
     q, g, starts, e_own, dp_own, stats_own = call(
         own_unit_body, "own_unit", [SMEM] + [VMEM] * 3,
         (shape(all_rows, bf16), shape(all_rows, bf16), shape((2, tokens), i32),
          wide, wide, stats))(doc_lengths, queries, d_out, own)
+    sent, stats_own = lax.optimization_barrier((own, stats_own))
+    if mutual:
+        two = (exchanged(sent, "ctx", 2), exchanged(sent, "ctx", 6))
+    else:
+        two = (shifted(sent, 2),)
     other_q = exchanged(queries, "ctx", 1)
     other_g = exchanged(d_out, "ctx", 1)
     four, starts = lax.optimization_barrier((four, starts))

time: 36.5 us -> 39.1 us (1.071)
  waiting for transfers between devices: 12.7 us -> 14.5 us
  other arithmetic: 0.03 us -> 0.94 us
  local copies, waits for them, and re-layouts: 1.6 us -> 0.95 us
  starting transfers between devices: 13.4 us -> 13.9 us
    ppermute x13, waiting for transfers between devices: 12.7 us -> 14.5 us  [exchanged(): lax.ppermute(block, axis, [(i, i ^ mask) for i in range(lax.axis_size(axi...]
    select_n x1, other arithmetic: 0.02 us -> 0.92 us  [per_device(): two = jnp.where(ctx & 2 == 2, *two) if mutual else two[0]]
    unnamed x6, local copies, waits for them, and re-layouts: 0.66 us -> 0.01 us
    ppermute x13, starting transfers between devices: 13.4 us -> 13.9 us  [exchanged(): lax.ppermute(block, axis, [(i, i ^ mask) for i in range(lax.axis_size(axi...]
  transfers between devices with their start and end apart: 13 -> 13, of which waited for: 9 -> 9; matrix products, arithmetic and copies ran while one was open for 3% -> 2% of each run, Pallas kernels for 15% -> 14%
where the time goes in v7:
time: 39.1 us; the launch traced here: 39 us
  waiting for transfers between devices  14.5 us (37%)
  starting transfers between devices  13.9 us (36%)
  Pallas kernels  7.91 us (20%)
  local copies, waits for them, and re-layouts  0.95 us (2%)
  other arithmetic  0.94 us (2%)
  between operations  0.75 us (2%)
    ppermute x13, waiting for transfers between devices, exchanged(): lax.ppermute(block, axis, [(i, i ^ mask) for i in range(lax.axis_size(axi...  14.5 us
    ppermute x13, starting transfers between devices, exchanged(): lax.ppermute(block, axis, [(i, i ^ mask) for i in range(lax.axis_size(axi...  13.9 us
    pallas_call x1, Pallas kernels, per_device(): call(own_terms_body, 'own_terms', [VMEM] * 15, (shape(pair, f32), shape(a...  1.66 us
    pallas_call x1, Pallas kernels, per_device(): call(own_unit_body, 'own_unit', [SMEM] + [VMEM] * 3, (shape(all_rows, bf1...  1.2 us
    pallas_call x1, Pallas kernels, per_device(): call(two_units_body, 'two_units', [VMEM] * 9, (wide, wide, stats) * 2 + (...  1.06 us
    squeeze x1, local copies, waits for them, and re-layouts, per_device(): lax.dynamic_index_in_dim(values, group, 0, keepdims=False)  0.94 us
    select_n x1, other arithmetic, per_device(): two = jnp.where(ctx & 2 == 2, *two) if mutual else two[0]  0.92 us
    pallas_call x1, Pallas kernels, per_device(): call(two_terms_body, 'two_terms', [VMEM] * 9, (shape(pair, bf16), half, h...  0.82 us
  transfers between devices with their start and end apart: 13, of which 9 were waited for; matrix products, arithmetic and copies ran while one was open for 2% of the time, Pallas kernels for 14%

profile of v7, /device:TPU:0, one launch (start us, length us, event | category | flops | bytes accessed | tf_op | source)
XLA Modules:
  0.0 39.0 jit_solution(12103064607124275989)
XLA Ops:
  0.6 0.5 %collective-permute-start.1 = (bf16[4,256,128]{2,1,0:T(8,128)(2,1)}, bf16[4,256,128]{2,1,0:T(8,128)(2,1)S(1)}, u32[]{:S(2)}, u32[]{:S(2)}) collective-permute-start(bf16[4,256,128]{2,1,0:T(8,128)(2,1)} %q_in.1), channel_id=1, source_target_pairs={{0,4},{4,0},{8,12},{12,8},{16,20},{20,16},{24,28},{28,24},{1,5},{5... | collective-permute-start | bytes 786440 | tf_op jit(solution)/shard_map/ppermute | solution.py:49
  1.1 0.1 collective-permute-start.2
  1.2 0.9 %dynamic-slice_bitcast_fusion = (bf16[256,128]{1,0:T(8,128)(2,1)S(1)}, bf16[256,128]{1,0:T(8,128)(2,1)S(1)}) fusion(bf16[2,256,128]{2,1,0:T(8,128)(2,1)} %param.7, s32[]{:T(128)S(6)} %select_n.19, bf16[2,256,128]{2,1,0:T(8,128)(2,1)} %param.6), kind=kLoop, calls=%fused_computation.2 | loop fusion | bytes 262148 | tf_op jit(solution)/shard_map/jit(dynamic_index_in_dim)/squeeze | solution.py:281
  2.2 3.0 %collective-permute-start = (bf16[256,256]{1,0:T(8,128)(2,1)S(1)}, bf16[256,256]{1,0:T(8,128)(2,1)S(1)}, u32[]{:S(2)}, u32[]{:S(2)}) collective-permute-start(bf16[256,256]{1,0:T(8,128)(2,1)S(1)} %pad_maximum_fusion.own_ref), channel_id=1, source_target_pairs={{0,16},{4,20},{8,24},{12,28},{16,0},{20,4},{24,8},{28,12},{1,17},{... | collective-permute-start | bytes 393224 | tf_op jit(solution)/shard_map/ppermute | solution.py:49
  5.2 1.2 %own_unit.1 = (bf16[4,256,128]{2,1,0:T(8,128)(2,1)S(1)}, bf16[4,256,128]{2,1,0:T(8,128)(2,1)S(1)}, s32[2,256]{1,0:T(2,128)S(1)}, f32[256,1024]{1,0:T(8,128)S(1)}...) custom-call(s32[4]{0:T(128)S(1)} %copy-done.2, bf16[4,256,128]{2,1,0:T(8,128)(2,1)S(1)} %copy-done, ...), custom_call_target="tpu_custom_call" | custom-call | flops 1048576 | bytes 1024 | tf_op jit(solution)/shard_map/own_unit/pallas_call | solution.py:283
  6.4 1.6 %collective-permute-start.4 = (bf16[256,256]{1,0:T(8,128)(2,1)S(1)}, bf16[256,256]{1,0:T(8,128)(2,1)}, u32[]{:S(2)}, u32[]{:S(2)}) collective-permute-start(bf16[256,256]{1,0:T(8,128)(2,1)S(1)} %pad_maximum_fusion.own_ref), channel_id=1, source_target_pairs={{0,24},{4,28},{8,16},{12,20},{16,8},{20,12},{24,0},{28,4},{1,25},{... | collective-permute-start | bytes 393224 | tf_op jit(solution)/shard_map/ppermute | solution.py:49
  8.0 0.5 %collective-permute-start.3 = (bf16[256,256]{1,0:T(8,128)(2,1)S(1)}, bf16[256,256]{1,0:T(8,128)(2,1)}, u32[]{:S(2)}, u32[]{:S(2)}) collective-permute-start(bf16[256,256]{1,0:T(8,128)(2,1)S(1)} %pad_maximum_fusion.own_ref), channel_id=1, source_target_pairs={{0,8},{4,12},{8,0},{12,4},{16,24},{20,28},{24,16},{28,20},{1,9},{5... | collective-permute-start | bytes 393224 | tf_op jit(solution)/shard_map/ppermute | solution.py:49
  8.5 0.4 %collective-permute-done.four_ref = bf16[256,256]{1,0:T(8,128)(2,1)S(1)} collective-permute-done((bf16[256,256]{1,0:T(8,128)(2,1)S(1)}, bf16[256,256]{1,0:T(8,128)(2,1)S(1)}, u32[]{:S(2)}, u32[]{:S(2)}) %collective-permute-start) | collective-permute-done | bytes 131104 | tf_op jit(solution)/shard_map/ppermute | solution.py:49
  9.0 0.6 %four_unit.1 = (f32[256,1024]{1,0:T(8,128)S(1)}, f32[256,1024]{1,0:T(8,128)S(1)}, f32[3,1024]{1,0:T(4,128)S(1)}) custom-call(s32[2,256]{1,0:T(2,128)S(1)} %get-tuple-element.54.starts_ref, bf16[4,256,128]{2,1,0:T(8,128)(2,1)S(1)} %get-tuple-element.55.q_ref, bf16[4,256,128]{2,1,0:T(8,128)(2,1)S(1)} %get-tuple-element.56.g_ref, ...), custom_call_target="tpu_custom_call" | custom-call | flops 1048576 | bytes 1024 | tf_op jit(solution)/shard_map/four_unit/pallas_call | solution.py:295
  9.6 0.6 %side_unit.1 = (f32[256,1024]{1,0:T(8,128)S(1)}, f32[256,1024]{1,0:T(8,128)S(1)}, f32[3,1024]{1,0:T(4,128)S(1)}) custom-call(s32[2,256]{1,0:T(2,128)S(1)} %get-tuple-element.54.starts_ref, bf16[4,256,128]{2,1,0:T(8,128)(2,1)S(1)} %collective-permute-done.1.other_q, bf16[4,256,128]{2,1,0:T(8,128)(2,1)S(1)} %collective-permute-done.2.other_g, ...), custom_call_target="tpu_custom_call" | custom-call | flops 1048576 | bytes 1024 | tf_op jit(solution)/shard_map/side_unit/pallas_call | solution.py:298
  10.2 3.7 %collective-permute-done.4 = bf16[256,256]{1,0:T(8,128)(2,1)} collective-permute-done((bf16[256,256]{1,0:T(8,128)(2,1)S(1)}, bf16[256,256]{1,0:T(8,128)(2,1)}, u32[]{:S(2)}, u32[]{:S(2)}) %collective-permute-start.4) | collective-permute-done | bytes 131104 | tf_op jit(solution)/shard_map/ppermute | solution.py:49
  13.9 1.0 %collective-permute-done.3 = bf16[256,256]{1,0:T(8,128)(2,1)} collective-permute-done((bf16[256,256]{1,0:T(8,128)(2,1)S(1)}, bf16[256,256]{1,0:T(8,128)(2,1)}, u32[]{:S(2)}, u32[]{:S(2)}) %collective-permute-start.3) | collective-permute-done | bytes 131104 | tf_op jit(solution)/shard_map/ppermute | solution.py:49
  14.9 0.9 %broadcast_select_fusion.two_ref = bf16[256,256]{1,0:T(8,128)(2,1)S(1)} fusion(bf16[256,256]{1,0:T(8,128)(2,1)} %collective-permute-done.3, bf16[256,256]{1,0:T(8,128)(2,1)} %collective-permute-done.4, pred[]{:T(512)S(6)} %eq.3), kind=kLoop, calls=%fused_computation.1 | loop fusion | flops 65536 | bytes 393217 | tf_op jit(solution)/shard_map/jit(_where)/select_n | solution.py:302
  15.8 1.1 %two_units.1 = (f32[256,1024]{1,0:T(8,128)S(1)}, f32[256,1024]{1,0:T(8,128)S(1)}, f32[3,1024]{1,0:T(4,128)S(1)}, f32[256,1024]{1,0:T(8,128)S(1)}, f32[256,1024]{...) custom-call(s32[2,256]{1,0:T(2,128)S(1)} %get-tuple-element.54.starts_ref, ...), custom_call_target="tpu_custom_call" | custom-call | flops 1048576 | bytes 1024 | tf_op jit(solution)/shard_map/two_units/pallas_call | solution.py:303
  16.9 0.1 collective-permute-start.5
  17.0 1.2 %collective-permute-done.5.taken_ref = f32[8,1024]{1,0:T(8,128)S(1)} collective-permute-done((f32[8,1024]{1,0:T(8,128)S(1)}, f32[8,1024]{1,0:T(8,128)S(1)}, u32[]{:S(2)}, u32[]{:S(2)}) %collective-permute-start.5) | collective-permute-done | bytes 32800 | tf_op jit(solution)/shard_map/ppermute | solution.py:49
  18.2 0.5 %four_terms.1 = (f32[8,1024]{1,0:T(8,128)S(1)}, bf16[256,256]{1,0:T(8,128)(2,1)S(1)}, bf16[256,1024]{1,0:T(8,128)(2,1)S(1)}) custom-call(f32[8,1024]{1,0:T(8,128)S(1)} %get-tuple-element.68.given_ref, f32[8,1024]{1,0:T(8,128)S(1)} %collective-permute-done.5.taken_ref, f32[3,1024]{1,0:T(4,128)S(1)} %get-tuple-element.65.stats_own, ...), custom_call_target="tpu_custom_call" | custom-call | flops 1048576 | bytes 1024 | tf_op jit(solution)/shard_map/four_terms/pallas_call | solution.py:308
  18.7 1.2 %collective-permute-start.6 = (bf16[256,256]{1,0:T(8,128)(2,1)S(1)}, bf16[256,256]{1,0:T(8,128)(2,1)S(1)}, u32[]{:S(2)}, u32[]{:S(2)}) collective-permute-start(bf16[256,256]{1,0:T(8,128)(2,1)S(1)} %get-tuple-element.86), channel_id=1, source_target_pairs={{0,16},{4,20},{8,24},{12,28},{16,0},{20,4},{24,8},{28,12},{1,17},{... | collective-permute-start | bytes 393224 | tf_op jit(solution)/shard_map/ppermute | solution.py:49
  19.9 0.8 %two_terms.1 = (bf16[256,256]{1,0:T(8,128)(2,1)S(1)}, bf16[256,1024]{1,0:T(8,128)(2,1)S(1)}, bf16[256,1024]{1,0:T(8,128)(2,1)S(1)}) custom-call(f32[8,1024]{1,0:T(8,128)S(1)} %get-tuple-element.75.coef_ref, f32[256,1024]{1,0:T(8,128)S(1)} %get-tuple-element.78.e_two, f32[256,1024]{1,0:T(8,128)S(1)} %get-tuple-element.79.dp_two, ...), custom_call_target="tpu_custom_call" | custom-call | flops 1048576 | bytes 1024 | tf_op jit(solution)/shard_map/two_terms/pallas_call | solution.py:314
  20.8 1.9 %collective-permute-start.8 = (bf16[256,256]{1,0:T(8,128)(2,1)S(1)}, bf16[256,256]{1,0:T(8,128)(2,1)S(1)}, u32[]{:S(2)}, u32[]{:S(2)}) collective-permute-start(bf16[256,256]{1,0:T(8,128)(2,1)S(1)} %get-tuple-element.87), channel_id=1, source_target_pairs={{0,24},{4,28},{8,16},{12,20},{16,8},{20,12},{24,0},{28,4},{1,25},{... | collective-permute-start | bytes 393224 | tf_op jit(solution)/shard_map/ppermute | solution.py:49
  22.6 0.5 %collective-permute-start.7 = (bf16[256,256]{1,0:T(8,128)(2,1)S(1)}, bf16[256,256]{1,0:T(8,128)(2,1)S(1)}, u32[]{:S(2)}, u32[]{:S(2)}) collective-permute-start(bf16[256,256]{1,0:T(8,128)(2,1)S(1)} %get-tuple-element.87), channel_id=1, source_target_pairs={{0,8},{4,12},{8,0},{12,4},{16,24},{20,28},{24,16},{28,20},{1,9},{5... | collective-permute-start | bytes 393224 | tf_op jit(solution)/shard_map/ppermute | solution.py:49
  23.1 1.7 %own_terms.1 = (f32[256,256]{1,0:T(8,128)S(1)}, f32[4,256,128]{2,1,0:T(8,128)S(1)}, bf16[4,256,128]{2,1,0:T(8,128)(2,1)S(1)}) custom-call(f32[8,1024]{1,0:T(8,128)S(1)} %get-tuple-element.75.coef_ref, f32[256,1024]{1,0:T(8,128)S(1)} %get-tuple-element.76.e_own, f32[256,1024]{1,0:T(8,128)S(1)} %get-tuple-element.77.dp_own, ...), custom_call_target="tpu_custom_call" | custom-call | flops 1048576 | bytes 1024 | tf_op jit(solution)/shard_map/own_terms/pallas_call | solution.py:325
  24.8 2.2 %collective-permute-done.6.back = bf16[256,256]{1,0:T(8,128)(2,1)S(1)} collective-permute-done((bf16[256,256]{1,0:T(8,128)(2,1)S(1)}, bf16[256,256]{1,0:T(8,128)(2,1)S(1)}, u32[]{:S(2)}, u32[]{:S(2)}) %collective-permute-start.6) | collective-permute-done | bytes 131104 | tf_op jit(solution)/shard_map/ppermute | solution.py:49
  27.1 1.0 %collective-permute-done.8.refs_1_ = bf16[256,256]{1,0:T(8,128)(2,1)S(1)} collective-permute-done((bf16[256,256]{1,0:T(8,128)(2,1)S(1)}, bf16[256,256]{1,0:T(8,128)(2,1)S(1)}, u32[]{:S(2)}, u32[]{:S(2)}) %collective-permute-start.8) | collective-permute-done | bytes 131104 | tf_op jit(solution)/shard_map/ppermute | solution.py:49
  28.1 1.6 %collective-permute-done.7.refs_0_ = bf16[256,256]{1,0:T(8,128)(2,1)S(1)} collective-permute-done((bf16[256,256]{1,0:T(8,128)(2,1)S(1)}, bf16[256,256]{1,0:T(8,128)(2,1)S(1)}, u32[]{:S(2)}, u32[]{:S(2)}) %collective-permute-start.7) | collective-permute-done | bytes 131104 | tf_op jit(solution)/shard_map/ppermute | solution.py:49
  29.8 0.1 collective-permute-start.12
  29.8 3.7 %collective-permute-start.9 = (bf16[64,256]{1,0:T(8,128)(2,1)S(1)}, bf16[64,256]{1,0:T(8,128)(2,1)S(1)}, u32[]{:S(2)}, u32[]{:S(2)}) collective-permute-start(bf16[64,256]{1,0:T(8,128)(2,1)S(1)} %get-tuple-element.88), channel_id=1, source_target_pairs={{0,3},{1,2},{2,1},{3,0},{4,7},{5,6},{6,5},{7,4},{8,11},{9,10},{10,... | collective-permute-start | bytes 98312 | tf_op jit(solution)/shard_map/ppermute | solution.py:49
  33.5 0.8 %collective-permute-start.11 = (bf16[64,256]{1,0:T(8,128)(2,1)S(1)}, bf16[64,256]{1,0:T(8,128)(2,1)S(1)}, u32[]{:S(2)}, u32[]{:S(2)}) collective-permute-start(bf16[64,256]{1,0:T(8,128)(2,1)S(1)} %get-tuple-element.90), channel_id=1, source_target_pairs={{0,1},{1,0},{2,3},{3,2},{4,5},{5,4},{6,7},{7,6},{8,9},{9,8},{10,11... | collective-permute-start | bytes 98312 | tf_op jit(solution)/shard_map/ppermute | solution.py:49
  34.3 0.7 %add_grads.1 = bf16[4,256,128]{2,1,0:T(8,128)(2,1)} custom-call(f32[4,256,128]{2,1,0:T(8,128)S(1)} %get-tuple-element.94.mine_ref, bf16[4,256,128]{2,1,0:T(8,128)(2,1)S(1)} %collective-permute-done.12.taken_ref), custom_call_target="tpu_custom_call" | custom-call | flops 1048576 | bytes 1024 | tf_op jit(solution)/shard_map/add_grads/pallas_call | solution.py:343
  35.0 0.6 %collective-permute-done.9.refs_0_ = bf16[64,256]{1,0:T(8,128)(2,1)S(1)} collective-permute-done((bf16[64,256]{1,0:T(8,128)(2,1)S(1)}, bf16[64,256]{1,0:T(8,128)(2,1)S(1)}, u32[]{:S(2)}, u32[]{:S(2)}) %collective-permute-start.9) | collective-permute-done | bytes 32800 | tf_op jit(solution)/shard_map/ppermute | solution.py:49
  35.6 2.7 %collective-permute-done.10.refs_1_ = bf16[64,256]{1,0:T(8,128)(2,1)S(1)} collective-permute-done((bf16[64,256]{1,0:T(8,128)(2,1)S(1)}, bf16[64,256]{1,0:T(8,128)(2,1)S(1)}, u32[]{:S(2)}, u32[]{:S(2)}) %collective-permute-start.10) | collective-permute-done | bytes 32800 | tf_op jit(solution)/shard_map/ppermute | solution.py:49
  38.3 0.6 %last.1 = (bf16[2,64,128]{2,1,0:T(8,128)(2,1)}, bf16[2,64,128]{2,1,0:T(8,128)(2,1)}) custom-call(bf16[64,256]{1,0:T(8,128)(2,1)S(1)} %collective-permute-done.9.refs_0_, bf16[64,256]{1,0:T(8,128)(2,1)S(1)} %collective-permute-done.10.refs_1_, bf16[64,256]{1,0:T(8,128)(2,1)S(1)} %collective-permute-done.11.refs_2_, f32[64,256]{1,0:T(8,128)S(1)} %get-tuple-element.100.refs_3_), custom_call_target="tpu_custom_call" | custom-call | flops 1048576 | bytes 1024 | tf_op jit(solution)/shard_map/last/pallas_call | solution.py:351
  (14 shorter events, 0.1 us)
Async XLA Ops:
  0.6 8.9 %collective-permute-start.1 = (bf16[4,256,128]{2,1,0:T(8,128)(2,1)}, bf16[4,256,128]{2,1,0:T(8,128)(2,1)S(1)}, u32[]{:S(2)}, u32[]{:S(2)}) collective-permute-start(bf16[4,256,128]{2,1,0:T(8,128)(2,1)} %q_in.1), channel_id=1, source_target_pairs={{0,4},{4,0},{8,12},{12,8},{16,20},{20,16},{24,28},{28,24},{1,5},{5... | collective-permute-start | bytes 786440 | tf_op jit(solution)/shard_map/ppermute | solution.py:49
  1.1 8.4 %collective-permute-start.2 = (bf16[4,256,128]{2,1,0:T(8,128)(2,1)}, bf16[4,256,128]{2,1,0:T(8,128)(2,1)S(1)}, u32[]{:S(2)}, u32[]{:S(2)}) collective-permute-start(bf16[4,256,128]{2,1,0:T(8,128)(2,1)} %g_in.1), channel_id=1, source_target_pairs={{0,4},{4,0},{8,12},{12,8},{16,20},{20,16},{24,28},{28,24},{1,5},{5... | collective-permute-start | bytes 786440 | tf_op jit(solution)/shard_map/ppermute | solution.py:49
  1.2 4.0 %copy-start = (bf16[4,256,128]{2,1,0:T(8,128)(2,1)S(1)}, bf16[4,256,128]{2,1,0:T(8,128)(2,1)}, u32[]{:S(2)}) copy-start(bf16[4,256,128]{2,1,0:T(8,128)(2,1)} %q_in.1) | copy-start | bytes 786436
  1.2 4.0 %copy-start.1 = (bf16[4,256,128]{2,1,0:T(8,128)(2,1)S(1)}, bf16[4,256,128]{2,1,0:T(8,128)(2,1)}, u32[]{:S(2)}) copy-start(bf16[4,256,128]{2,1,0:T(8,128)(2,1)} %g_in.1) | copy-start | bytes 786436
  2.2 3.1 %copy-start.2 = (s32[4]{0:T(128)S(1)}, s32[4]{0:T(128)}, u32[]{:S(2)}) copy-start(s32[4]{0:T(128)} %lengths_ref.1) | copy-start | bytes 52
  2.2 6.8 %collective-permute-start = (bf16[256,256]{1,0:T(8,128)(2,1)S(1)}, bf16[256,256]{1,0:T(8,128)(2,1)S(1)}, u32[]{:S(2)}, u32[]{:S(2)}) collective-permute-start(bf16[256,256]{1,0:T(8,128)(2,1)S(1)} %pad_maximum_fusion.own_ref), channel_id=1, source_target_pairs={{0,16},{4,20},{8,24},{12,28},{16,0},{20,4},{24,8},{28,12},{1,17},{... | collective-permute-start | bytes 393224 | tf_op jit(solution)/shard_map/ppermute | solution.py:49
  6.4 7.5 %collective-permute-start.4 = (bf16[256,256]{1,0:T(8,128)(2,1)S(1)}, bf16[256,256]{1,0:T(8,128)(2,1)}, u32[]{:S(2)}, u32[]{:S(2)}) collective-permute-start(bf16[256,256]{1,0:T(8,128)(2,1)S(1)} %pad_maximum_fusion.own_ref), channel_id=1, source_target_pairs={{0,24},{4,28},{8,16},{12,20},{16,8},{20,12},{24,0},{28,4},{1,25},{... | collective-permute-start | bytes 393224 | tf_op jit(solution)/shard_map/ppermute | solution.py:49
  8.0 6.9 %collective-permute-start.3 = (bf16[256,256]{1,0:T(8,128)(2,1)S(1)}, bf16[256,256]{1,0:T(8,128)(2,1)}, u32[]{:S(2)}, u32[]{:S(2)}) collective-permute-start(bf16[256,256]{1,0:T(8,128)(2,1)S(1)} %pad_maximum_fusion.own_ref), channel_id=1, source_target_pairs={{0,8},{4,12},{8,0},{12,4},{16,24},{20,28},{24,16},{28,20},{1,9},{5... | collective-permute-start | bytes 393224 | tf_op jit(solution)/shard_map/ppermute | solution.py:49
  16.9 1.3 %collective-permute-start.5 = (f32[8,1024]{1,0:T(8,128)S(1)}, f32[8,1024]{1,0:T(8,128)S(1)}, u32[]{:S(2)}, u32[]{:S(2)}) collective-permute-start(f32[8,1024]{1,0:T(8,128)S(1)} %get-tuple-element.68.given_ref), channel_id=1, source_target_pairs={{0,4},{4,0},{8,12},{12,8},{16,20},{20,16},{24,28},{28,24},{1,5},{5... | collective-permute-start | bytes 98312 | tf_op jit(solution)/shard_map/ppermute | solution.py:49
  18.7 8.4 %collective-permute-start.6 = (bf16[256,256]{1,0:T(8,128)(2,1)S(1)}, bf16[256,256]{1,0:T(8,128)(2,1)S(1)}, u32[]{:S(2)}, u32[]{:S(2)}) collective-permute-start(bf16[256,256]{1,0:T(8,128)(2,1)S(1)} %get-tuple-element.86), channel_id=1, source_target_pairs={{0,16},{4,20},{8,24},{12,28},{16,0},{20,4},{24,8},{28,12},{1,17},{... | collective-permute-start | bytes 393224 | tf_op jit(solution)/shard_map/ppermute | solution.py:49
  20.8 7.3 %collective-permute-start.8 = (bf16[256,256]{1,0:T(8,128)(2,1)S(1)}, bf16[256,256]{1,0:T(8,128)(2,1)S(1)}, u32[]{:S(2)}, u32[]{:S(2)}) collective-permute-start(bf16[256,256]{1,0:T(8,128)(2,1)S(1)} %get-tuple-element.87), channel_id=1, source_target_pairs={{0,24},{4,28},{8,16},{12,20},{16,8},{20,12},{24,0},{28,4},{1,25},{... | collective-permute-start | bytes 393224 | tf_op jit(solution)/shard_map/ppermute | solution.py:49
  22.6 7.1 %collective-permute-start.7 = (bf16[256,256]{1,0:T(8,128)(2,1)S(1)}, bf16[256,256]{1,0:T(8,128)(2,1)S(1)}, u32[]{:S(2)}, u32[]{:S(2)}) collective-permute-start(bf16[256,256]{1,0:T(8,128)(2,1)S(1)} %get-tuple-element.87), channel_id=1, source_target_pairs={{0,8},{4,12},{8,0},{12,4},{16,24},{20,28},{24,16},{28,20},{1,9},{5... | collective-permute-start | bytes 393224 | tf_op jit(solution)/shard_map/ppermute | solution.py:49
  29.8 4.5 %collective-permute-start.12 = (bf16[4,256,128]{2,1,0:T(8,128)(2,1)S(1)}, bf16[4,256,128]{2,1,0:T(8,128)(2,1)S(1)}, u32[]{:S(2)}, u32[]{:S(2)}) collective-permute-start(bf16[4,256,128]{2,1,0:T(8,128)(2,1)S(1)} %get-tuple-element.95), channel_id=1, source_target_pairs={{0,4},{4,0},{8,12},{12,8},{16,20},{20,16},{24,28},{28,24},{1,5},{5... | collective-permute-start | bytes 786440 | tf_op jit(solution)/shard_map/ppermute | solution.py:49
  29.8 5.8 %collective-permute-start.9 = (bf16[64,256]{1,0:T(8,128)(2,1)S(1)}, bf16[64,256]{1,0:T(8,128)(2,1)S(1)}, u32[]{:S(2)}, u32[]{:S(2)}) collective-permute-start(bf16[64,256]{1,0:T(8,128)(2,1)S(1)} %get-tuple-element.88), channel_id=1, source_target_pairs={{0,3},{1,2},{2,1},{3,0},{4,7},{5,6},{6,5},{7,4},{8,11},{9,10},{10,... | collective-permute-start | bytes 98312 | tf_op jit(solution)/shard_map/ppermute | solution.py:49
  33.5 4.8 %collective-permute-start.10 = (bf16[64,256]{1,0:T(8,128)(2,1)S(1)}, bf16[64,256]{1,0:T(8,128)(2,1)S(1)}, u32[]{:S(2)}, u32[]{:S(2)}) collective-permute-start(bf16[64,256]{1,0:T(8,128)(2,1)S(1)} %get-tuple-element.89), channel_id=1, source_target_pairs={{0,2},{1,3},{2,0},{3,1},{4,6},{5,7},{6,4},{7,5},{8,10},{9,11},{10,... | collective-permute-start | bytes 98312 | tf_op jit(solution)/shard_map/ppermute | solution.py:49
  33.5 4.8 %collective-permute-start.11 = (bf16[64,256]{1,0:T(8,128)(2,1)S(1)}, bf16[64,256]{1,0:T(8,128)(2,1)S(1)}, u32[]{:S(2)}, u32[]{:S(2)}) collective-permute-start(bf16[64,256]{1,0:T(8,128)(2,1)S(1)} %get-tuple-element.90), channel_id=1, source_target_pairs={{0,1},{1,0},{2,3},{3,2},{4,5},{5,4},{6,7},{7,6},{8,9},{9,8},{10,11... | collective-permute-start | bytes 98312 | tf_op jit(solution)/shard_map/ppermute | solution.py:49

commit v8 on v6

--- a/solution.py
+++ b/solution.py
@@ -47,6 +47,10 @@
 
 def exchanged(block, axis, mask):
     return lax.ppermute(block, axis, [(i, i ^ mask) for i in range(lax.axis_size(axis))])
+
+
+def crossed(block):
+    return lax.ppermute(block, "ctx", [(i, i ^ 6 if 2 <= i < 6 else i) for i in range(8)])
 
 
 def second_core():
@@ -281,7 +285,7 @@
          lax.dynamic_index_in_dim(values, group, 0, keepdims=False)], axis=1)
     four = exchanged(own, "ctx", 4) if mutual else shifted(own, 4)
     if mutual:
-        two = (exchanged(own, "ctx", 2), exchanged(own, "ctx", 6))
+        two = (exchanged(own, "ctx", 2), crossed(own))
     else:
         two = (shifted(own, 2),)
     q, g, starts, e_own, dp_own, stats_own = call(
@@ -316,7 +320,7 @@
     )(coef, e_two, dp_two, e_cross, dp_cross, q, g, other_q, other_g)
     if mutual:
         backs = [exchanged(four_terms, "ctx", 4), exchanged(two_terms, "ctx", 2),
-                 exchanged(two_terms, "ctx", 6)]
+                 crossed(two_terms)]
         uses = [lambda i: i < 4, lambda i: i & 2 == 0, lambda i: i & 6 == 2]
     else:
         backs = [shifted(four_terms, -4), shifted(two_terms, -2)]

time: 36.5 us -> 40.1 us (1.099)
  starting transfers between devices: 13.4 us -> 17.2 us
    ppermute x13 -> x11, starting transfers between devices: 13.4 us -> 15.9 us  [exchanged(): lax.ppermute(block, axis, [(i, i ^ mask) for i in range(lax.axis_size(axi...]
    ppermute x0 -> x2, starting transfers between devices: none -> 1.33 us  [crossed(): lax.ppermute(block, 'ctx', [(i, i ^ 6 if 2 <= i < 6 else i) for i in rang...]
    ppermute x13 -> x11, waiting for transfers between devices: 12.7 us -> 12.4 us  [exchanged(): lax.ppermute(block, axis, [(i, i ^ mask) for i in range(lax.axis_size(axi...]
  transfers between devices with their start and end apart: 13 -> 13, of which waited for: 9 -> 5; matrix products, arithmetic and copies ran while one was open for 3% -> 2% of each run, Pallas kernels for 15% -> 14%
where the time goes in v8:
time: 40.1 us; the launch traced here: 40 us
  starting transfers between devices  17.2 us (43%)
  waiting for transfers between devices  12.4 us (31%)
  Pallas kernels  7.91 us (20%)
  local copies, waits for them, and re-layouts  1.6 us (4%)
  between operations  0.79 us (2%)
    ppermute x11, starting transfers between devices, exchanged(): lax.ppermute(block, axis, [(i, i ^ mask) for i in range(lax.axis_size(axi...  15.9 us
    ppermute x11, waiting for transfers between devices, exchanged(): lax.ppermute(block, axis, [(i, i ^ mask) for i in range(lax.axis_size(axi...  12.4 us
    pallas_call x1, Pallas kernels, per_device(): call(own_terms_body, 'own_terms', [VMEM] * 15, (shape(pair, f32), shape(a...  1.66 us
    ppermute x2, starting transfers between devices, crossed(): lax.ppermute(block, 'ctx', [(i, i ^ 6 if 2 <= i < 6 else i) for i in rang...  1.33 us
    pallas_call x1, Pallas kernels, per_device(): call(own_unit_body, 'own_unit', [SMEM] + [VMEM] * 3, (shape(all_rows, bf1...  1.2 us
    pallas_call x1, Pallas kernels, per_device(): call(two_units_body, 'two_units', [VMEM] * 9, (wide, wide, stats) * 2 + (...  1.06 us
    squeeze x1, local copies, waits for them, and re-layouts, per_device(): lax.dynamic_index_in_dim(values, group, 0, keepdims=False)  0.94 us
    pallas_call x1, Pallas kernels, per_device(): call(two_terms_body, 'two_terms', [VMEM] * 9, (shape(pair, bf16), half, h...  0.82 us
  transfers between devices with their start and end apart: 13, of which 5 were waited for; matrix products, arithmetic and copies ran while one was open for 2% of the time, Pallas kernels for 14%

profile of v8, /device:TPU:0, one launch (start us, length us, event | category | flops | bytes accessed | tf_op | source)
XLA Modules:
  0.0 40.0 jit_solution(4443495817627605297)
XLA Ops:
  0.6 0.5 %collective-permute-start.1 = (bf16[4,256,128]{2,1,0:T(8,128)(2,1)}, bf16[4,256,128]{2,1,0:T(8,128)(2,1)S(1)}, u32[]{:S(2)}, u32[]{:S(2)}) collective-permute-start(bf16[4,256,128]{2,1,0:T(8,128)(2,1)} %q_in.1), channel_id=1, source_target_pairs={{0,4},{4,0},{8,12},{12,8},{16,20},{20,16},{24,28},{28,24},{1,5},{5... | collective-permute-start | bytes 786440 | tf_op jit(solution)/shard_map/ppermute | solution.py:49
  1.1 0.1 collective-permute-start.2
  1.2 0.9 %dynamic-slice_bitcast_fusion = (bf16[256,128]{1,0:T(8,128)(2,1)S(1)}, bf16[256,128]{1,0:T(8,128)(2,1)S(1)}) fusion(bf16[2,256,128]{2,1,0:T(8,128)(2,1)} %param.7, s32[]{:T(128)S(6)} %select_n.19, bf16[2,256,128]{2,1,0:T(8,128)(2,1)} %param.6), kind=kLoop, calls=%fused_computation.2 | loop fusion | bytes 262148 | tf_op jit(solution)/shard_map/jit(dynamic_index_in_dim)/squeeze | solution.py:285
  2.2 3.0 %collective-permute-start = (bf16[256,256]{1,0:T(8,128)(2,1)S(1)}, bf16[256,256]{1,0:T(8,128)(2,1)S(1)}, u32[]{:S(2)}, u32[]{:S(2)}) collective-permute-start(bf16[256,256]{1,0:T(8,128)(2,1)S(1)} %pad_maximum_fusion.own_ref), channel_id=1, source_target_pairs={{0,16},{4,20},{8,24},{12,28},{16,0},{20,4},{24,8},{28,12},{1,17},{... | collective-permute-start | bytes 393224 | tf_op jit(solution)/shard_map/ppermute | solution.py:49
  5.2 0.7 %collective-permute-start.4 = (bf16[256,256]{1,0:T(8,128)(2,1)S(1)}, bf16[256,256]{1,0:T(8,128)(2,1)S(1)}, u32[]{:S(2)}, u32[]{:S(2)}) collective-permute-start(bf16[256,256]{1,0:T(8,128)(2,1)S(1)} %pad_maximum_fusion.own_ref), channel_id=1, source_target_pairs={{0,0},{4,4},{8,16},{12,20},{16,8},{20,12},{24,24},{28,28},{1,1},{5... | collective-permute-start | bytes 393224 | tf_op jit(solution)/shard_map/ppermute | solution.py:53
  5.9 2.8 %collective-permute-start.3 = (bf16[256,256]{1,0:T(8,128)(2,1)S(1)}, bf16[256,256]{1,0:T(8,128)(2,1)S(1)}, u32[]{:S(2)}, u32[]{:S(2)}) collective-permute-start(bf16[256,256]{1,0:T(8,128)(2,1)S(1)} %pad_maximum_fusion.own_ref), channel_id=1, source_target_pairs={{0,8},{4,12},{8,0},{12,4},{16,24},{20,28},{24,16},{28,20},{1,9},{5... | collective-permute-start | bytes 393224 | tf_op jit(solution)/shard_map/ppermute | solution.py:49
  8.7 0.6 %copy-done.2 = s32[4]{0:T(128)S(1)} copy-done((s32[4]{0:T(128)S(1)}, s32[4]{0:T(128)}, u32[]{:S(2)}) %copy-start.2) | copy-done | bytes 40
  9.3 1.2 %own_unit.1 = (bf16[4,256,128]{2,1,0:T(8,128)(2,1)S(1)}, bf16[4,256,128]{2,1,0:T(8,128)(2,1)S(1)}, s32[2,256]{1,0:T(2,128)S(1)}, f32[256,1024]{1,0:T(8,128)S(1)}...) custom-call(s32[4]{0:T(128)S(1)} %copy-done.2, bf16[4,256,128]{2,1,0:T(8,128)(2,1)S(1)} %copy-done, ...), custom_call_target="tpu_custom_call" | custom-call | flops 1048576 | bytes 1024 | tf_op jit(solution)/shard_map/own_unit/pallas_call | solution.py:291
  10.6 0.6 %four_unit.1 = (f32[256,1024]{1,0:T(8,128)S(1)}, f32[256,1024]{1,0:T(8,128)S(1)}, f32[3,1024]{1,0:T(4,128)S(1)}) custom-call(s32[2,256]{1,0:T(2,128)S(1)} %get-tuple-element.52.starts_ref, bf16[4,256,128]{2,1,0:T(8,128)(2,1)S(1)} %get-tuple-element.53.q_ref, bf16[4,256,128]{2,1,0:T(8,128)(2,1)S(1)} %get-tuple-element.54.g_ref, ...), custom_call_target="tpu_custom_call" | custom-call | flops 1048576 | bytes 1024 | tf_op jit(solution)/shard_map/four_unit/pallas_call | solution.py:298
  11.2 0.0 collective-permute-done.2.other_g
  11.2 0.6 %side_unit.1 = (f32[256,1024]{1,0:T(8,128)S(1)}, f32[256,1024]{1,0:T(8,128)S(1)}, f32[3,1024]{1,0:T(4,128)S(1)}) custom-call(s32[2,256]{1,0:T(2,128)S(1)} %get-tuple-element.52.starts_ref, bf16[4,256,128]{2,1,0:T(8,128)(2,1)S(1)} %collective-permute-done.1.other_q, bf16[4,256,128]{2,1,0:T(8,128)(2,1)S(1)} %collective-permute-done.2.other_g, ...), custom_call_target="tpu_custom_call" | custom-call | flops 1048576 | bytes 1024 | tf_op jit(solution)/shard_map/side_unit/pallas_call | solution.py:301
  11.8 3.1 %collective-permute-done.3 = bf16[256,256]{1,0:T(8,128)(2,1)S(1)} collective-permute-done((bf16[256,256]{1,0:T(8,128)(2,1)S(1)}, bf16[256,256]{1,0:T(8,128)(2,1)S(1)}, u32[]{:S(2)}, u32[]{:S(2)}) %collective-permute-start.3) | collective-permute-done | bytes 131104 | tf_op jit(solution)/shard_map/ppermute | solution.py:49
  14.9 1.1 %two_units.1 = (f32[256,1024]{1,0:T(8,128)S(1)}, f32[256,1024]{1,0:T(8,128)S(1)}, f32[3,1024]{1,0:T(4,128)S(1)}, f32[256,1024]{1,0:T(8,128)S(1)}, f32[256,1024]{...) custom-call(s32[2,256]{1,0:T(2,128)S(1)} %get-tuple-element.52.starts_ref, ...), custom_call_target="tpu_custom_call" | custom-call | flops 1048576 | bytes 1024 | tf_op jit(solution)/shard_map/two_units/pallas_call | solution.py:306
  15.9 0.1 collective-permute-start.5
  16.0 1.2 %collective-permute-done.5.taken_ref = f32[8,1024]{1,0:T(8,128)S(1)} collective-permute-done((f32[8,1024]{1,0:T(8,128)S(1)}, f32[8,1024]{1,0:T(8,128)S(1)}, u32[]{:S(2)}, u32[]{:S(2)}) %collective-permute-start.5) | collective-permute-done | bytes 32800 | tf_op jit(solution)/shard_map/ppermute | solution.py:49
  17.2 0.5 %four_terms.1 = (f32[8,1024]{1,0:T(8,128)S(1)}, bf16[256,256]{1,0:T(8,128)(2,1)S(1)}, bf16[256,1024]{1,0:T(8,128)(2,1)S(1)}) custom-call(f32[8,1024]{1,0:T(8,128)S(1)} %get-tuple-element.64.given_ref, f32[8,1024]{1,0:T(8,128)S(1)} %collective-permute-done.5.taken_ref, f32[3,1024]{1,0:T(4,128)S(1)} %get-tuple-element.61.stats_own, ...), custom_call_target="tpu_custom_call" | custom-call | flops 1048576 | bytes 1024 | tf_op jit(solution)/shard_map/four_terms/pallas_call | solution.py:311
  17.7 0.8 %collective-permute-start.6 = (bf16[256,256]{1,0:T(8,128)(2,1)S(1)}, bf16[256,256]{1,0:T(8,128)(2,1)S(1)}, u32[]{:S(2)}, u32[]{:S(2)}) collective-permute-start(bf16[256,256]{1,0:T(8,128)(2,1)S(1)} %get-tuple-element.82), channel_id=1, source_target_pairs={{0,16},{4,20},{8,24},{12,28},{16,0},{20,4},{24,8},{28,12},{1,17},{... | collective-permute-start | bytes 393224 | tf_op jit(solution)/shard_map/ppermute | solution.py:49
  18.5 0.8 %two_terms.1 = (bf16[256,256]{1,0:T(8,128)(2,1)S(1)}, bf16[256,1024]{1,0:T(8,128)(2,1)S(1)}, bf16[256,1024]{1,0:T(8,128)(2,1)S(1)}) custom-call(f32[8,1024]{1,0:T(8,128)S(1)} %get-tuple-element.71.coef_ref, f32[256,1024]{1,0:T(8,128)S(1)} %get-tuple-element.74.e_two, f32[256,1024]{1,0:T(8,128)S(1)} %get-tuple-element.75.dp_two, ...), custom_call_target="tpu_custom_call" | custom-call | flops 1048576 | bytes 1024 | tf_op jit(solution)/shard_map/two_terms/pallas_call | solution.py:317
  19.3 0.7 %collective-permute-start.8 = (bf16[256,256]{1,0:T(8,128)(2,1)S(1)}, bf16[256,256]{1,0:T(8,128)(2,1)S(1)}, u32[]{:S(2)}, u32[]{:S(2)}) collective-permute-start(bf16[256,256]{1,0:T(8,128)(2,1)S(1)} %get-tuple-element.83), channel_id=1, source_target_pairs={{0,0},{4,4},{8,16},{12,20},{16,8},{20,12},{24,24},{28,28},{1,1},{5... | collective-permute-start | bytes 393224 | tf_op jit(solution)/shard_map/ppermute | solution.py:53
  20.0 4.1 %collective-permute-start.7 = (bf16[256,256]{1,0:T(8,128)(2,1)S(1)}, bf16[256,256]{1,0:T(8,128)(2,1)S(1)}, u32[]{:S(2)}, u32[]{:S(2)}) collective-permute-start(bf16[256,256]{1,0:T(8,128)(2,1)S(1)} %get-tuple-element.83), channel_id=1, source_target_pairs={{0,8},{4,12},{8,0},{12,4},{16,24},{20,28},{24,16},{28,20},{1,9},{5... | collective-permute-start | bytes 393224 | tf_op jit(solution)/shard_map/ppermute | solution.py:49
  24.1 1.7 %own_terms.1 = (f32[256,256]{1,0:T(8,128)S(1)}, f32[4,256,128]{2,1,0:T(8,128)S(1)}, bf16[4,256,128]{2,1,0:T(8,128)(2,1)S(1)}) custom-call(f32[8,1024]{1,0:T(8,128)S(1)} %get-tuple-element.71.coef_ref, f32[256,1024]{1,0:T(8,128)S(1)} %get-tuple-element.72.e_own, f32[256,1024]{1,0:T(8,128)S(1)} %get-tuple-element.73.dp_own, ...), custom_call_target="tpu_custom_call" | custom-call | flops 1048576 | bytes 1024 | tf_op jit(solution)/shard_map/own_terms/pallas_call | solution.py:328
  25.8 0.0 collective-permute-done.6.back
  25.8 0.0 collective-permute-done.8.refs_1_
  25.8 4.7 %collective-permute-done.7.refs_0_ = bf16[256,256]{1,0:T(8,128)(2,1)S(1)} collective-permute-done((bf16[256,256]{1,0:T(8,128)(2,1)S(1)}, bf16[256,256]{1,0:T(8,128)(2,1)S(1)}, u32[]{:S(2)}, u32[]{:S(2)}) %collective-permute-start.7) | collective-permute-done | bytes 131104 | tf_op jit(solution)/shard_map/ppermute | solution.py:49
  30.5 0.1 sums.1
  30.6 0.1 collective-permute-start.12
  30.7 3.9 %collective-permute-start.9 = (bf16[64,256]{1,0:T(8,128)(2,1)S(1)}, bf16[64,256]{1,0:T(8,128)(2,1)S(1)}, u32[]{:S(2)}, u32[]{:S(2)}) collective-permute-start(bf16[64,256]{1,0:T(8,128)(2,1)S(1)} %get-tuple-element.84), channel_id=1, source_target_pairs={{0,3},{1,2},{2,1},{3,0},{4,7},{5,6},{6,5},{7,4},{8,11},{9,10},{10,... | collective-permute-start | bytes 98312 | tf_op jit(solution)/shard_map/ppermute | solution.py:49
  34.5 0.6 %collective-permute-start.11 = (bf16[64,256]{1,0:T(8,128)(2,1)S(1)}, bf16[64,256]{1,0:T(8,128)(2,1)S(1)}, u32[]{:S(2)}, u32[]{:S(2)}) collective-permute-start(bf16[64,256]{1,0:T(8,128)(2,1)S(1)} %get-tuple-element.86), channel_id=1, source_target_pairs={{0,1},{1,0},{2,3},{3,2},{4,5},{5,4},{6,7},{7,6},{8,9},{9,8},{10,11... | collective-permute-start | bytes 98312 | tf_op jit(solution)/shard_map/ppermute | solution.py:49
  35.2 0.7 %add_grads.1 = bf16[4,256,128]{2,1,0:T(8,128)(2,1)} custom-call(f32[4,256,128]{2,1,0:T(8,128)S(1)} %get-tuple-element.90.mine_ref, bf16[4,256,128]{2,1,0:T(8,128)(2,1)S(1)} %collective-permute-done.12.taken_ref), custom_call_target="tpu_custom_call" | custom-call | flops 1048576 | bytes 1024 | tf_op jit(solution)/shard_map/add_grads/pallas_call | solution.py:346
  35.9 0.6 %collective-permute-done.9.refs_0_ = bf16[64,256]{1,0:T(8,128)(2,1)S(1)} collective-permute-done((bf16[64,256]{1,0:T(8,128)(2,1)S(1)}, bf16[64,256]{1,0:T(8,128)(2,1)S(1)}, u32[]{:S(2)}, u32[]{:S(2)}) %collective-permute-start.9) | collective-permute-done | bytes 32800 | tf_op jit(solution)/shard_map/ppermute | solution.py:49
  36.5 2.8 %collective-permute-done.10.refs_1_ = bf16[64,256]{1,0:T(8,128)(2,1)S(1)} collective-permute-done((bf16[64,256]{1,0:T(8,128)(2,1)S(1)}, bf16[64,256]{1,0:T(8,128)(2,1)S(1)}, u32[]{:S(2)}, u32[]{:S(2)}) %collective-permute-start.10) | collective-permute-done | bytes 32800 | tf_op jit(solution)/shard_map/ppermute | solution.py:49
  39.3 0.6 %last.1 = (bf16[2,64,128]{2,1,0:T(8,128)(2,1)}, bf16[2,64,128]{2,1,0:T(8,128)(2,1)}) custom-call(bf16[64,256]{1,0:T(8,128)(2,1)S(1)} %collective-permute-done.9.refs_0_, bf16[64,256]{1,0:T(8,128)(2,1)S(1)} %collective-permute-done.10.refs_1_, bf16[64,256]{1,0:T(8,128)(2,1)S(1)} %collective-permute-done.11.refs_2_, f32[64,256]{1,0:T(8,128)S(1)} %get-tuple-element.96.refs_3_), custom_call_target="tpu_custom_call" | custom-call | flops 1048576 | bytes 1024 | tf_op jit(solution)/shard_map/last/pallas_call | solution.py:354
  (14 shorter events, 0.1 us)
Async XLA Ops:
  0.6 10.5 %collective-permute-start.1 = (bf16[4,256,128]{2,1,0:T(8,128)(2,1)}, bf16[4,256,128]{2,1,0:T(8,128)(2,1)S(1)}, u32[]{:S(2)}, u32[]{:S(2)}) collective-permute-start(bf16[4,256,128]{2,1,0:T(8,128)(2,1)} %q_in.1), channel_id=1, source_target_pairs={{0,4},{4,0},{8,12},{12,8},{16,20},{20,16},{24,28},{28,24},{1,5},{5... | collective-permute-start | bytes 786440 | tf_op jit(solution)/shard_map/ppermute | solution.py:49
  1.1 10.0 %collective-permute-start.2 = (bf16[4,256,128]{2,1,0:T(8,128)(2,1)}, bf16[4,256,128]{2,1,0:T(8,128)(2,1)S(1)}, u32[]{:S(2)}, u32[]{:S(2)}) collective-permute-start(bf16[4,256,128]{2,1,0:T(8,128)(2,1)} %g_in.1), channel_id=1, source_target_pairs={{0,4},{4,0},{8,12},{12,8},{16,20},{20,16},{24,28},{28,24},{1,5},{5... | collective-permute-start | bytes 786440 | tf_op jit(solution)/shard_map/ppermute | solution.py:49
  1.2 7.5 %copy-start = (bf16[4,256,128]{2,1,0:T(8,128)(2,1)S(1)}, bf16[4,256,128]{2,1,0:T(8,128)(2,1)}, u32[]{:S(2)}) copy-start(bf16[4,256,128]{2,1,0:T(8,128)(2,1)} %q_in.1) | copy-start | bytes 786436
  1.2 7.5 %copy-start.1 = (bf16[4,256,128]{2,1,0:T(8,128)(2,1)S(1)}, bf16[4,256,128]{2,1,0:T(8,128)(2,1)}, u32[]{:S(2)}) copy-start(bf16[4,256,128]{2,1,0:T(8,128)(2,1)} %g_in.1) | copy-start | bytes 786436
  2.2 8.4 %collective-permute-start = (bf16[256,256]{1,0:T(8,128)(2,1)S(1)}, bf16[256,256]{1,0:T(8,128)(2,1)S(1)}, u32[]{:S(2)}, u32[]{:S(2)}) collective-permute-start(bf16[256,256]{1,0:T(8,128)(2,1)S(1)} %pad_maximum_fusion.own_ref), channel_id=1, source_target_pairs={{0,16},{4,20},{8,24},{12,28},{16,0},{20,4},{24,8},{28,12},{1,17},{... | collective-permute-start | bytes 393224 | tf_op jit(solution)/shard_map/ppermute | solution.py:49
  5.2 6.5 %collective-permute-start.4 = (bf16[256,256]{1,0:T(8,128)(2,1)S(1)}, bf16[256,256]{1,0:T(8,128)(2,1)S(1)}, u32[]{:S(2)}, u32[]{:S(2)}) collective-permute-start(bf16[256,256]{1,0:T(8,128)(2,1)S(1)} %pad_maximum_fusion.own_ref), channel_id=1, source_target_pairs={{0,0},{4,4},{8,16},{12,20},{16,8},{20,12},{24,24},{28,28},{1,1},{5... | collective-permute-start | bytes 393224 | tf_op jit(solution)/shard_map/ppermute | solution.py:53
  5.9 9.0 %collective-permute-start.3 = (bf16[256,256]{1,0:T(8,128)(2,1)S(1)}, bf16[256,256]{1,0:T(8,128)(2,1)S(1)}, u32[]{:S(2)}, u32[]{:S(2)}) collective-permute-start(bf16[256,256]{1,0:T(8,128)(2,1)S(1)} %pad_maximum_fusion.own_ref), channel_id=1, source_target_pairs={{0,8},{4,12},{8,0},{12,4},{16,24},{20,28},{24,16},{28,20},{1,9},{5... | collective-permute-start | bytes 393224 | tf_op jit(solution)/shard_map/ppermute | solution.py:49
  8.7 0.7 %copy-start.2 = (s32[4]{0:T(128)S(1)}, s32[4]{0:T(128)}, u32[]{:S(2)}) copy-start(s32[4]{0:T(128)} %lengths_ref.1) | copy-start | bytes 52
  15.9 1.3 %collective-permute-start.5 = (f32[8,1024]{1,0:T(8,128)S(1)}, f32[8,1024]{1,0:T(8,128)S(1)}, u32[]{:S(2)}, u32[]{:S(2)}) collective-permute-start(f32[8,1024]{1,0:T(8,128)S(1)} %get-tuple-element.64.given_ref), channel_id=1, source_target_pairs={{0,4},{4,0},{8,12},{12,8},{16,20},{20,16},{24,28},{28,24},{1,5},{5... | collective-permute-start | bytes 98312 | tf_op jit(solution)/shard_map/ppermute | solution.py:49
  17.7 8.0 %collective-permute-start.6 = (bf16[256,256]{1,0:T(8,128)(2,1)S(1)}, bf16[256,256]{1,0:T(8,128)(2,1)S(1)}, u32[]{:S(2)}, u32[]{:S(2)}) collective-permute-start(bf16[256,256]{1,0:T(8,128)(2,1)S(1)} %get-tuple-element.82), channel_id=1, source_target_pairs={{0,16},{4,20},{8,24},{12,28},{16,0},{20,4},{24,8},{28,12},{1,17},{... | collective-permute-start | bytes 393224 | tf_op jit(solution)/shard_map/ppermute | solution.py:49
  19.3 6.5 %collective-permute-start.8 = (bf16[256,256]{1,0:T(8,128)(2,1)S(1)}, bf16[256,256]{1,0:T(8,128)(2,1)S(1)}, u32[]{:S(2)}, u32[]{:S(2)}) collective-permute-start(bf16[256,256]{1,0:T(8,128)(2,1)S(1)} %get-tuple-element.83), channel_id=1, source_target_pairs={{0,0},{4,4},{8,16},{12,20},{16,8},{20,12},{24,24},{28,28},{1,1},{5... | collective-permute-start | bytes 393224 | tf_op jit(solution)/shard_map/ppermute | solution.py:53
  20.0 10.5 %collective-permute-start.7 = (bf16[256,256]{1,0:T(8,128)(2,1)S(1)}, bf16[256,256]{1,0:T(8,128)(2,1)S(1)}, u32[]{:S(2)}, u32[]{:S(2)}) collective-permute-start(bf16[256,256]{1,0:T(8,128)(2,1)S(1)} %get-tuple-element.83), channel_id=1, source_target_pairs={{0,8},{4,12},{8,0},{12,4},{16,24},{20,28},{24,16},{28,20},{1,9},{5... | collective-permute-start | bytes 393224 | tf_op jit(solution)/shard_map/ppermute | solution.py:49
  30.6 4.6 %collective-permute-start.12 = (bf16[4,256,128]{2,1,0:T(8,128)(2,1)S(1)}, bf16[4,256,128]{2,1,0:T(8,128)(2,1)S(1)}, u32[]{:S(2)}, u32[]{:S(2)}) collective-permute-start(bf16[4,256,128]{2,1,0:T(8,128)(2,1)S(1)} %get-tuple-element.91), channel_id=1, source_target_pairs={{0,4},{4,0},{8,12},{12,8},{16,20},{20,16},{24,28},{28,24},{1,5},{5... | collective-permute-start | bytes 786440 | tf_op jit(solution)/shard_map/ppermute | solution.py:49
  30.7 5.9 %collective-permute-start.9 = (bf16[64,256]{1,0:T(8,128)(2,1)S(1)}, bf16[64,256]{1,0:T(8,128)(2,1)S(1)}, u32[]{:S(2)}, u32[]{:S(2)}) collective-permute-start(bf16[64,256]{1,0:T(8,128)(2,1)S(1)} %get-tuple-element.84), channel_id=1, source_target_pairs={{0,3},{1,2},{2,1},{3,0},{4,7},{5,6},{6,5},{7,4},{8,11},{9,10},{10,... | collective-permute-start | bytes 98312 | tf_op jit(solution)/shard_map/ppermute | solution.py:49
  34.5 4.8 %collective-permute-start.10 = (bf16[64,256]{1,0:T(8,128)(2,1)S(1)}, bf16[64,256]{1,0:T(8,128)(2,1)S(1)}, u32[]{:S(2)}, u32[]{:S(2)}) collective-permute-start(bf16[64,256]{1,0:T(8,128)(2,1)S(1)} %get-tuple-element.85), channel_id=1, source_target_pairs={{0,2},{1,3},{2,0},{3,1},{4,6},{5,7},{6,4},{7,5},{8,10},{9,11},{10,... | collective-permute-start | bytes 98312 | tf_op jit(solution)/shard_map/ppermute | solution.py:49
  34.5 4.8 %collective-permute-start.11 = (bf16[64,256]{1,0:T(8,128)(2,1)S(1)}, bf16[64,256]{1,0:T(8,128)(2,1)S(1)}, u32[]{:S(2)}, u32[]{:S(2)}) collective-permute-start(bf16[64,256]{1,0:T(8,128)(2,1)S(1)} %get-tuple-element.86), channel_id=1, source_target_pairs={{0,1},{1,0},{2,3},{3,2},{4,5},{5,4},{6,7},{7,6},{8,9},{9,8},{10,11... | collective-permute-start | bytes 98312 | tf_op jit(solution)/shard_map/ppermute | solution.py:49
